TPU v7x, 256 devices: a whole 4x4x8 slice. The times are simulated.
256 devices in a mesh: rows: 256 (over z, y, x, core).
Axes of the slice: x: 4, y: 4, z: 8, core: 2. Of those that a mesh axis runs over, the one named last changes fastest.
Arguments:
- vectors: bfloat16 [16, 32, 65536], P(None, None, 'rows'), may hold values from -6 to 6
- factors: bfloat16 [10, 64, 64, 32768], P(None, None, None, 'rows'), may hold values from -0.75 to 0.75
- neighbor_blocks: bfloat16 [3, 32, 32, 65536], P(None, None, None, 'rows'), may hold values from -0.625 to 0.625
Outputs:
- product: bfloat16 [16, 32, 65536], P(None, None, 'rows')
All inputs are finite; a program needn't handle non-finite values.
Results may differ from a plain program's by a relative error of at most 0.0094.
Values may be sent and summed in bfloat16 or wider, within the bound.
No kernel may reach another device: no remote copies, remote signals or barrier semaphores. Data moves between devices by JAX's collectives and lax.ppermute only.
A program may use at most 128 MiB of HBM per device.

v0:
```python
import functools

import jax
import jax.numpy as jnp
from jax import lax
from jax.experimental import pallas as pl
from jax.experimental.pallas import tpu as pltpu
from jax.sharding import PartitionSpec as P

RHS = 16
RANK = 32
HALF = 128
QUADS = 32
LANES = 128
BF16 = jnp.bfloat16
F32 = jnp.float32


def lane_bit(shape, step, dtype=jnp.int32):
    return (lax.broadcasted_iota(dtype, shape, len(shape) - 1) & step) != 0


def swap_major_lanes(blocks):
    blocks = list(blocks)
    shape = blocks[0].shape
    for step in (16, 8, 4, 2, 1):
        upper = lane_bit(shape, step)
        for low in range(QUADS):
            if low & step:
                continue
            high = low + step
            first, second = blocks[low], blocks[high]
            blocks[low] = jnp.where(upper, pltpu.roll(second, step, 1), first)
            blocks[high] = jnp.where(upper, second, pltpu.roll(first, LANES - step, 1))
    return blocks


def arrange_section(weights_ref, arranged_ref):
    for half in range(2):
        for rows in range(0, 2 * RANK, 16):
            blocks = [weights_ref[half * RANK + a, rows : rows + 16, :] for a in range(RANK)]
            for q, block in enumerate(swap_major_lanes(blocks)):
                arranged_ref[q, half, rows : rows + 16, :] = block


def diagonal_blocks(block, group):
    lane = lax.broadcasted_iota(jnp.int32, block.shape, 1)
    return jnp.where((lane >> 5) & 3 == group, block, jnp.zeros_like(block))


def section_quad(arranged_ref, q, lower, higher):
    tiles = []
    for half in range(2):
        rows = slice(half * RANK, (half + 1) * RANK)
        dense = jnp.concatenate([arranged_ref[q, 0, rows, :], arranged_ref[q, 1, rows, :]], axis=1)
        tiles += [diagonal_blocks(dense, group) for group in range(4)]
    matrix = jnp.concatenate(tiles, axis=0)
    stack = jnp.concatenate([lower, higher], axis=1)
    return jnp.dot(stack, matrix, preferred_element_type=F32)


def emit_halves(mixed, q, upper, own_ref, send_ref):
    first, second = mixed[:, :LANES], mixed[:, LANES:]
    own_ref[q] = jnp.where(upper, second, first)
    send_ref[q] = jnp.where(upper, first, second)


def level_bit(level):
    return (lax.axis_index("rows") >> level) & 1 == 1


def head_kernel(vectors_ref, weights_ref, own_ref, send_ref, halves_ref, rows_ref, arranged_ref):
    arrange_section(weights_ref.at[0], arranged_ref)
    for half in range(2):
        lanes = slice(half * HALF, (half + 1) * HALF)
        for r in range(RHS):
            rows_ref[r * RANK : (r + 1) * RANK, :] = vectors_ref[r, :, lanes].astype(F32)
        blocks = [rows_ref[pl.ds(a, RHS, stride=RANK), :].astype(BF16) for a in range(RANK)]
        for q, block in enumerate(swap_major_lanes(blocks)):
            halves_ref[half, q] = block
    upper = level_bit(0)
    for q in range(QUADS):
        mixed = section_quad(arranged_ref, q, halves_ref[0, q], halves_ref[1, q]).astype(BF16)
        emit_halves(mixed, q, upper, own_ref, send_ref)


def arrange_kernel(weights_ref, after_ref, arranged_ref):
    del after_ref
    arrange_section(weights_ref.at[0], arranged_ref)


def level_kernel(level, last, arranged_ref, kept_ref, received_ref, own_ref, send_ref):
    upper = level_bit(level)
    next_upper = False if last else level_bit(level + 1)
    for q in range(QUADS):
        kept, received = kept_ref[q], received_ref[q]
        lower = jnp.where(upper, received, kept)
        higher = jnp.where(upper, kept, received)
        mixed = section_quad(arranged_ref, q, lower, higher).astype(BF16)
        emit_halves(mixed, q, next_upper, own_ref, send_ref)


def near_kernel(halves_ref, before_ref, after_ref, blocks_ref, near_ref, arranged_ref):
    group = lax.broadcasted_iota(jnp.int32, (RHS, LANES), 1) >> 5
    for half in range(2):
        for shift in range(3):
            for rows in range(0, RANK, 16):
                lanes = slice(half * HALF, (half + 1) * HALF)
                blocks = [blocks_ref[shift, a, rows : rows + 16, lanes] for a in range(RANK)]
                for q, block in enumerate(swap_major_lanes(blocks)):
                    arranged_ref[shift, q, rows : rows + 16, :] = block
        edge_before = before_ref[...] if half == 0 else halves_ref[0, QUADS - 1]
        edge_after = after_ref[...] if half == 1 else halves_ref[1, 0]
        for q in range(QUADS):
            centre = halves_ref[half, q]
            if q > 0:
                before = halves_ref[half, q - 1]
            else:
                last = halves_ref[half, QUADS - 1]
                before = pltpu.roll(jnp.where(group == 3, edge_before, last), RANK, 1)
            if q < QUADS - 1:
                after = halves_ref[half, q + 1]
            else:
                first = halves_ref[half, 0]
                after = pltpu.roll(jnp.where(group == 0, edge_after, first), LANES - RANK, 1)
            tiles = [
                diagonal_blocks(arranged_ref[shift, q], part) for shift in range(3) for part in range(4)
            ]
            matrix = jnp.concatenate(tiles, axis=0)
            stack = jnp.concatenate([centre, before, after], axis=1)
            near_ref[half, q] = jnp.dot(stack, matrix, preferred_element_type=F32)


def root_kernel(arranged_ref, first_ref, second_ref, near_ref, product_ref, rows_ref):
    blocks = [[], []]
    for q in range(QUADS):
        mixed = section_quad(arranged_ref, q, first_ref[q], second_ref[q])
        for half in range(2):
            total = mixed[:, half * LANES : (half + 1) * LANES] + near_ref[half, q]
            blocks[half].append(total.astype(BF16))
    for half in range(2):
        lanes = slice(half * HALF, (half + 1) * HALF)
        for a, block in enumerate(swap_major_lanes(blocks[half])):
            rows_ref[half, a * RHS : (a + 1) * RHS, :] = block.astype(F32)
        for r in range(RHS):
            product_ref[r, :, lanes] = rows_ref[half, pl.ds(r, RANK, stride=RHS), :].astype(BF16)


VMEM_SPEC = pl.BlockSpec(memory_space=pltpu.VMEM)
ANY_SPEC = pl.BlockSpec(memory_space=pl.ANY)
PAYLOAD = jax.ShapeDtypeStruct((QUADS, RHS, LANES), BF16)
ARRANGED = (QUADS, 2, 2 * RANK, LANES)


def one_section(index):
    return pl.BlockSpec((1, 2 * RANK, 2 * RANK, HALF), lambda step: (index, 0, 0, 0))


def whole(shape):
    return pl.BlockSpec(shape, lambda step: (0,) * len(shape))


def params(mib):
    return pltpu.CompilerParams(vmem_limit_bytes=mib * 2**20)


def arrange(factors, index, after):
    return pl.pallas_call(
        arrange_kernel,
        grid=(1,),
        out_shape=jax.ShapeDtypeStruct(ARRANGED, BF16),
        in_specs=[one_section(index), ANY_SPEC],
        out_specs=whole(ARRANGED),
        compiler_params=params(8),
        cost_estimate=pl.CostEstimate(flops=2 * 10**6, bytes_accessed=2 * 2**20, transcendentals=0),
        name="arrange",
    )(factors, after)


def head(vectors, factors):
    return pl.pallas_call(
        head_kernel,
        grid=(1,),
        out_shape=(PAYLOAD, PAYLOAD, jax.ShapeDtypeStruct((2, QUADS, RHS, LANES), BF16)),
        in_specs=[whole((RHS, RANK, 2 * HALF)), one_section(0)],
        out_specs=(whole(PAYLOAD.shape), whole(PAYLOAD.shape), whole((2, QUADS, RHS, LANES))),
        scratch_shapes=[pltpu.VMEM((RHS * RANK, LANES), F32), pltpu.VMEM(ARRANGED, BF16)],
        compiler_params=params(12),
        name="head",
    )(vectors, factors)


def level_step(level, last, arranged, kept, received):
    return pl.pallas_call(
        functools.partial(level_kernel, level, last),
        out_shape=(PAYLOAD, PAYLOAD),
        in_specs=[VMEM_SPEC] * 3,
        out_specs=(VMEM_SPEC, VMEM_SPEC),
        compiler_params=params(6),
        name="level",
    )(arranged, kept, received)


def near_field(halves, before, after, neighbor_blocks):
    return pl.pallas_call(
        near_kernel,
        out_shape=jax.ShapeDtypeStruct((2, QUADS, RHS, LANES), F32),
        in_specs=[VMEM_SPEC] * 4,
        out_specs=VMEM_SPEC,
        scratch_shapes=[pltpu.VMEM((3, QUADS, RANK, LANES), BF16)],
        compiler_params=params(12),
        cost_estimate=pl.CostEstimate(flops=4 * 10**6, bytes_accessed=3 * 2**20, transcendentals=0),
        name="near",
    )(halves, before, after, neighbor_blocks)


def root(arranged, first, second, near):
    return pl.pallas_call(
        root_kernel,
        out_shape=jax.ShapeDtypeStruct((RHS, RANK, 2 * HALF), BF16),
        in_specs=[VMEM_SPEC] * 4,
        out_specs=VMEM_SPEC,
        scratch_shapes=[pltpu.VMEM((2, RHS * RANK, LANES), F32)],
        compiler_params=params(12),
        name="root",
    )(arranged, first, second, near)


def shards(vectors, factors, neighbor_blocks):
    level_count = factors.shape[0] - 2
    count = lax.axis_size("rows")
    kept, sending, halves = head(vectors, factors)
    before = lax.ppermute(halves[1, QUADS - 1], "rows", [(i, i + 1) for i in range(count - 1)])
    after = lax.ppermute(halves[0, 0], "rows", [(i + 1, i) for i in range(count - 1)])
    near = near_field(halves, before, after, neighbor_blocks)
    for level in range(level_count):
        received = lax.ppermute(sending, "rows", [(i, i ^ (1 << level)) for i in range(count)])
        arranged = arrange(factors, level + 1, sending)
        kept, sending = level_step(level, level == level_count - 1, arranged, kept, received)
    arranged = arrange(factors, level_count + 1, received)
    return root(arranged, kept, sending, near)


def solution(mesh):
    placed = (P(None, None, "rows"), P(None, None, None, "rows"), P(None, None, None, "rows"))
    return jax.shard_map(
        shards, mesh=mesh, in_specs=placed, out_specs=P(None, None, "rows"), check_vma=False
    )
```

profile of v0, /device:TPU:7, one launch (start us, length us, event | category | flops | bytes accessed | tf_op | source)
XLA Modules:
  0.0 85.8 jit_solution(11309681813858870438)
XLA Ops:
  0.0 4.0 %copy-done = bf16[10,64,64,128]{3,2,1,0:T(8,128)(2,1)S(1)} copy-done((bf16[10,64,64,128]{3,2,1,0:T(8,128)(2,1)S(1)}, bf16[10,64,64,128]{3,2,1,0:T(8,128)(2,1)}, u32[]{:S(2)}) %copy-start) | copy-done | bytes 10485784
  4.0 0.9 %copy-done.3 = bf16[16,32,256]{2,1,0:T(8,128)(2,1)S(1)} copy-done((bf16[16,32,256]{2,1,0:T(8,128)(2,1)S(1)}, bf16[16,32,256]{2,1,0:T(8,128)(2,1)}, u32[]{:S(2)}) %copy-start.3) | copy-done | bytes 262168
  5.0 3.3 %head.1 = (bf16[32,16,128]{2,1,0:T(8,128)(2,1)S(1)}, bf16[32,16,128]{2,1,0:T(8,128)(2,1)S(1)}, bf16[2,32,16,128]{3,2,1,0:T(8,128)(2,1)S(1)}) custom-call(bf16[16,32,256]{2,1,0:T(8,128)(2,1)S(1)} %copy-done.3, bf16[10,64,64,128]{3,2,1,0:T(8,128)(2,1)S(1)} %copy-done), custom_call_target="tpu_custom_call" | custom-call | tf_op jit(solution)/shard_map/head/pallas_call | solution.py:181
  8.3 0.7 collective-permute-start
  9.0 2.6 %arrange.9.arranged_ref = bf16[32,2,64,128]{3,2,1,0:T(8,128)(2,1)S(1)} custom-call(bf16[10,64,64,128]{3,2,1,0:T(8,128)(2,1)S(1)} %copy-done.1, bf16[32,16,128]{2,1,0:T(8,128)(2,1)S(1)} %get-tuple-element.24.after_ref), custom_call_target="tpu_custom_call" | custom-call | flops 2000000 | bytes 2097152 | tf_op jit(solution)/shard_map/arrange/pallas_call | solution.py:168
  11.7 0.7 level.8
  12.9 2.6 %arrange.10.arranged_ref = bf16[32,2,64,128]{3,2,1,0:T(8,128)(2,1)S(1)} custom-call(bf16[10,64,64,128]{3,2,1,0:T(8,128)(2,1)S(1)} %copy-done.1, bf16[32,16,128]{2,1,0:T(8,128)(2,1)S(1)} %get-tuple-element.26.after_ref), custom_call_target="tpu_custom_call" | custom-call | flops 2000000 | bytes 2097152 | tf_op jit(solution)/shard_map/arrange/pallas_call | solution.py:168
  15.6 1.2 %collective-permute-done.1.received_ref = bf16[32,16,128]{2,1,0:T(8,128)(2,1)S(1)} collective-permute-done((bf16[32,16,128]{2,1,0:T(8,128)(2,1)S(1)}, bf16[32,16,128]{2,1,0:T(8,128)(2,1)S(1)}, u32[]{:S(2)}, u32[]{:S(2)}) %collective-permute-start.1) | collective-permute-done | bytes 131104 | tf_op jit(solution)/shard_map/ppermute | solution.py:237
  16.8 0.7 level.9
  17.5 2.1 %collective-permute-start.2 = (bf16[32,16,128]{2,1,0:T(8,128)(2,1)S(1)}, bf16[32,16,128]{2,1,0:T(8,128)(2,1)S(1)}, u32[]{:S(2)}, u32[]{:S(2)}) collective-permute-start(bf16[32,16,128]{2,1,0:T(8,128)(2,1)S(1)} %get-tuple-element.28.after_ref), channel_id=1, source_target_pairs={{0,4},{1,5},{2,6},{3,7},{4,0},{5,1},{6,2},{7,3},{8,12},{9,13},{10,... | collective-permute-start | bytes 393224 | tf_op jit(solution)/shard_map/ppermute | solution.py:237
  19.5 2.6 %arrange.11.arranged_ref = bf16[32,2,64,128]{3,2,1,0:T(8,128)(2,1)S(1)} custom-call(bf16[10,64,64,128]{3,2,1,0:T(8,128)(2,1)S(1)} %copy-done.1, bf16[32,16,128]{2,1,0:T(8,128)(2,1)S(1)} %get-tuple-element.28.after_ref), custom_call_target="tpu_custom_call" | custom-call | flops 2000000 | bytes 2097152 | tf_op jit(solution)/shard_map/arrange/pallas_call | solution.py:168
  22.2 0.7 collective-permute-done.2.received_ref
  23.5 1.6 %collective-permute-start.3 = (bf16[32,16,128]{2,1,0:T(8,128)(2,1)S(1)}, bf16[32,16,128]{2,1,0:T(8,128)(2,1)S(1)}, u32[]{:S(2)}, u32[]{:S(2)}) collective-permute-start(bf16[32,16,128]{2,1,0:T(8,128)(2,1)S(1)} %get-tuple-element.30.after_ref), channel_id=1, source_target_pairs={{0,8},{1,9},{2,10},{3,11},{4,12},{5,13},{6,14},{7,15},{8,0},{9,1},... | collective-permute-start | bytes 393224 | tf_op jit(solution)/shard_map/ppermute | solution.py:237
  25.1 2.6 %arrange.12.arranged_ref = bf16[32,2,64,128]{3,2,1,0:T(8,128)(2,1)S(1)} custom-call(bf16[10,64,64,128]{3,2,1,0:T(8,128)(2,1)S(1)} %copy-done.1, bf16[32,16,128]{2,1,0:T(8,128)(2,1)S(1)} %get-tuple-element.30.after_ref), custom_call_target="tpu_custom_call" | custom-call | flops 2000000 | bytes 2097152 | tf_op jit(solution)/shard_map/arrange/pallas_call | solution.py:168
  27.7 0.7 level.11
  28.4 2.9 %collective-permute-start.4 = (bf16[32,16,128]{2,1,0:T(8,128)(2,1)S(1)}, bf16[32,16,128]{2,1,0:T(8,128)(2,1)S(1)}, u32[]{:S(2)}, u32[]{:S(2)}) collective-permute-start(bf16[32,16,128]{2,1,0:T(8,128)(2,1)S(1)} %get-tuple-element.32.after_ref), channel_id=1, source_target_pairs={{0,16},{1,17},{2,18},{3,19},{4,20},{5,21},{6,22},{7,23},{8,24},{9,... | collective-permute-start | bytes 393224 | tf_op jit(solution)/shard_map/ppermute | solution.py:237
  31.3 2.6 %arrange.13.arranged_ref = bf16[32,2,64,128]{3,2,1,0:T(8,128)(2,1)S(1)} custom-call(bf16[10,64,64,128]{3,2,1,0:T(8,128)(2,1)S(1)} %copy-done.1, bf16[32,16,128]{2,1,0:T(8,128)(2,1)S(1)} %get-tuple-element.32.after_ref), custom_call_target="tpu_custom_call" | custom-call | flops 2000000 | bytes 2097152 | tf_op jit(solution)/shard_map/arrange/pallas_call | solution.py:168
  33.9 0.7 collective-permute-done.4.received_ref
  34.6 0.7 level.12
  35.2 1.7 %collective-permute-start.5 = (bf16[32,16,128]{2,1,0:T(8,128)(2,1)S(1)}, bf16[32,16,128]{2,1,0:T(8,128)(2,1)S(1)}, u32[]{:S(2)}, u32[]{:S(2)}) collective-permute-start(bf16[32,16,128]{2,1,0:T(8,128)(2,1)S(1)} %get-tuple-element.34.after_ref), channel_id=1, source_target_pairs={{0,32},{1,33},{2,34},{3,35},{4,36},{5,37},{6,38},{7,39},{8,40},{9,... | collective-permute-start | bytes 393224 | tf_op jit(solution)/shard_map/ppermute | solution.py:237
  37.0 2.6 %arrange.14.arranged_ref = bf16[32,2,64,128]{3,2,1,0:T(8,128)(2,1)S(1)} custom-call(bf16[10,64,64,128]{3,2,1,0:T(8,128)(2,1)S(1)} %copy-done.1, bf16[32,16,128]{2,1,0:T(8,128)(2,1)S(1)} %get-tuple-element.34.after_ref), custom_call_target="tpu_custom_call" | custom-call | flops 2000000 | bytes 2097152 | tf_op jit(solution)/shard_map/arrange/pallas_call | solution.py:168
  39.6 0.7 level.13
  40.3 3.1 %collective-permute-start.6 = (bf16[32,16,128]{2,1,0:T(8,128)(2,1)S(1)}, bf16[32,16,128]{2,1,0:T(8,128)(2,1)S(1)}, u32[]{:S(2)}, u32[]{:S(2)}) collective-permute-start(bf16[32,16,128]{2,1,0:T(8,128)(2,1)S(1)} %get-tuple-element.36.after_ref), channel_id=1, source_target_pairs={{0,64},{1,65},{2,66},{3,67},{4,68},{5,69},{6,70},{7,71},{8,72},{9,... | collective-permute-start | bytes 393224 | tf_op jit(solution)/shard_map/ppermute | solution.py:237
  43.3 2.6 %arrange.15.arranged_ref = bf16[32,2,64,128]{3,2,1,0:T(8,128)(2,1)S(1)} custom-call(bf16[10,64,64,128]{3,2,1,0:T(8,128)(2,1)S(1)} %copy-done.1, bf16[32,16,128]{2,1,0:T(8,128)(2,1)S(1)} %get-tuple-element.36.after_ref), custom_call_target="tpu_custom_call" | custom-call | flops 2000000 | bytes 2097152 | tf_op jit(solution)/shard_map/arrange/pallas_call | solution.py:168
  46.8 6.8 %collective-permute-start.7 = (bf16[32,16,128]{2,1,0:T(8,128)(2,1)S(1)}, bf16[32,16,128]{2,1,0:T(8,128)(2,1)S(1)}, u32[]{:S(2)}, u32[]{:S(2)}) collective-permute-start(bf16[32,16,128]{2,1,0:T(8,128)(2,1)S(1)} %get-tuple-element.38.after_ref), channel_id=1, source_target_pairs={{0,128},{1,129},{2,130},{3,131},{4,132},{5,133},{6,134},{7,135},{8... | collective-permute-start | bytes 393224 | tf_op jit(solution)/shard_map/ppermute | solution.py:237
  53.6 13.2 %collective-permute-start.8 = (bf16[16,128]{1,0:T(8,128)(2,1)S(1)}, bf16[16,128]{1,0:T(8,128)(2,1)S(1)}, u32[]{:S(2)}, u32[]{:S(2)}) collective-permute-start(bf16[16,128]{1,0:T(8,128)(2,1)S(1)} %get-tuple-element.44), channel_id=1, source_target_pairs={{0,1},{1,2},{2,3},{3,4},{4,5},{5,6},{6,7},{7,8},{8,9},{9,10},{10,1... | collective-permute-start | bytes 12296 | tf_op jit(solution)/shard_map/ppermute | solution.py:233
  66.9 2.1 %collective-permute-start.9 = (bf16[16,128]{1,0:T(8,128)(2,1)S(1)}, bf16[16,128]{1,0:T(8,128)(2,1)S(1)}, u32[]{:S(2)}, u32[]{:S(2)}) collective-permute-start(bf16[16,128]{1,0:T(8,128)(2,1)S(1)} %get-tuple-element.43), channel_id=1, source_target_pairs={{1,0},{2,1},{3,2},{4,3},{5,4},{6,5},{7,6},{8,7},{9,8},{10,9},{11,1... | collective-permute-start | bytes 12296 | tf_op jit(solution)/shard_map/ppermute | solution.py:234
  69.1 4.9 %collective-permute-done.9.after_ref = bf16[16,128]{1,0:T(8,128)(2,1)S(1)} collective-permute-done((bf16[16,128]{1,0:T(8,128)(2,1)S(1)}, bf16[16,128]{1,0:T(8,128)(2,1)S(1)}, u32[]{:S(2)}, u32[]{:S(2)}) %collective-permute-start.9) | collective-permute-done | bytes 4128 | tf_op jit(solution)/shard_map/ppermute | solution.py:234
  73.9 4.1 %near.1.near_ref = f32[2,32,16,128]{3,2,1,0:T(8,128)S(1)} custom-call(bf16[2,32,16,128]{3,2,1,0:T(8,128)(2,1)S(1)} %get-tuple-element.42.halves_ref, bf16[16,128]{1,0:T(8,128)(2,1)S(1)} %collective-permute-done.8.before_ref, bf16[16,128]{1,0:T(8,128)(2,1)S(1)} %collective-permute-done.9.after_ref, bf16[3,32,32,256]{3,2,1,0:T(8,128)(2,1)S(1)} %copy-done.2), custom_call_target="tpu_custom_call" | custom-call | flops 4000000 | bytes 3145728 | tf_op jit(solution)/shard_map/near/pallas_call | solution.py:205
  78.0 2.6 %arrange.17.arranged_ref = bf16[32,2,64,128]{3,2,1,0:T(8,128)(2,1)S(1)} custom-call(bf16[10,64,64,128]{3,2,1,0:T(8,128)(2,1)S(1)} %copy-done.1, bf16[32,16,128]{2,1,0:T(8,128)(2,1)S(1)} %get-tuple-element.38.after_ref), custom_call_target="tpu_custom_call" | custom-call | flops 2000000 | bytes 2097152 | tf_op jit(solution)/shard_map/arrange/pallas_call | solution.py:168
  80.7 2.6 %arrange.16.arranged_ref = bf16[32,2,64,128]{3,2,1,0:T(8,128)(2,1)S(1)} custom-call(bf16[10,64,64,128]{3,2,1,0:T(8,128)(2,1)S(1)} %copy-done.1, bf16[32,16,128]{2,1,0:T(8,128)(2,1)S(1)} %collective-permute-done.7.after_ref.received_ref), custom_call_target="tpu_custom_call" | custom-call | flops 2000000 | bytes 2097152 | tf_op jit(solution)/shard_map/arrange/pallas_call | solution.py:168
  83.9 1.9 %root.1 = bf16[16,32,256]{2,1,0:T(8,128)(2,1)} custom-call(bf16[32,2,64,128]{3,2,1,0:T(8,128)(2,1)S(1)} %arrange.16.arranged_ref, bf16[32,16,128]{2,1,0:T(8,128)(2,1)S(1)} %get-tuple-element.40.first_ref, bf16[32,16,128]{2,1,0:T(8,128)(2,1)S(1)} %get-tuple-element.41.second_ref, f32[2,32,16,128]{3,2,1,0:T(8,128)S(1)} %near.1.near_ref), custom_call_target="tpu_custom_call" | custom-call | tf_op jit(solution)/shard_map/root/pallas_call | solution.py:218
  (17 shorter events, 2.8 us)
Async XLA Ops:
  0.0 4.0 %copy-start = (bf16[10,64,64,128]{3,2,1,0:T(8,128)(2,1)S(1)}, bf16[10,64,64,128]{3,2,1,0:T(8,128)(2,1)}, u32[]{:S(2)}) copy-start(bf16[10,64,64,128]{3,2,1,0:T(8,128)(2,1)} %weights_ref.19) | copy-start | bytes 31457284
  4.0 0.9 %copy-start.3 = (bf16[16,32,256]{2,1,0:T(8,128)(2,1)S(1)}, bf16[16,32,256]{2,1,0:T(8,128)(2,1)}, u32[]{:S(2)}) copy-start(bf16[16,32,256]{2,1,0:T(8,128)(2,1)} %vectors_ref.1) | copy-start | bytes 786436
  5.0 4.1 %copy-start.1 = (bf16[10,64,64,128]{3,2,1,0:T(8,128)(2,1)S(1)}, bf16[10,64,64,128]{3,2,1,0:T(8,128)(2,1)}, u32[]{:S(2)}) copy-start(bf16[10,64,64,128]{3,2,1,0:T(8,128)(2,1)} %weights_ref.19) | copy-start | bytes 31457284
  8.3 3.4 %collective-permute-start = (bf16[32,16,128]{2,1,0:T(8,128)(2,1)S(1)}, bf16[32,16,128]{2,1,0:T(8,128)(2,1)S(1)}, u32[]{:S(2)}, u32[]{:S(2)}) collective-permute-start(bf16[32,16,128]{2,1,0:T(8,128)(2,1)S(1)} %get-tuple-element.24.after_ref), channel_id=1, source_target_pairs={{0,1},{1,0},{2,3},{3,2},{4,5},{5,4},{6,7},{7,6},{8,9},{9,8},{10,11... | collective-permute-start | bytes 393224 | tf_op jit(solution)/shard_map/ppermute | solution.py:237
  12.3 4.5 %collective-permute-start.1 = (bf16[32,16,128]{2,1,0:T(8,128)(2,1)S(1)}, bf16[32,16,128]{2,1,0:T(8,128)(2,1)S(1)}, u32[]{:S(2)}, u32[]{:S(2)}) collective-permute-start(bf16[32,16,128]{2,1,0:T(8,128)(2,1)S(1)} %get-tuple-element.26.after_ref), channel_id=1, source_target_pairs={{0,2},{1,3},{2,0},{3,1},{4,6},{5,7},{6,4},{7,5},{8,10},{9,11},{10,... | collective-permute-start | bytes 393224 | tf_op jit(solution)/shard_map/ppermute | solution.py:237
  17.5 5.4 %collective-permute-start.2 = (bf16[32,16,128]{2,1,0:T(8,128)(2,1)S(1)}, bf16[32,16,128]{2,1,0:T(8,128)(2,1)S(1)}, u32[]{:S(2)}, u32[]{:S(2)}) collective-permute-start(bf16[32,16,128]{2,1,0:T(8,128)(2,1)S(1)} %get-tuple-element.28.after_ref), channel_id=1, source_target_pairs={{0,4},{1,5},{2,6},{3,7},{4,0},{5,1},{6,2},{7,3},{8,12},{9,13},{10,... | collective-permute-start | bytes 393224 | tf_op jit(solution)/shard_map/ppermute | solution.py:237
  23.5 4.2 %collective-permute-start.3 = (bf16[32,16,128]{2,1,0:T(8,128)(2,1)S(1)}, bf16[32,16,128]{2,1,0:T(8,128)(2,1)S(1)}, u32[]{:S(2)}, u32[]{:S(2)}) collective-permute-start(bf16[32,16,128]{2,1,0:T(8,128)(2,1)S(1)} %get-tuple-element.30.after_ref), channel_id=1, source_target_pairs={{0,8},{1,9},{2,10},{3,11},{4,12},{5,13},{6,14},{7,15},{8,0},{9,1},... | collective-permute-start | bytes 393224 | tf_op jit(solution)/shard_map/ppermute | solution.py:237
  28.4 6.2 %collective-permute-start.4 = (bf16[32,16,128]{2,1,0:T(8,128)(2,1)S(1)}, bf16[32,16,128]{2,1,0:T(8,128)(2,1)S(1)}, u32[]{:S(2)}, u32[]{:S(2)}) collective-permute-start(bf16[32,16,128]{2,1,0:T(8,128)(2,1)S(1)} %get-tuple-element.32.after_ref), channel_id=1, source_target_pairs={{0,16},{1,17},{2,18},{3,19},{4,20},{5,21},{6,22},{7,23},{8,24},{9,... | collective-permute-start | bytes 393224 | tf_op jit(solution)/shard_map/ppermute | solution.py:237
  35.2 38.7 %copy-start.2 = (bf16[3,32,32,256]{3,2,1,0:T(8,128)(2,1)S(1)}, bf16[3,32,32,256]{3,2,1,0:T(8,128)(2,1)}, u32[]{:S(2)}) copy-start(bf16[3,32,32,256]{3,2,1,0:T(8,128)(2,1)} %blocks_ref.1) | copy-start | bytes 4718596
  35.2 4.4 %collective-permute-start.5 = (bf16[32,16,128]{2,1,0:T(8,128)(2,1)S(1)}, bf16[32,16,128]{2,1,0:T(8,128)(2,1)S(1)}, u32[]{:S(2)}, u32[]{:S(2)}) collective-permute-start(bf16[32,16,128]{2,1,0:T(8,128)(2,1)S(1)} %get-tuple-element.34.after_ref), channel_id=1, source_target_pairs={{0,32},{1,33},{2,34},{3,35},{4,36},{5,37},{6,38},{7,39},{8,40},{9,... | collective-permute-start | bytes 393224 | tf_op jit(solution)/shard_map/ppermute | solution.py:237
  40.3 5.9 %collective-permute-start.6 = (bf16[32,16,128]{2,1,0:T(8,128)(2,1)S(1)}, bf16[32,16,128]{2,1,0:T(8,128)(2,1)S(1)}, u32[]{:S(2)}, u32[]{:S(2)}) collective-permute-start(bf16[32,16,128]{2,1,0:T(8,128)(2,1)S(1)} %get-tuple-element.36.after_ref), channel_id=1, source_target_pairs={{0,64},{1,65},{2,66},{3,67},{4,68},{5,69},{6,70},{7,71},{8,72},{9,... | collective-permute-start | bytes 393224 | tf_op jit(solution)/shard_map/ppermute | solution.py:237
  46.8 33.8 %collective-permute-start.7 = (bf16[32,16,128]{2,1,0:T(8,128)(2,1)S(1)}, bf16[32,16,128]{2,1,0:T(8,128)(2,1)S(1)}, u32[]{:S(2)}, u32[]{:S(2)}) collective-permute-start(bf16[32,16,128]{2,1,0:T(8,128)(2,1)S(1)} %get-tuple-element.38.after_ref), channel_id=1, source_target_pairs={{0,128},{1,129},{2,130},{3,131},{4,132},{5,133},{6,134},{7,135},{8... | collective-permute-start | bytes 393224 | tf_op jit(solution)/shard_map/ppermute | solution.py:237
  53.6 15.4 %collective-permute-start.8 = (bf16[16,128]{1,0:T(8,128)(2,1)S(1)}, bf16[16,128]{1,0:T(8,128)(2,1)S(1)}, u32[]{:S(2)}, u32[]{:S(2)}) collective-permute-start(bf16[16,128]{1,0:T(8,128)(2,1)S(1)} %get-tuple-element.44), channel_id=1, source_target_pairs={{0,1},{1,2},{2,3},{3,4},{4,5},{5,6},{6,7},{7,8},{8,9},{9,10},{10,1... | collective-permute-start | bytes 12296 | tf_op jit(solution)/shard_map/ppermute | solution.py:233
  66.9 7.0 %collective-permute-start.9 = (bf16[16,128]{1,0:T(8,128)(2,1)S(1)}, bf16[16,128]{1,0:T(8,128)(2,1)S(1)}, u32[]{:S(2)}, u32[]{:S(2)}) collective-permute-start(bf16[16,128]{1,0:T(8,128)(2,1)S(1)} %get-tuple-element.43), channel_id=1, source_target_pairs={{1,0},{2,1},{3,2},{4,3},{5,4},{6,5},{7,6},{8,7},{9,8},{10,9},{11,1... | collective-permute-start | bytes 12296 | tf_op jit(solution)/shard_map/ppermute | solution.py:234
where the time goes:
time: 86 us; the launch traced here: 85.8 us
  Pallas kernels  38.2 us (44%)
  starting transfers between devices  34.8 us (40%)
  waiting for transfers between devices  7.73 us (9%)
  local copies, waits for them, and re-layouts  4.96 us (6%)
    pallas_call x9, Pallas kernels, arrange(): pl.pallas_call(arrange_kernel, grid=(1,), out_shape=jax.ShapeDtypeStruct(...  23.7 us
    ppermute x8, starting transfers between devices, shards(): lax.ppermute(sending, 'rows', [(i, i ^ 1 << level) for i in range(count)])  19.4 us
    ppermute x1, starting transfers between devices, shards(): lax.ppermute(halves[1, QUADS - 1], 'rows', [(i, i + 1) for i in range(cou...  13.2 us
    pallas_call x8, Pallas kernels, level_step(): pl.pallas_call(functools.partial(level_kernel, level, last), out_shape=(P...  5.25 us
    unnamed x8, local copies, waits for them, and re-layouts  4.96 us
    ppermute x1, waiting for transfers between devices, shards(): lax.ppermute(halves[0, 0], 'rows', [(i + 1, i) for i in range(count - 1)])  4.88 us
    pallas_call x1, Pallas kernels, near_field(): pl.pallas_call(near_kernel, out_shape=jax.ShapeDtypeStruct((2, QUADS, RHS...  4.06 us
    pallas_call x1, Pallas kernels, head(): pl.pallas_call(head_kernel, grid=(1,), out_shape=(PAYLOAD, PAYLOAD, jax.S...  3.33 us
  transfers between devices with their start and end apart: 10, of which 5 were waited for; matrix products, arithmetic and copies ran while one was open for 0% of the time, Pallas kernels for 29%

commit v1 on v0

v1 whole, which is shorter than its diff:
```python
import functools

import jax
import jax.numpy as jnp
from jax import lax
from jax.experimental import pallas as pl
from jax.experimental.pallas import tpu as pltpu
from jax.sharding import PartitionSpec as P

RHS = 16
RANK = 32
HALF = 128
QUADS = 32
LANES = 128
PITCH = LANES + 1
CHAINS = 2
SLOTS = QUADS // CHAINS
PIECES = 4
NEAR_LEVEL = 2
BF16 = jnp.bfloat16
F32 = jnp.float32


def lane_bit(shape, step, dtype=jnp.int32):
    return (lax.broadcasted_iota(dtype, shape, len(shape) - 1) & step) != 0


def swap_major_lanes(blocks):
    blocks = list(blocks)
    shape = blocks[0].shape
    for step in (16, 8, 4, 2, 1):
        upper = lane_bit(shape, step)
        for low in range(QUADS):
            if low & step:
                continue
            high = low + step
            first, second = blocks[low], blocks[high]
            blocks[low] = jnp.where(upper, pltpu.roll(second, step, 1), first)
            blocks[high] = jnp.where(upper, second, pltpu.roll(first, LANES - step, 1))
    return blocks


def arrange_section(weights_ref, arranged_ref, turned_ref):
    for a in range(RANK):
        both = jnp.concatenate([weights_ref[a], weights_ref[RANK + a]], axis=0)
        turned_ref[a * PITCH : a * PITCH + LANES, :] = both.T.astype(F32)
    for q in range(QUADS):
        rows = [turned_ref[pl.ds(part * QUADS + q, RANK, stride=PITCH), :] for part in range(4)]
        turned = jnp.concatenate(rows, axis=0).astype(BF16).T
        arranged_ref[q] = turned.reshape(2, 2 * RANK, LANES)


def diagonal_blocks(block, group):
    lane = lax.broadcasted_iota(jnp.int32, block.shape, 1)
    return jnp.where((lane >> 5) & 3 == group, block, jnp.zeros_like(block))


def section_quad(arranged_ref, q, lower, higher):
    tiles = []
    for half in range(2):
        rows = slice(half * RANK, (half + 1) * RANK)
        dense = jnp.concatenate([arranged_ref[q, 0, rows, :], arranged_ref[q, 1, rows, :]], axis=1)
        tiles += [diagonal_blocks(dense, group) for group in range(4)]
    matrix = jnp.concatenate(tiles, axis=0)
    stack = jnp.concatenate([lower, higher], axis=1)
    return jnp.dot(stack, matrix, preferred_element_type=F32)


def emit_halves(mixed, q, upper, own_ref, send_ref):
    first, second = mixed[:, :LANES], mixed[:, LANES:]
    own_ref[q] = jnp.where(upper, second, first)
    send_ref[q] = jnp.where(upper, first, second)


def level_bit(level):
    return (lax.axis_index("rows") >> level) & 1 == 1


def edge_lanes(part):
    return lax.broadcasted_iota(jnp.int32, (RHS, LANES), 1) >> 5 == part


def head_kernel(vectors_hbm, weights_hbm, *refs):
    outputs, scratch = refs[: 2 * CHAINS + 1], refs[2 * CHAINS + 1 :]
    halves_ref = outputs[2 * CHAINS]
    vectors_ref, weights_ref, rows_ref, turned_ref, arranged_ref, sems = scratch
    copy = pltpu.make_async_copy(vectors_hbm, vectors_ref, sems.at[0])
    copy.start()
    pieces = []
    for piece in range(PIECES):
        size = RANK // PIECES
        for half in range(2):
            rows = pl.ds(half * RANK + piece * size, size)
            pieces.append(
                pltpu.make_async_copy(
                    weights_hbm.at[0, rows], weights_ref.at[rows], sems.at[1 + 2 * piece + half]
                )
            )
            pieces[-1].start()
    copy.wait()
    for half in range(2):
        lanes = slice(half * HALF, (half + 1) * HALF)
        for r in range(RHS):
            start = r * (RANK + 1)
            rows_ref[half, start : start + RANK, :] = vectors_ref[r, :, lanes].astype(F32)
        blocks = [rows_ref[half, pl.ds(a, RHS, stride=RANK + 1), :].astype(BF16) for a in range(RANK)]
        for q, block in enumerate(swap_major_lanes(blocks)):
            halves_ref[half, q] = block
    for piece in pieces:
        piece.wait()
    arrange_section(weights_ref, arranged_ref, turned_ref)
    upper = level_bit(0)
    for chain in range(CHAINS):
        own_ref, send_ref = outputs[2 * chain : 2 * chain + 2]
        for slot in range(SLOTS):
            q = chain * SLOTS + slot
            mixed = section_quad(arranged_ref, q, halves_ref[0, q], halves_ref[1, q]).astype(BF16)
            emit_halves(mixed, slot, upper, own_ref, send_ref)
        if chain == 0:
            edge = jnp.where(edge_lanes(0), halves_ref[0, 0], halves_ref[1, QUADS - 1])
            own_ref[SLOTS] = edge
            send_ref[SLOTS] = edge


def arrange_kernel(index, weights_ref, after_ref, arranged_ref, turned_ref):
    del after_ref
    arrange_section(weights_ref.at[index], arranged_ref, turned_ref)


def level_kernel(level, last, chain, *refs):
    arranged_ref, kept_ref, received_ref = refs[:3]
    outputs = refs[len(refs) - (3 if chain == 0 else 2) :]
    own_ref, send_ref = outputs[:2]
    upper = level_bit(level)
    next_upper = False if last else level_bit(level + 1)
    for slot in range(SLOTS):
        kept, received = kept_ref[slot], received_ref[slot]
        lower = jnp.where(upper, received, kept)
        higher = jnp.where(upper, kept, received)
        mixed = section_quad(arranged_ref, chain * SLOTS + slot, lower, higher).astype(BF16)
        emit_halves(mixed, slot, next_upper, own_ref, send_ref)
    if chain == 0:
        beside_ref, new_beside_ref = refs[3], outputs[2]
        inner = lax.axis_index("rows") & (2**level - 1)
        above = jnp.logical_and(jnp.logical_not(upper), inner == 2**level - 1)
        below = jnp.logical_and(upper, inner == 0)
        kept, received = kept_ref[SLOTS], received_ref[SLOTS]
        first, final = edge_lanes(0), edge_lanes(3)
        beside = jnp.where(jnp.logical_and(first, above), received, beside_ref[...])
        new_beside_ref[...] = jnp.where(jnp.logical_and(final, below), received, beside)
        if not last:
            theirs = jnp.logical_xor(first, jnp.logical_not(upper))
            edge = jnp.where(theirs, received, kept)
            own_ref[SLOTS] = edge
            send_ref[SLOTS] = edge


def near_kernel(halves_ref, blocks_ref, after_ref, near_ref, border_ref, arranged_ref, turned_ref):
    del after_ref
    first_group, last_group = edge_lanes(0), edge_lanes(3)
    zeros = jnp.zeros((RHS, LANES), BF16)
    for half in range(2):
        lanes = slice(half * HALF, (half + 1) * HALF)
        for a in range(RANK):
            shifts = [blocks_ref[shift, a, :, lanes] for shift in (0, 1, 2, 0)]
            turned = jnp.concatenate(shifts, axis=0).T.astype(F32)
            turned_ref[a * PITCH : a * PITCH + LANES, :] = turned
        for q in range(QUADS):
            rows = [turned_ref[pl.ds(part * QUADS + q, RANK, stride=PITCH), :] for part in range(4)]
            arranged_ref[q] = jnp.concatenate(rows, axis=0).astype(BF16).T
        if half == 0:
            border_ref[0] = arranged_ref[0, RANK : 2 * RANK, :]
        else:
            border_ref[1] = arranged_ref[QUADS - 1, 2 * RANK : 3 * RANK, :]
        edge_before = zeros if half == 0 else halves_ref[0, QUADS - 1]
        edge_after = zeros if half == 1 else halves_ref[1, 0]
        for q in range(QUADS):
            centre = halves_ref[half, q]
            if q > 0:
                before = halves_ref[half, q - 1]
            else:
                final = halves_ref[half, QUADS - 1]
                before = pltpu.roll(jnp.where(last_group, edge_before, final), RANK, 1)
            if q < QUADS - 1:
                after = halves_ref[half, q + 1]
            else:
                first = halves_ref[half, 0]
                after = pltpu.roll(jnp.where(first_group, edge_after, first), LANES - RANK, 1)
            tiles = [
                diagonal_blocks(arranged_ref[q, shift * RANK : (shift + 1) * RANK, :], part)
                for shift in range(3)
                for part in range(4)
            ]
            matrix = jnp.concatenate(tiles, axis=0)
            stack = jnp.concatenate([centre, before, after], axis=1)
            near_ref[half, q] = jnp.dot(stack, matrix, preferred_element_type=F32)


def border_term(border_ref, beside_ref, half):
    zeros = jnp.zeros((RHS, LANES), BF16)
    if half == 0:
        edge = pltpu.roll(jnp.where(edge_lanes(3), beside_ref[...], zeros), RANK, 1)
    else:
        edge = pltpu.roll(jnp.where(edge_lanes(0), beside_ref[...], zeros), LANES - RANK, 1)
    tiles = [diagonal_blocks(border_ref[half], part) for part in range(4)]
    return jnp.dot(edge, jnp.concatenate(tiles, axis=0), preferred_element_type=F32)


def root_kernel(*refs):
    arranged_ref, near_ref, border_ref, beside_ref = refs[:4]
    stacks, (product_ref, rows_ref) = refs[4 : 4 + 2 * CHAINS], refs[4 + 2 * CHAINS :]
    blocks = [[], []]
    for q in range(QUADS):
        chain, slot = divmod(q, SLOTS)
        mixed = section_quad(arranged_ref, q, stacks[2 * chain][slot], stacks[2 * chain + 1][slot])
        for half in range(2):
            total = mixed[:, half * LANES : (half + 1) * LANES] + near_ref[half, q]
            if q == half * (QUADS - 1):
                total = total + border_term(border_ref, beside_ref, half)
            blocks[half].append(total.astype(BF16))
    for half in range(2):
        lanes = slice(half * HALF, (half + 1) * HALF)
        for a, block in enumerate(swap_major_lanes(blocks[half])):
            start = a * (RHS + 1)
            rows_ref[half, start : start + RHS, :] = block.astype(F32)
        for r in range(RHS):
            product_ref[r, :, lanes] = rows_ref[half, pl.ds(r, RANK, stride=RHS + 1), :].astype(BF16)


VMEM_SPEC = pl.BlockSpec(memory_space=pltpu.VMEM)
ANY_SPEC = pl.BlockSpec(memory_space=pl.ANY)
HBM_SPEC = pl.BlockSpec(memory_space=pltpu.HBM)
TURNED = pltpu.VMEM((RANK * PITCH, LANES), F32)
ARRANGED = (QUADS, 2, 2 * RANK, LANES)
EDGE = jax.ShapeDtypeStruct((RHS, LANES), BF16)


def payload(chain, edge=True):
    return jax.ShapeDtypeStruct((SLOTS + (edge and chain == 0), RHS, LANES), BF16)


def params(mib):
    return pltpu.CompilerParams(vmem_limit_bytes=mib * 2**20)


def in_hbm(array):
    return pltpu.with_memory_space_constraint(array, pltpu.HBM)


def arrange(factors, index, after):
    return pl.pallas_call(
        functools.partial(arrange_kernel, index),
        out_shape=jax.ShapeDtypeStruct(ARRANGED, BF16),
        in_specs=[VMEM_SPEC, ANY_SPEC],
        out_specs=VMEM_SPEC,
        scratch_shapes=[TURNED],
        compiler_params=params(16),
        cost_estimate=pl.CostEstimate(flops=2 * 10**6, bytes_accessed=2 * 2**20, transcendentals=0),
        name="arrange",
    )(factors, after)


def head(vectors, factors):
    outs = [payload(chain) for chain in range(CHAINS) for _ in range(2)]
    *pairs, halves = pl.pallas_call(
        head_kernel,
        out_shape=(*outs, jax.ShapeDtypeStruct((2, QUADS, RHS, LANES), BF16)),
        in_specs=[HBM_SPEC, HBM_SPEC],
        out_specs=(VMEM_SPEC,) * (2 * CHAINS + 1),
        scratch_shapes=[
            pltpu.VMEM((RHS, RANK, 2 * HALF), BF16),
            pltpu.VMEM((2 * RANK, 2 * RANK, HALF), BF16),
            pltpu.VMEM((2, RHS * (RANK + 1), LANES), F32),
            TURNED,
            pltpu.VMEM(ARRANGED, BF16),
            pltpu.SemaphoreType.DMA((1 + 2 * PIECES,)),
        ],
        compiler_params=params(14),
        name="head",
    )(in_hbm(vectors), in_hbm(factors))
    return pairs[::2], pairs[1::2], halves


def level_step(level, last, chain, arranged, kept, received, beside, after=()):
    edges = [beside] if chain == 0 else []
    outs = [payload(chain, not last)] * 2 + [EDGE] * len(edges)
    return pl.pallas_call(
        functools.partial(level_kernel, level, last, chain),
        out_shape=tuple(outs),
        in_specs=[VMEM_SPEC] * (3 + len(edges)) + [ANY_SPEC] * len(after),
        out_specs=(VMEM_SPEC,) * len(outs),
        compiler_params=params(6),
        name="level",
    )(arranged, kept, received, *edges, *after)


def near_field(halves, neighbor_blocks, after):
    return pl.pallas_call(
        near_kernel,
        out_shape=(
            jax.ShapeDtypeStruct((2, QUADS, RHS, LANES), F32),
            jax.ShapeDtypeStruct((2, RANK, LANES), BF16),
        ),
        in_specs=[VMEM_SPEC, VMEM_SPEC, ANY_SPEC],
        out_specs=(VMEM_SPEC, VMEM_SPEC),
        scratch_shapes=[pltpu.VMEM((QUADS, LANES, LANES), BF16), TURNED],
        compiler_params=params(12),
        cost_estimate=pl.CostEstimate(flops=4 * 10**6, bytes_accessed=3 * 2**20, transcendentals=0),
        name="near",
    )(halves, neighbor_blocks, after)


def root(arranged, near, border, beside, stacks):
    return pl.pallas_call(
        root_kernel,
        out_shape=jax.ShapeDtypeStruct((RHS, RANK, 2 * HALF), BF16),
        in_specs=[VMEM_SPEC] * (4 + len(stacks)),
        out_specs=VMEM_SPEC,
        scratch_shapes=[pltpu.VMEM((2, (RHS + 1) * RANK, LANES), F32)],
        compiler_params=params(12),
        name="root",
    )(arranged, near, border, beside, *stacks)


def shards(vectors, factors, neighbor_blocks):
    level_count = factors.shape[0] - 2
    count = lax.axis_size("rows")
    kept, sending, halves = head(vectors, factors)
    beside = jnp.zeros(EDGE.shape, EDGE.dtype)
    for level in range(level_count):
        last = level == level_count - 1
        partners = [(i, i ^ (1 << level)) for i in range(count)]
        received = [lax.ppermute(part, "rows", partners) for part in sending]
        arranged = arrange(factors, level + 1, sending[-1])
        extra = ()
        if level == NEAR_LEVEL:
            near, border = near_field(halves, neighbor_blocks, sending[-1])
            extra = (near,)
        if last:
            root_arranged = arrange(factors, level_count + 1, sending[-1])
            extra = (root_arranged,)
        for chain in range(CHAINS):
            outs = level_step(
                level, last, chain, arranged, kept[chain], received[chain], beside, extra * (chain == 0)
            )
            kept[chain], sending[chain] = outs[:2]
            if chain == 0:
                beside = outs[2]
    stacks = [stack for pair in zip(kept, sending) for stack in pair]
    return root(root_arranged, near, border, beside, stacks)


def solution(mesh):
    placed = (P(None, None, "rows"), P(None, None, None, "rows"), P(None, None, None, "rows"))
    return jax.shard_map(
        shards, mesh=mesh, in_specs=placed, out_specs=P(None, None, "rows"), check_vma=False
    )
```

time: 86 us -> 60.7 us (0.71)
  the two profiles are of different devices: /device:TPU:7 before, /device:TPU:6 now
where the time goes in v1:
time: 60.7 us; the launch traced here: 59.6 us
  starting transfers between devices  33 us (54%)
  Pallas kernels  18.3 us (30%)
  waiting for transfers between devices  7.24 us (12%)
  local copies, waits for them, and re-layouts  0.93 us (2%)
    ppermute x16, starting transfers between devices, shards(): received = [lax.ppermute(part, 'rows', partners) for part in sending]  33 us
    ppermute x16, waiting for transfers between devices, shards(): received = [lax.ppermute(part, 'rows', partners) for part in sending]  7.24 us
    pallas_call x16, Pallas kernels, level_step(): pl.pallas_call(functools.partial(level_kernel, level, last, chain), out_s...  6.17 us
    pallas_call x9, Pallas kernels, arrange(): pl.pallas_call(functools.partial(arrange_kernel, index), out_shape=jax.Sh...  5.74 us
    pallas_call x1, Pallas kernels, head(): pl.pallas_call(head_kernel, out_shape=(*outs, jax.ShapeDtypeStruct((2, QU...  2.88 us
    pallas_call x1, Pallas kernels, root(): pl.pallas_call(root_kernel, out_shape=jax.ShapeDtypeStruct((RHS, RANK, 2...  1.84 us
    pallas_call x1, Pallas kernels, near_field(): pl.pallas_call(near_kernel, out_shape=(jax.ShapeDtypeStruct((2, QUADS, RH...  1.65 us
  transfers between devices with their start and end apart: 16, of which 6 were waited for; matrix products, arithmetic and copies ran while one was open for 0% of the time, Pallas kernels for 22%

profile of v1, /device:TPU:6, one launch (start us, length us, event | category | flops | bytes accessed | tf_op | source)
XLA Modules:
  0.0 59.6 jit_solution(15179418843456871191)
XLA Ops:
  0.0 2.9 %head.1 = (bf16[17,16,128]{2,1,0:T(8,128)(2,1)S(1)}, bf16[17,16,128]{2,1,0:T(8,128)(2,1)S(1)}, bf16[16,16,128]{2,1,0:T(8,128)(2,1)S(1)}, bf16[16,16,128]{2,1,0:T(8,128)(2,1)S(1)}, bf16[2,32,16,128]{3,2,1,0:T(8,128)(2,1)S(1)}) custom-call(bf16[16,32,256]{2,1,0:T(8,128)(2,1)} %vectors_hbm.1, bf16[10,64,64,128]{3,2,1,0:T(8,128)(2,1)} %weights_ref.17), custom_call_target="tpu_custom_call" | custom-call | tf_op jit(solution)/shard_map/head/pallas_call | solution.py:265
  3.5 0.9 %copy-done = bf16[10,64,64,128]{3,2,1,0:T(8,128)(2,1)S(1)} copy-done((bf16[10,64,64,128]{3,2,1,0:T(8,128)(2,1)S(1)}, bf16[10,64,64,128]{3,2,1,0:T(8,128)(2,1)}, u32[]{:S(2)}) %copy-start) | copy-done | bytes 10485784
  4.4 0.6 %arrange.9.refs_0_ = bf16[32,2,64,128]{3,2,1,0:T(8,128)(2,1)S(1)} custom-call(bf16[10,64,64,128]{3,2,1,0:T(8,128)(2,1)S(1)} %copy-done, bf16[16,16,128]{2,1,0:T(8,128)(2,1)S(1)} %get-tuple-element.52.after_ref), custom_call_target="tpu_custom_call" | custom-call | flops 2000000 | bytes 2097152 | tf_op jit(solution)/shard_map/arrange/pallas_call | solution.py:251
  5.5 0.9 %collective-permute-start.8 = (bf16[17,16,128]{2,1,0:T(8,128)(2,1)S(1)}, bf16[17,16,128]{2,1,0:T(8,128)(2,1)S(1)}, u32[]{:S(2)}, u32[]{:S(2)}) collective-permute-start(bf16[17,16,128]{2,1,0:T(8,128)(2,1)S(1)} %get-tuple-element.73), channel_id=1, source_target_pairs={{0,2},{1,3},{2,0},{3,1},{4,6},{5,7},{6,4},{7,5},{8,10},{9,11},{10,... | collective-permute-start | bytes 208904 | tf_op jit(solution)/shard_map/ppermute | solution.py:333
  6.8 1.3 %collective-permute-start.1 = (bf16[16,16,128]{2,1,0:T(8,128)(2,1)S(1)}, bf16[16,16,128]{2,1,0:T(8,128)(2,1)S(1)}, u32[]{:S(2)}, u32[]{:S(2)}) collective-permute-start(bf16[16,16,128]{2,1,0:T(8,128)(2,1)S(1)} %get-tuple-element.54.after_ref), channel_id=1, source_target_pairs={{0,2},{1,3},{2,0},{3,1},{4,6},{5,7},{6,4},{7,5},{8,10},{9,11},{10,... | collective-permute-start | bytes 196616 | tf_op jit(solution)/shard_map/ppermute | solution.py:333
  8.1 0.6 %arrange.10.refs_0_ = bf16[32,2,64,128]{3,2,1,0:T(8,128)(2,1)S(1)} custom-call(bf16[10,64,64,128]{3,2,1,0:T(8,128)(2,1)S(1)} %copy-done, bf16[16,16,128]{2,1,0:T(8,128)(2,1)S(1)} %get-tuple-element.54.after_ref), custom_call_target="tpu_custom_call" | custom-call | flops 2000000 | bytes 2097152 | tf_op jit(solution)/shard_map/arrange/pallas_call | solution.py:251
  8.7 1.8 %collective-permute-done.8.refs_2_ = bf16[17,16,128]{2,1,0:T(8,128)(2,1)S(1)} collective-permute-done((bf16[17,16,128]{2,1,0:T(8,128)(2,1)S(1)}, bf16[17,16,128]{2,1,0:T(8,128)(2,1)S(1)}, u32[]{:S(2)}, u32[]{:S(2)}) %collective-permute-start.8) | collective-permute-done | bytes 69664 | tf_op jit(solution)/shard_map/ppermute | solution.py:333
  10.8 1.4 %collective-permute-start.9 = (bf16[17,16,128]{2,1,0:T(8,128)(2,1)S(1)}, bf16[17,16,128]{2,1,0:T(8,128)(2,1)S(1)}, u32[]{:S(2)}, u32[]{:S(2)}) collective-permute-start(bf16[17,16,128]{2,1,0:T(8,128)(2,1)S(1)} %get-tuple-element.76), channel_id=1, source_target_pairs={{0,4},{1,5},{2,6},{3,7},{4,0},{5,1},{6,2},{7,3},{8,12},{9,13},{10,... | collective-permute-start | bytes 208904 | tf_op jit(solution)/shard_map/ppermute | solution.py:333
  12.6 2.3 %collective-permute-start.2 = (bf16[16,16,128]{2,1,0:T(8,128)(2,1)S(1)}, bf16[16,16,128]{2,1,0:T(8,128)(2,1)S(1)}, u32[]{:S(2)}, u32[]{:S(2)}) collective-permute-start(bf16[16,16,128]{2,1,0:T(8,128)(2,1)S(1)} %get-tuple-element.56.after_ref), channel_id=1, source_target_pairs={{0,4},{1,5},{2,6},{3,7},{4,0},{5,1},{6,2},{7,3},{8,12},{9,13},{10,... | collective-permute-start | bytes 196616 | tf_op jit(solution)/shard_map/ppermute | solution.py:333
  14.9 0.6 %arrange.11.refs_0_ = bf16[32,2,64,128]{3,2,1,0:T(8,128)(2,1)S(1)} custom-call(bf16[10,64,64,128]{3,2,1,0:T(8,128)(2,1)S(1)} %copy-done, bf16[16,16,128]{2,1,0:T(8,128)(2,1)S(1)} %get-tuple-element.56.after_ref), custom_call_target="tpu_custom_call" | custom-call | flops 2000000 | bytes 2097152 | tf_op jit(solution)/shard_map/arrange/pallas_call | solution.py:251
  15.6 1.7 %near.1 = (f32[2,32,16,128]{3,2,1,0:T(8,128)S(1)}, bf16[2,32,128]{2,1,0:T(8,128)(2,1)S(1)}) custom-call(bf16[2,32,16,128]{3,2,1,0:T(8,128)(2,1)S(1)} %get-tuple-element.67.halves_ref, bf16[3,32,32,256]{3,2,1,0:T(8,128)(2,1)S(1)} %copy-done.1, bf16[16,16,128]{2,1,0:T(8,128)(2,1)S(1)} %get-tuple-element.56.after_ref), custom_call_target="tpu_custom_call" | custom-call | flops 4000000 | bytes 3145728 | tf_op jit(solution)/shard_map/near/pallas_call | solution.py:298
  17.6 1.7 %collective-permute-start.10 = (bf16[17,16,128]{2,1,0:T(8,128)(2,1)S(1)}, bf16[17,16,128]{2,1,0:T(8,128)(2,1)S(1)}, u32[]{:S(2)}, u32[]{:S(2)}) collective-permute-start(bf16[17,16,128]{2,1,0:T(8,128)(2,1)S(1)} %get-tuple-element.79), channel_id=1, source_target_pairs={{0,8},{1,9},{2,10},{3,11},{4,12},{5,13},{6,14},{7,15},{8,0},{9,1},... | collective-permute-start | bytes 208904 | tf_op jit(solution)/shard_map/ppermute | solution.py:333
  19.7 0.6 %collective-permute-start.3 = (bf16[16,16,128]{2,1,0:T(8,128)(2,1)S(1)}, bf16[16,16,128]{2,1,0:T(8,128)(2,1)S(1)}, u32[]{:S(2)}, u32[]{:S(2)}) collective-permute-start(bf16[16,16,128]{2,1,0:T(8,128)(2,1)S(1)} %get-tuple-element.58.after_ref), channel_id=1, source_target_pairs={{0,8},{1,9},{2,10},{3,11},{4,12},{5,13},{6,14},{7,15},{8,0},{9,1},... | collective-permute-start | bytes 196616 | tf_op jit(solution)/shard_map/ppermute | solution.py:333
  20.3 0.6 %arrange.12.refs_0_ = bf16[32,2,64,128]{3,2,1,0:T(8,128)(2,1)S(1)} custom-call(bf16[10,64,64,128]{3,2,1,0:T(8,128)(2,1)S(1)} %copy-done, bf16[16,16,128]{2,1,0:T(8,128)(2,1)S(1)} %get-tuple-element.58.after_ref), custom_call_target="tpu_custom_call" | custom-call | flops 2000000 | bytes 2097152 | tf_op jit(solution)/shard_map/arrange/pallas_call | solution.py:251
  21.0 1.1 %collective-permute-done.10.refs_2_ = bf16[17,16,128]{2,1,0:T(8,128)(2,1)S(1)} collective-permute-done((bf16[17,16,128]{2,1,0:T(8,128)(2,1)S(1)}, bf16[17,16,128]{2,1,0:T(8,128)(2,1)S(1)}, u32[]{:S(2)}, u32[]{:S(2)}) %collective-permute-start.10) | collective-permute-done | bytes 69664 | tf_op jit(solution)/shard_map/ppermute | solution.py:333
  22.4 3.5 %collective-permute-start.11 = (bf16[17,16,128]{2,1,0:T(8,128)(2,1)S(1)}, bf16[17,16,128]{2,1,0:T(8,128)(2,1)S(1)}, u32[]{:S(2)}, u32[]{:S(2)}) collective-permute-start(bf16[17,16,128]{2,1,0:T(8,128)(2,1)S(1)} %get-tuple-element.82), channel_id=1, source_target_pairs={{0,16},{1,17},{2,18},{3,19},{4,20},{5,21},{6,22},{7,23},{8,24},{9,... | collective-permute-start | bytes 208904 | tf_op jit(solution)/shard_map/ppermute | solution.py:333
  26.3 1.1 %collective-permute-start.4 = (bf16[16,16,128]{2,1,0:T(8,128)(2,1)S(1)}, bf16[16,16,128]{2,1,0:T(8,128)(2,1)S(1)}, u32[]{:S(2)}, u32[]{:S(2)}) collective-permute-start(bf16[16,16,128]{2,1,0:T(8,128)(2,1)S(1)} %get-tuple-element.60.after_ref), channel_id=1, source_target_pairs={{0,16},{1,17},{2,18},{3,19},{4,20},{5,21},{6,22},{7,23},{8,24},{9,... | collective-permute-start | bytes 196616 | tf_op jit(solution)/shard_map/ppermute | solution.py:333
  27.4 0.6 %arrange.13.refs_0_ = bf16[32,2,64,128]{3,2,1,0:T(8,128)(2,1)S(1)} custom-call(bf16[10,64,64,128]{3,2,1,0:T(8,128)(2,1)S(1)} %copy-done, bf16[16,16,128]{2,1,0:T(8,128)(2,1)S(1)} %get-tuple-element.60.after_ref), custom_call_target="tpu_custom_call" | custom-call | flops 2000000 | bytes 2097152 | tf_op jit(solution)/shard_map/arrange/pallas_call | solution.py:251
  28.9 2.0 %collective-permute-start.12 = (bf16[17,16,128]{2,1,0:T(8,128)(2,1)S(1)}, bf16[17,16,128]{2,1,0:T(8,128)(2,1)S(1)}, u32[]{:S(2)}, u32[]{:S(2)}) collective-permute-start(bf16[17,16,128]{2,1,0:T(8,128)(2,1)S(1)} %get-tuple-element.85), channel_id=1, source_target_pairs={{0,32},{1,33},{2,34},{3,35},{4,36},{5,37},{6,38},{7,39},{8,40},{9,... | collective-permute-start | bytes 208904 | tf_op jit(solution)/shard_map/ppermute | solution.py:333
  30.9 1.2 %collective-permute-done.4.refs_2_ = bf16[16,16,128]{2,1,0:T(8,128)(2,1)S(1)} collective-permute-done((bf16[16,16,128]{2,1,0:T(8,128)(2,1)S(1)}, bf16[16,16,128]{2,1,0:T(8,128)(2,1)S(1)}, u32[]{:S(2)}, u32[]{:S(2)}) %collective-permute-start.4) | collective-permute-done | bytes 65568 | tf_op jit(solution)/shard_map/ppermute | solution.py:333
  32.5 2.0 %collective-permute-start.5 = (bf16[16,16,128]{2,1,0:T(8,128)(2,1)S(1)}, bf16[16,16,128]{2,1,0:T(8,128)(2,1)S(1)}, u32[]{:S(2)}, u32[]{:S(2)}) collective-permute-start(bf16[16,16,128]{2,1,0:T(8,128)(2,1)S(1)} %get-tuple-element.62.after_ref), channel_id=1, source_target_pairs={{0,32},{1,33},{2,34},{3,35},{4,36},{5,37},{6,38},{7,39},{8,40},{9,... | collective-permute-start | bytes 196616 | tf_op jit(solution)/shard_map/ppermute | solution.py:333
  34.5 0.6 %arrange.14.refs_0_ = bf16[32,2,64,128]{3,2,1,0:T(8,128)(2,1)S(1)} custom-call(bf16[10,64,64,128]{3,2,1,0:T(8,128)(2,1)S(1)} %copy-done, bf16[16,16,128]{2,1,0:T(8,128)(2,1)S(1)} %get-tuple-element.62.after_ref), custom_call_target="tpu_custom_call" | custom-call | flops 2000000 | bytes 2097152 | tf_op jit(solution)/shard_map/arrange/pallas_call | solution.py:251
  35.5 3.3 %collective-permute-start.13 = (bf16[17,16,128]{2,1,0:T(8,128)(2,1)S(1)}, bf16[17,16,128]{2,1,0:T(8,128)(2,1)S(1)}, u32[]{:S(2)}, u32[]{:S(2)}) collective-permute-start(bf16[17,16,128]{2,1,0:T(8,128)(2,1)S(1)} %get-tuple-element.88), channel_id=1, source_target_pairs={{0,64},{1,65},{2,66},{3,67},{4,68},{5,69},{6,70},{7,71},{8,72},{9,... | collective-permute-start | bytes 208904 | tf_op jit(solution)/shard_map/ppermute | solution.py:333
  39.3 1.3 %collective-permute-start.6 = (bf16[16,16,128]{2,1,0:T(8,128)(2,1)S(1)}, bf16[16,16,128]{2,1,0:T(8,128)(2,1)S(1)}, u32[]{:S(2)}, u32[]{:S(2)}) collective-permute-start(bf16[16,16,128]{2,1,0:T(8,128)(2,1)S(1)} %get-tuple-element.64.after_ref), channel_id=1, source_target_pairs={{0,64},{1,65},{2,66},{3,67},{4,68},{5,69},{6,70},{7,71},{8,72},{9,... | collective-permute-start | bytes 196616 | tf_op jit(solution)/shard_map/ppermute | solution.py:333
  40.6 0.6 %arrange.15.refs_0_ = bf16[32,2,64,128]{3,2,1,0:T(8,128)(2,1)S(1)} custom-call(bf16[10,64,64,128]{3,2,1,0:T(8,128)(2,1)S(1)} %copy-done, bf16[16,16,128]{2,1,0:T(8,128)(2,1)S(1)} %get-tuple-element.64.after_ref), custom_call_target="tpu_custom_call" | custom-call | flops 2000000 | bytes 2097152 | tf_op jit(solution)/shard_map/arrange/pallas_call | solution.py:251
  41.2 0.5 collective-permute-done.13.refs_2_
  42.1 6.2 %collective-permute-start.14 = (bf16[17,16,128]{2,1,0:T(8,128)(2,1)S(1)}, bf16[17,16,128]{2,1,0:T(8,128)(2,1)S(1)}, u32[]{:S(2)}, u32[]{:S(2)}) collective-permute-start(bf16[17,16,128]{2,1,0:T(8,128)(2,1)S(1)} %get-tuple-element.91), channel_id=1, source_target_pairs={{0,128},{1,129},{2,130},{3,131},{4,132},{5,133},{6,134},{7,135},{8... | collective-permute-start | bytes 208904 | tf_op jit(solution)/shard_map/ppermute | solution.py:333
  48.7 4.8 %collective-permute-start.15 = (bf16[16,16,128]{2,1,0:T(8,128)(2,1)S(1)}, bf16[16,16,128]{2,1,0:T(8,128)(2,1)S(1)}, u32[]{:S(2)}, u32[]{:S(2)}) collective-permute-start(bf16[16,16,128]{2,1,0:T(8,128)(2,1)S(1)} %get-tuple-element.66.after_ref), channel_id=1, source_target_pairs={{0,128},{1,129},{2,130},{3,131},{4,132},{5,133},{6,134},{7,135},{8... | collective-permute-start | bytes 196616 | tf_op jit(solution)/shard_map/ppermute | solution.py:333
  53.5 0.6 %arrange.17.refs_0_ = bf16[32,2,64,128]{3,2,1,0:T(8,128)(2,1)S(1)} custom-call(bf16[10,64,64,128]{3,2,1,0:T(8,128)(2,1)S(1)} %copy-done, bf16[16,16,128]{2,1,0:T(8,128)(2,1)S(1)} %get-tuple-element.66.after_ref), custom_call_target="tpu_custom_call" | custom-call | flops 2000000 | bytes 2097152 | tf_op jit(solution)/shard_map/arrange/pallas_call | solution.py:251
  54.1 0.6 %arrange.16.refs_4_.refs_0_ = bf16[32,2,64,128]{3,2,1,0:T(8,128)(2,1)S(1)} custom-call(bf16[10,64,64,128]{3,2,1,0:T(8,128)(2,1)S(1)} %copy-done, bf16[16,16,128]{2,1,0:T(8,128)(2,1)S(1)} %get-tuple-element.66.after_ref), custom_call_target="tpu_custom_call" | custom-call | flops 2000000 | bytes 2097152 | tf_op jit(solution)/shard_map/arrange/pallas_call | solution.py:251
  54.8 2.2 %collective-permute-done.15.refs_2_ = bf16[16,16,128]{2,1,0:T(8,128)(2,1)S(1)} collective-permute-done((bf16[16,16,128]{2,1,0:T(8,128)(2,1)S(1)}, bf16[16,16,128]{2,1,0:T(8,128)(2,1)S(1)}, u32[]{:S(2)}, u32[]{:S(2)}) %collective-permute-start.15) | collective-permute-done | bytes 65568 | tf_op jit(solution)/shard_map/ppermute | solution.py:333
  57.7 1.8 %root.1 = bf16[16,32,256]{2,1,0:T(8,128)(2,1)} custom-call(bf16[32,2,64,128]{3,2,1,0:T(8,128)(2,1)S(1)} %arrange.16.refs_4_.refs_0_, f32[2,32,16,128]{3,2,1,0:T(8,128)S(1)} %get-tuple-element.68.refs_4_.refs_1_, bf16[2,32,128]{2,1,0:T(8,128)(2,1)S(1)} %get-tuple-element.69.refs_2_, bf16[16,128]{1,0:T(8,128)(2,1)S(1)} %get-tuple-element.93.refs_3_, ...), custom_call_target="tpu_custom_call" | custom-call | tf_op jit(solution)/shard_map/root/pallas_call | solution.py:314
  (33 shorter events, 7.2 us)
Async XLA Ops:
  0.0 4.4 %copy-start = (bf16[10,64,64,128]{3,2,1,0:T(8,128)(2,1)S(1)}, bf16[10,64,64,128]{3,2,1,0:T(8,128)(2,1)}, u32[]{:S(2)}) copy-start(bf16[10,64,64,128]{3,2,1,0:T(8,128)(2,1)} %weights_ref.17) | copy-start | bytes 31457284
  2.9 2.2 %collective-permute-start.7 = (bf16[17,16,128]{2,1,0:T(8,128)(2,1)S(1)}, bf16[17,16,128]{2,1,0:T(8,128)(2,1)S(1)}, u32[]{:S(2)}, u32[]{:S(2)}) collective-permute-start(bf16[17,16,128]{2,1,0:T(8,128)(2,1)S(1)} %get-tuple-element.71), channel_id=1, source_target_pairs={{0,1},{1,0},{2,3},{3,2},{4,5},{5,4},{6,7},{7,6},{8,9},{9,8},{10,11... | collective-permute-start | bytes 208904 | tf_op jit(solution)/shard_map/ppermute | solution.py:333
  3.0 3.4 %collective-permute-start = (bf16[16,16,128]{2,1,0:T(8,128)(2,1)S(1)}, bf16[16,16,128]{2,1,0:T(8,128)(2,1)S(1)}, u32[]{:S(2)}, u32[]{:S(2)}) collective-permute-start(bf16[16,16,128]{2,1,0:T(8,128)(2,1)S(1)} %get-tuple-element.52.after_ref), channel_id=1, source_target_pairs={{0,1},{1,0},{2,3},{3,2},{4,5},{5,4},{6,7},{7,6},{8,9},{9,8},{10,11... | collective-permute-start | bytes 196616 | tf_op jit(solution)/shard_map/ppermute | solution.py:333
  5.5 5.0 %collective-permute-start.8 = (bf16[17,16,128]{2,1,0:T(8,128)(2,1)S(1)}, bf16[17,16,128]{2,1,0:T(8,128)(2,1)S(1)}, u32[]{:S(2)}, u32[]{:S(2)}) collective-permute-start(bf16[17,16,128]{2,1,0:T(8,128)(2,1)S(1)} %get-tuple-element.73), channel_id=1, source_target_pairs={{0,2},{1,3},{2,0},{3,1},{4,6},{5,7},{6,4},{7,5},{8,10},{9,11},{10,... | collective-permute-start | bytes 208904 | tf_op jit(solution)/shard_map/ppermute | solution.py:333
  6.8 8.8 %copy-start.1 = (bf16[3,32,32,256]{3,2,1,0:T(8,128)(2,1)S(1)}, bf16[3,32,32,256]{3,2,1,0:T(8,128)(2,1)}, u32[]{:S(2)}) copy-start(bf16[3,32,32,256]{3,2,1,0:T(8,128)(2,1)} %blocks_ref.1) | copy-start | bytes 4718596
  6.8 5.4 %collective-permute-start.1 = (bf16[16,16,128]{2,1,0:T(8,128)(2,1)S(1)}, bf16[16,16,128]{2,1,0:T(8,128)(2,1)S(1)}, u32[]{:S(2)}, u32[]{:S(2)}) collective-permute-start(bf16[16,16,128]{2,1,0:T(8,128)(2,1)S(1)} %get-tuple-element.54.after_ref), channel_id=1, source_target_pairs={{0,2},{1,3},{2,0},{3,1},{4,6},{5,7},{6,4},{7,5},{8,10},{9,11},{10,... | collective-permute-start | bytes 196616 | tf_op jit(solution)/shard_map/ppermute | solution.py:333
  10.8 6.4 %collective-permute-start.9 = (bf16[17,16,128]{2,1,0:T(8,128)(2,1)S(1)}, bf16[17,16,128]{2,1,0:T(8,128)(2,1)S(1)}, u32[]{:S(2)}, u32[]{:S(2)}) collective-permute-start(bf16[17,16,128]{2,1,0:T(8,128)(2,1)S(1)} %get-tuple-element.76), channel_id=1, source_target_pairs={{0,4},{1,5},{2,6},{3,7},{4,0},{5,1},{6,2},{7,3},{8,12},{9,13},{10,... | collective-permute-start | bytes 208904 | tf_op jit(solution)/shard_map/ppermute | solution.py:333
  12.6 6.7 %collective-permute-start.2 = (bf16[16,16,128]{2,1,0:T(8,128)(2,1)S(1)}, bf16[16,16,128]{2,1,0:T(8,128)(2,1)S(1)}, u32[]{:S(2)}, u32[]{:S(2)}) collective-permute-start(bf16[16,16,128]{2,1,0:T(8,128)(2,1)S(1)} %get-tuple-element.56.after_ref), channel_id=1, source_target_pairs={{0,4},{1,5},{2,6},{3,7},{4,0},{5,1},{6,2},{7,3},{8,12},{9,13},{10,... | collective-permute-start | bytes 196616 | tf_op jit(solution)/shard_map/ppermute | solution.py:333
  17.6 4.4 %collective-permute-start.10 = (bf16[17,16,128]{2,1,0:T(8,128)(2,1)S(1)}, bf16[17,16,128]{2,1,0:T(8,128)(2,1)S(1)}, u32[]{:S(2)}, u32[]{:S(2)}) collective-permute-start(bf16[17,16,128]{2,1,0:T(8,128)(2,1)S(1)} %get-tuple-element.79), channel_id=1, source_target_pairs={{0,8},{1,9},{2,10},{3,11},{4,12},{5,13},{6,14},{7,15},{8,0},{9,1},... | collective-permute-start | bytes 208904 | tf_op jit(solution)/shard_map/ppermute | solution.py:333
  19.7 6.2 %collective-permute-start.3 = (bf16[16,16,128]{2,1,0:T(8,128)(2,1)S(1)}, bf16[16,16,128]{2,1,0:T(8,128)(2,1)S(1)}, u32[]{:S(2)}, u32[]{:S(2)}) collective-permute-start(bf16[16,16,128]{2,1,0:T(8,128)(2,1)S(1)} %get-tuple-element.58.after_ref), channel_id=1, source_target_pairs={{0,8},{1,9},{2,10},{3,11},{4,12},{5,13},{6,14},{7,15},{8,0},{9,1},... | collective-permute-start | bytes 196616 | tf_op jit(solution)/shard_map/ppermute | solution.py:333
  22.4 6.1 %collective-permute-start.11 = (bf16[17,16,128]{2,1,0:T(8,128)(2,1)S(1)}, bf16[17,16,128]{2,1,0:T(8,128)(2,1)S(1)}, u32[]{:S(2)}, u32[]{:S(2)}) collective-permute-start(bf16[17,16,128]{2,1,0:T(8,128)(2,1)S(1)} %get-tuple-element.82), channel_id=1, source_target_pairs={{0,16},{1,17},{2,18},{3,19},{4,20},{5,21},{6,22},{7,23},{8,24},{9,... | collective-permute-start | bytes 208904 | tf_op jit(solution)/shard_map/ppermute | solution.py:333
  26.3 5.8 %collective-permute-start.4 = (bf16[16,16,128]{2,1,0:T(8,128)(2,1)S(1)}, bf16[16,16,128]{2,1,0:T(8,128)(2,1)S(1)}, u32[]{:S(2)}, u32[]{:S(2)}) collective-permute-start(bf16[16,16,128]{2,1,0:T(8,128)(2,1)S(1)} %get-tuple-element.60.after_ref), channel_id=1, source_target_pairs={{0,16},{1,17},{2,18},{3,19},{4,20},{5,21},{6,22},{7,23},{8,24},{9,... | collective-permute-start | bytes 196616 | tf_op jit(solution)/shard_map/ppermute | solution.py:333
  28.9 6.3 %collective-permute-start.12 = (bf16[17,16,128]{2,1,0:T(8,128)(2,1)S(1)}, bf16[17,16,128]{2,1,0:T(8,128)(2,1)S(1)}, u32[]{:S(2)}, u32[]{:S(2)}) collective-permute-start(bf16[17,16,128]{2,1,0:T(8,128)(2,1)S(1)} %get-tuple-element.85), channel_id=1, source_target_pairs={{0,32},{1,33},{2,34},{3,35},{4,36},{5,37},{6,38},{7,39},{8,40},{9,... | collective-permute-start | bytes 208904 | tf_op jit(solution)/shard_map/ppermute | solution.py:333
  32.5 6.4 %collective-permute-start.5 = (bf16[16,16,128]{2,1,0:T(8,128)(2,1)S(1)}, bf16[16,16,128]{2,1,0:T(8,128)(2,1)S(1)}, u32[]{:S(2)}, u32[]{:S(2)}) collective-permute-start(bf16[16,16,128]{2,1,0:T(8,128)(2,1)S(1)} %get-tuple-element.62.after_ref), channel_id=1, source_target_pairs={{0,32},{1,33},{2,34},{3,35},{4,36},{5,37},{6,38},{7,39},{8,40},{9,... | collective-permute-start | bytes 196616 | tf_op jit(solution)/shard_map/ppermute | solution.py:333
  35.5 6.2 %collective-permute-start.13 = (bf16[17,16,128]{2,1,0:T(8,128)(2,1)S(1)}, bf16[17,16,128]{2,1,0:T(8,128)(2,1)S(1)}, u32[]{:S(2)}, u32[]{:S(2)}) collective-permute-start(bf16[17,16,128]{2,1,0:T(8,128)(2,1)S(1)} %get-tuple-element.88), channel_id=1, source_target_pairs={{0,64},{1,65},{2,66},{3,67},{4,68},{5,69},{6,70},{7,71},{8,72},{9,... | collective-permute-start | bytes 208904 | tf_op jit(solution)/shard_map/ppermute | solution.py:333
  39.3 9.1 %collective-permute-start.6 = (bf16[16,16,128]{2,1,0:T(8,128)(2,1)S(1)}, bf16[16,16,128]{2,1,0:T(8,128)(2,1)S(1)}, u32[]{:S(2)}, u32[]{:S(2)}) collective-permute-start(bf16[16,16,128]{2,1,0:T(8,128)(2,1)S(1)} %get-tuple-element.64.after_ref), channel_id=1, source_target_pairs={{0,64},{1,65},{2,66},{3,67},{4,68},{5,69},{6,70},{7,71},{8,72},{9,... | collective-permute-start | bytes 196616 | tf_op jit(solution)/shard_map/ppermute | solution.py:333
  42.1 15.2 %collective-permute-start.14 = (bf16[17,16,128]{2,1,0:T(8,128)(2,1)S(1)}, bf16[17,16,128]{2,1,0:T(8,128)(2,1)S(1)}, u32[]{:S(2)}, u32[]{:S(2)}) collective-permute-start(bf16[17,16,128]{2,1,0:T(8,128)(2,1)S(1)} %get-tuple-element.91), channel_id=1, source_target_pairs={{0,128},{1,129},{2,130},{3,131},{4,132},{5,133},{6,134},{7,135},{8... | collective-permute-start | bytes 208904 | tf_op jit(solution)/shard_map/ppermute | solution.py:333
  48.7 8.3 %collective-permute-start.15 = (bf16[16,16,128]{2,1,0:T(8,128)(2,1)S(1)}, bf16[16,16,128]{2,1,0:T(8,128)(2,1)S(1)}, u32[]{:S(2)}, u32[]{:S(2)}) collective-permute-start(bf16[16,16,128]{2,1,0:T(8,128)(2,1)S(1)} %get-tuple-element.66.after_ref), channel_id=1, source_target_pairs={{0,128},{1,129},{2,130},{3,131},{4,132},{5,133},{6,134},{7,135},{8... | collective-permute-start | bytes 196616 | tf_op jit(solution)/shard_map/ppermute | solution.py:333

commit v2 on v1

v2 whole, which is shorter than its diff:
```python
import functools

import jax
import jax.numpy as jnp
from jax import lax
from jax.experimental import pallas as pl
from jax.experimental.pallas import tpu as pltpu
from jax.sharding import PartitionSpec as P

RHS = 16
RANK = 32
HALF = 128
QUADS = 32
LANES = 128
PITCH = LANES + 1
CHAINS = 2
SLOTS = QUADS // CHAINS
BF16 = jnp.bfloat16
F32 = jnp.float32


def lane_bit(shape, step, dtype=jnp.int32):
    return (lax.broadcasted_iota(dtype, shape, len(shape) - 1) & step) != 0


def swap_lane_groups(blocks):
    blocks = list(blocks)
    for step in (2, 1):
        lanes = step * QUADS
        upper = lane_bit(blocks[0].shape, lanes)
        for low in range(4):
            if low & step:
                continue
            high = low + step
            first, second = blocks[low], blocks[high]
            blocks[low] = jnp.where(upper, pltpu.roll(second, lanes, 1), first)
            blocks[high] = jnp.where(upper, second, pltpu.roll(first, LANES - lanes, 1))
    return blocks


def arrange_section(weights_ref, arranged_ref, turned_ref):
    for a in range(RANK):
        both = jnp.concatenate([weights_ref[a], weights_ref[RANK + a]], axis=0)
        turned_ref[a * PITCH : a * PITCH + LANES, :] = both.T.astype(F32)
    for q in range(QUADS):
        rows = [turned_ref[pl.ds(part * QUADS + q, RANK, stride=PITCH), :] for part in range(4)]
        turned = jnp.concatenate(rows, axis=0).astype(BF16).T
        arranged_ref[q] = turned.reshape(2, 2 * RANK, LANES)


def diagonal_blocks(block, group):
    lane = lax.broadcasted_iota(jnp.int32, block.shape, 1)
    return jnp.where((lane >> 5) & 3 == group, block, jnp.zeros_like(block))


def section_quad(arranged_ref, q, lower, higher):
    tiles = []
    for half in range(2):
        rows = slice(half * RANK, (half + 1) * RANK)
        dense = jnp.concatenate([arranged_ref[q, 0, rows, :], arranged_ref[q, 1, rows, :]], axis=1)
        tiles += [diagonal_blocks(dense, group) for group in range(4)]
    matrix = jnp.concatenate(tiles, axis=0)
    stack = jnp.concatenate([lower, higher], axis=1)
    return jnp.dot(stack, matrix, preferred_element_type=F32)


def emit_halves(mixed, q, upper, own_ref, send_ref):
    first, second = mixed[:, :LANES], mixed[:, LANES:]
    own_ref[q] = jnp.where(upper, second, first)
    send_ref[q] = jnp.where(upper, first, second)


def level_bit(level):
    return (lax.axis_index("rows") >> level) & 1 == 1


def edge_lanes(part):
    return lax.broadcasted_iota(jnp.int32, (RHS, LANES), 1) >> 5 == part


def head_kernel(vectors_hbm, weights_hbm, *refs):
    outputs, scratch = refs[: 2 * CHAINS + 2], refs[2 * CHAINS + 2 :]
    halves_ref, next_ref = outputs[2 * CHAINS :]
    vectors_ref, weights_ref, rows_ref, turned_ref, arranged_ref, sems = scratch
    copies = [
        pltpu.make_async_copy(vectors_hbm, vectors_ref, sems.at[0]),
        pltpu.make_async_copy(weights_hbm.at[0], weights_ref, sems.at[1]),
        pltpu.make_async_copy(weights_hbm.at[1], next_ref, sems.at[2]),
    ]
    for copy in copies:
        copy.start()
    copies[0].wait()
    for half in range(2):
        lanes = slice(half * HALF, (half + 1) * HALF)
        for e in range(4):
            parts = [
                swap_lane_groups([vectors_ref[4 * d + e, rows : rows + 16, lanes] for d in range(4)])
                for rows in (0, 16)
            ]
            tall = jnp.concatenate([parts[upper][g4] for g4 in range(4) for upper in range(2)], axis=0)
            turned = tall.T.astype(F32)
            for d in range(4):
                start = (4 * d + e) * (QUADS + 1)
                rows_ref[half, start : start + QUADS, :] = turned[d * QUADS : (d + 1) * QUADS, :]
        for q in range(QUADS):
            halves_ref[half, q] = rows_ref[half, pl.ds(q, RHS, stride=QUADS + 1), :].astype(BF16)
    copies[1].wait()
    arrange_section(weights_ref, arranged_ref, turned_ref)
    upper = level_bit(0)
    for chain in range(CHAINS):
        own_ref, send_ref = outputs[2 * chain : 2 * chain + 2]
        for slot in range(SLOTS):
            q = chain * SLOTS + slot
            mixed = section_quad(arranged_ref, q, halves_ref[0, q], halves_ref[1, q]).astype(BF16)
            emit_halves(mixed, slot, upper, own_ref, send_ref)
        if chain == 0:
            edge = jnp.where(edge_lanes(0), halves_ref[0, 0], halves_ref[1, QUADS - 1])
            own_ref[SLOTS] = edge
            send_ref[SLOTS] = edge
    copies[2].wait()


def arrange_kernel(index, weights_ref, after_ref, arranged_ref, turned_ref):
    del after_ref
    arrange_section(weights_ref if index is None else weights_ref.at[index], arranged_ref, turned_ref)


def mix_quad(arranged_ref, q, upper, kept, received):
    lower = jnp.where(upper, received, kept)
    higher = jnp.where(upper, kept, received)
    return section_quad(arranged_ref, q, lower, higher).astype(BF16)


def meet_border(level, upper, kept, received, beside):
    inner = lax.axis_index("rows") & (2**level - 1)
    above = jnp.logical_and(jnp.logical_not(upper), inner == 2**level - 1)
    below = jnp.logical_and(upper, inner == 0)
    beside = jnp.where(jnp.logical_and(edge_lanes(0), above), received, beside)
    return jnp.where(jnp.logical_and(edge_lanes(3), below), received, beside)


def level_kernel(level, chain, merge, *refs):
    arranged_ref, kept_ref, received_ref = refs[:3]
    outputs = refs[len(refs) - (3 if chain == 0 else 2) :]
    own_ref, send_ref = outputs[:2]
    upper, next_upper = level_bit(level), level_bit(level + 1)
    for slot in range(SLOTS):
        q = chain * SLOTS + slot
        mixed = mix_quad(arranged_ref, q, upper, kept_ref[slot], received_ref[slot])
        emit_halves(mixed, q if merge else slot, next_upper, own_ref, send_ref)
    if chain == 0:
        kept, received = kept_ref[SLOTS], received_ref[SLOTS]
        outputs[2][...] = meet_border(level, upper, kept, received, refs[3][...])
        theirs = jnp.logical_xor(edge_lanes(0), jnp.logical_not(upper))
        edge = jnp.where(theirs, received, kept)
        place = QUADS if merge else SLOTS
        own_ref[place] = edge
        send_ref[place] = edge


def near_kernel(halves_ref, blocks_ref, after_ref, near_ref, border_ref, arranged_ref, turned_ref):
    del after_ref
    first_group, last_group = edge_lanes(0), edge_lanes(3)
    zeros = jnp.zeros((RHS, LANES), BF16)
    for half in range(2):
        lanes = slice(half * HALF, (half + 1) * HALF)
        for a in range(RANK):
            shifts = [blocks_ref[shift, a, :, lanes] for shift in (0, 1, 2, 0)]
            turned = jnp.concatenate(shifts, axis=0).T.astype(F32)
            turned_ref[a * PITCH : a * PITCH + LANES, :] = turned
        for q in range(QUADS):
            rows = [turned_ref[pl.ds(part * QUADS + q, RANK, stride=PITCH), :] for part in range(4)]
            arranged_ref[q] = jnp.concatenate(rows, axis=0).astype(BF16).T
        if half == 0:
            border_ref[0] = arranged_ref[0, RANK : 2 * RANK, :]
        else:
            border_ref[1] = arranged_ref[QUADS - 1, 2 * RANK : 3 * RANK, :]
        edge_before = zeros if half == 0 else halves_ref[0, QUADS - 1]
        edge_after = zeros if half == 1 else halves_ref[1, 0]
        for q in range(QUADS):
            centre = halves_ref[half, q]
            if q > 0:
                before = halves_ref[half, q - 1]
            else:
                final = halves_ref[half, QUADS - 1]
                before = pltpu.roll(jnp.where(last_group, edge_before, final), RANK, 1)
            if q < QUADS - 1:
                after = halves_ref[half, q + 1]
            else:
                first = halves_ref[half, 0]
                after = pltpu.roll(jnp.where(first_group, edge_after, first), LANES - RANK, 1)
            tiles = [
                diagonal_blocks(arranged_ref[q, shift * RANK : (shift + 1) * RANK, :], part)
                for shift in range(3)
                for part in range(4)
            ]
            matrix = jnp.concatenate(tiles, axis=0)
            stack = jnp.concatenate([centre, before, after], axis=1)
            near_ref[half, q] = jnp.dot(stack, matrix, preferred_element_type=F32)


def border_term(border_ref, beside, half):
    zeros = jnp.zeros((RHS, LANES), BF16)
    if half == 0:
        edge = pltpu.roll(jnp.where(edge_lanes(3), beside, zeros), RANK, 1)
    else:
        edge = pltpu.roll(jnp.where(edge_lanes(0), beside, zeros), LANES - RANK, 1)
    tiles = [diagonal_blocks(border_ref[half], part) for part in range(4)]
    return jnp.dot(edge, jnp.concatenate(tiles, axis=0), preferred_element_type=F32)


def tail_kernel(
    level, last_ref, root_ref, kept_ref, received_ref, beside_ref, near_ref, border_ref, product_ref, rows_ref
):
    upper = level_bit(level)
    beside = meet_border(level, upper, kept_ref[QUADS], received_ref[QUADS], beside_ref[...])
    for q in range(QUADS):
        mixed = mix_quad(last_ref, q, upper, kept_ref[q], received_ref[q])
        mixed = section_quad(root_ref, q, mixed[:, :LANES], mixed[:, LANES:])
        for half in range(2):
            total = mixed[:, half * LANES : (half + 1) * LANES] + near_ref[half, q]
            if q == half * (QUADS - 1):
                total = total + border_term(border_ref, beside, half)
            rows_ref[half, q * (RHS + 1) : q * (RHS + 1) + RHS, :] = total
    for half in range(2):
        lanes = slice(half * HALF, (half + 1) * HALF)
        for e in range(4):
            rows = [rows_ref[half, pl.ds(4 * d + e, QUADS, stride=RHS + 1), :] for d in range(4)]
            turned = jnp.concatenate(rows, axis=0).astype(BF16).T
            for row in (0, 16):
                blocks = [turned[g4 * RANK + row : g4 * RANK + row + 16, :] for g4 in range(4)]
                for d, block in enumerate(swap_lane_groups(blocks)):
                    product_ref[4 * d + e, row : row + 16, lanes] = block


VMEM_SPEC = pl.BlockSpec(memory_space=pltpu.VMEM)
ANY_SPEC = pl.BlockSpec(memory_space=pl.ANY)
HBM_SPEC = pl.BlockSpec(memory_space=pltpu.HBM)
TURNED = pltpu.VMEM((RANK * PITCH, LANES), F32)
ARRANGED = (QUADS, 2, 2 * RANK, LANES)
EDGE = jax.ShapeDtypeStruct((RHS, LANES), BF16)


def payload(chain, merge=False):
    slots = QUADS + 1 if merge else SLOTS + (chain == 0)
    return jax.ShapeDtypeStruct((slots, RHS, LANES), BF16)


def params(mib):
    return pltpu.CompilerParams(vmem_limit_bytes=mib * 2**20)


def in_hbm(array):
    return pltpu.with_memory_space_constraint(array, pltpu.HBM)


def arrange(factors, index, after):
    return pl.pallas_call(
        functools.partial(arrange_kernel, index),
        out_shape=jax.ShapeDtypeStruct(ARRANGED, BF16),
        in_specs=[VMEM_SPEC, ANY_SPEC],
        out_specs=VMEM_SPEC,
        scratch_shapes=[TURNED],
        compiler_params=params(16),
        cost_estimate=pl.CostEstimate(flops=2 * 10**6, bytes_accessed=2 * 2**20, transcendentals=0),
        name="arrange",
    )(factors, after)


def head(vectors, factors):
    section = (2 * RANK, 2 * RANK, HALF)
    outs = [payload(chain) for chain in range(CHAINS) for _ in range(2)]
    outs += [jax.ShapeDtypeStruct((2, QUADS, RHS, LANES), BF16), jax.ShapeDtypeStruct(section, BF16)]
    *pairs, halves, section_1 = pl.pallas_call(
        head_kernel,
        out_shape=tuple(outs),
        in_specs=[HBM_SPEC, HBM_SPEC],
        out_specs=(VMEM_SPEC,) * len(outs),
        scratch_shapes=[
            pltpu.VMEM((RHS, RANK, 2 * HALF), BF16),
            pltpu.VMEM(section, BF16),
            pltpu.VMEM((2, RHS * (QUADS + 1), LANES), F32),
            TURNED,
            pltpu.VMEM(ARRANGED, BF16),
            pltpu.SemaphoreType.DMA((3,)),
        ],
        compiler_params=params(14),
        name="head",
    )(in_hbm(vectors), in_hbm(factors))
    return pairs[::2], pairs[1::2], halves, section_1


def level_step(level, chain, arranged, kept, received, beside, into=None):
    merge = into is not None
    edges = [beside] if chain == 0 else []
    filled = list(into) if merge and chain > 0 else []
    outs = [payload(chain, merge)] * 2 + [EDGE] * len(edges)
    return pl.pallas_call(
        functools.partial(level_kernel, level, chain, merge),
        out_shape=tuple(outs),
        in_specs=[VMEM_SPEC] * (3 + len(edges) + len(filled)),
        out_specs=(VMEM_SPEC,) * len(outs),
        input_output_aliases={3: 0, 4: 1} if filled else {},
        compiler_params=params(6),
        name="level",
    )(arranged, kept, received, *edges, *filled)


def near_field(halves, neighbor_blocks, after):
    return pl.pallas_call(
        near_kernel,
        out_shape=(
            jax.ShapeDtypeStruct((2, QUADS, RHS, LANES), F32),
            jax.ShapeDtypeStruct((2, RANK, LANES), BF16),
        ),
        in_specs=[VMEM_SPEC, VMEM_SPEC, ANY_SPEC],
        out_specs=(VMEM_SPEC, VMEM_SPEC),
        scratch_shapes=[pltpu.VMEM((QUADS, LANES, LANES), BF16), TURNED],
        compiler_params=params(12),
        cost_estimate=pl.CostEstimate(flops=4 * 10**6, bytes_accessed=3 * 2**20, transcendentals=0),
        name="near",
    )(halves, neighbor_blocks, after)


def tail(level, *operands):
    return pl.pallas_call(
        functools.partial(tail_kernel, level),
        out_shape=jax.ShapeDtypeStruct((RHS, RANK, 2 * HALF), BF16),
        in_specs=[VMEM_SPEC] * len(operands),
        out_specs=VMEM_SPEC,
        scratch_shapes=[pltpu.VMEM((2, QUADS * (RHS + 1), LANES), F32)],
        compiler_params=params(12),
        name="tail",
    )(*operands)


def shards(vectors, factors, neighbor_blocks):
    level_count = factors.shape[0] - 2
    count = lax.axis_size("rows")
    kept, sending, halves, section_1 = head(vectors, factors)
    sending[0], factors = lax.optimization_barrier((sending[0], factors))
    beside = jnp.zeros(EDGE.shape, EDGE.dtype)
    for level in range(level_count - 1):
        partners = [(i, i ^ (1 << level)) for i in range(count)]
        received = [lax.ppermute(part, "rows", partners) for part in sending]
        if level == 0:
            arranged = arrange(section_1, None, sending[-1])
        else:
            arranged = arrange(factors, level + 1, sending[-1])
        into = () if level == level_count - 2 else None
        for chain in range(CHAINS):
            outs = level_step(level, chain, arranged, kept[chain], received[chain], beside, into)
            kept[chain], sending[chain] = outs[:2]
            if chain == 0:
                beside = outs[2]
            if into is not None:
                into = outs[:2]
    level = level_count - 1
    kept, sending = into
    received = lax.ppermute(sending, "rows", [(i, i ^ (1 << level)) for i in range(count)])
    near, border = near_field(halves, neighbor_blocks, sending)
    last = arrange(factors, level + 1, sending)
    root = arrange(factors, level + 2, sending)
    return tail(level, last, root, kept, received, beside, near, border)


def solution(mesh):
    placed = (P(None, None, "rows"), P(None, None, None, "rows"), P(None, None, None, "rows"))
    return jax.shard_map(
        shards, mesh=mesh, in_specs=placed, out_specs=P(None, None, "rows"), check_vma=False
    )
```

time: 60.7 us -> 58.6 us (0.965)
  starting transfers between devices: 33 us -> 30.3 us
  waiting for transfers between devices: 7.24 us -> 9.19 us
  local copies, waits for them, and re-layouts: 0.93 us -> 0.01 us
    ppermute x16 -> x14, starting transfers between devices: 33 us -> 22.5 us  [shards(): received = [lax.ppermute(part, 'rows', partners) for part in sending]]
    ppermute x0 -> x1, starting transfers between devices: none -> 7.71 us  [shards(): lax.ppermute(sending, 'rows', [(i, i ^ 1 << level) for i in range(count)])]
    ppermute x16 -> x14, waiting for transfers between devices: 7.24 us -> 9.17 us  [shards(): received = [lax.ppermute(part, 'rows', partners) for part in sending]]
    unnamed x4, local copies, waits for them, and re-layouts: 0.93 us -> 0.01 us
    pallas_call x18 -> x16, Pallas kernels: 10.9 us -> 10.7 us  [the longest x14 5.4 us: level_step(): pl.pallas_call(functools.partial(level_kernel, level, chain, merge), out_...]
  transfers between devices with their start and end apart: 16 -> 15, of which waited for: 6 -> 8; matrix products, arithmetic and copies ran while one was open for 0% -> 0% of each run, Pallas kernels for 22% -> 22%
where the time goes in v2:
time: 58.6 us; the launch traced here: 57.7 us
  starting transfers between devices  30.3 us (52%)
  Pallas kernels  18.1 us (31%)
  waiting for transfers between devices  9.19 us (16%)
    ppermute x14, starting transfers between devices, shards(): received = [lax.ppermute(part, 'rows', partners) for part in sending]  22.5 us
    ppermute x14, waiting for transfers between devices, shards(): received = [lax.ppermute(part, 'rows', partners) for part in sending]  9.17 us
    ppermute x1, starting transfers between devices, shards(): lax.ppermute(sending, 'rows', [(i, i ^ 1 << level) for i in range(count)])  7.71 us
    pallas_call x9, Pallas kernels, arrange(): pl.pallas_call(functools.partial(arrange_kernel, index), out_shape=jax.Sh...  5.74 us
    pallas_call x14, Pallas kernels, level_step(): pl.pallas_call(functools.partial(level_kernel, level, chain, merge), out_...  5.4 us
    pallas_call x1, Pallas kernels, head(): pl.pallas_call(head_kernel, out_shape=tuple(outs), in_specs=[HBM_SPEC, HB...  2.79 us
    pallas_call x1, Pallas kernels, tail(): pl.pallas_call(functools.partial(tail_kernel, level), out_shape=jax.Shape...  2.48 us
    pallas_call x1, Pallas kernels, near_field(): pl.pallas_call(near_kernel, out_shape=(jax.ShapeDtypeStruct((2, QUADS, RH...  1.66 us
  transfers between devices with their start and end apart: 15, of which 8 were waited for; matrix products, arithmetic and copies ran while one was open for 0% of the time, Pallas kernels for 22%

profile of v2, /device:TPU:6, one launch (start us, length us, event | category | flops | bytes accessed | tf_op | source)
XLA Modules:
  0.0 57.7 jit_solution(10113153845883838877)
XLA Ops:
  0.0 2.8 %head.1 = (bf16[17,16,128]{2,1,0:T(8,128)(2,1)S(1)}, bf16[17,16,128]{2,1,0:T(8,128)(2,1)S(1)}, bf16[16,16,128]{2,1,0:T(8,128)(2,1)S(1)}, bf16[16,16,128]{2,1,0:T...) custom-call(bf16[16,32,256]{2,1,0:T(8,128)(2,1)} %vectors_hbm.1, ...), custom_call_target="tpu_custom_call" | custom-call | tf_op jit(solution)/shard_map/head/pallas_call | solution.py:274
  2.9 0.5 collective-permute-start
  3.4 0.6 %arrange.9.refs_0_ = bf16[32,2,64,128]{3,2,1,0:T(8,128)(2,1)S(1)} custom-call(bf16[64,64,128]{2,1,0:T(8,128)(2,1)S(1)} %get-tuple-element.52.weights_ref, bf16[16,16,128]{2,1,0:T(8,128)(2,1)S(1)} %get-tuple-element.53.after_ref), custom_call_target="tpu_custom_call" | custom-call | flops 2000000 | bytes 2097152 | tf_op jit(solution)/shard_map/arrange/pallas_call | solution.py:258
  4.5 0.9 %collective-permute-start.8 = (bf16[17,16,128]{2,1,0:T(8,128)(2,1)S(1)}, bf16[17,16,128]{2,1,0:T(8,128)(2,1)S(1)}, u32[]{:S(2)}, u32[]{:S(2)}) collective-permute-start(bf16[17,16,128]{2,1,0:T(8,128)(2,1)S(1)} %get-tuple-element.70), channel_id=1, source_target_pairs={{0,2},{1,3},{2,0},{3,1},{4,6},{5,7},{6,4},{7,5},{8,10},{9,11},{10,... | collective-permute-start | bytes 208904 | tf_op jit(solution)/shard_map/ppermute | solution.py:345
  5.8 1.3 %collective-permute-start.1 = (bf16[16,16,128]{2,1,0:T(8,128)(2,1)S(1)}, bf16[16,16,128]{2,1,0:T(8,128)(2,1)S(1)}, u32[]{:S(2)}, u32[]{:S(2)}) collective-permute-start(bf16[16,16,128]{2,1,0:T(8,128)(2,1)S(1)} %get-tuple-element.55.after_ref), channel_id=1, source_target_pairs={{0,2},{1,3},{2,0},{3,1},{4,6},{5,7},{6,4},{7,5},{8,10},{9,11},{10,... | collective-permute-start | bytes 196616 | tf_op jit(solution)/shard_map/ppermute | solution.py:345
  7.1 0.6 %arrange.10.refs_0_ = bf16[32,2,64,128]{3,2,1,0:T(8,128)(2,1)S(1)} custom-call(bf16[10,64,64,128]{3,2,1,0:T(8,128)(2,1)S(1)} %copy-done, bf16[16,16,128]{2,1,0:T(8,128)(2,1)S(1)} %get-tuple-element.55.after_ref), custom_call_target="tpu_custom_call" | custom-call | flops 2000000 | bytes 2097152 | tf_op jit(solution)/shard_map/arrange/pallas_call | solution.py:258
  7.8 1.7 %collective-permute-done.8.refs_2_ = bf16[17,16,128]{2,1,0:T(8,128)(2,1)S(1)} collective-permute-done((bf16[17,16,128]{2,1,0:T(8,128)(2,1)S(1)}, bf16[17,16,128]{2,1,0:T(8,128)(2,1)S(1)}, u32[]{:S(2)}, u32[]{:S(2)}) %collective-permute-start.8) | collective-permute-done | bytes 69664 | tf_op jit(solution)/shard_map/ppermute | solution.py:345
  9.8 1.4 %collective-permute-start.9 = (bf16[17,16,128]{2,1,0:T(8,128)(2,1)S(1)}, bf16[17,16,128]{2,1,0:T(8,128)(2,1)S(1)}, u32[]{:S(2)}, u32[]{:S(2)}) collective-permute-start(bf16[17,16,128]{2,1,0:T(8,128)(2,1)S(1)} %get-tuple-element.73), channel_id=1, source_target_pairs={{0,4},{1,5},{2,6},{3,7},{4,0},{5,1},{6,2},{7,3},{8,12},{9,13},{10,... | collective-permute-start | bytes 208904 | tf_op jit(solution)/shard_map/ppermute | solution.py:345
  11.6 2.3 %collective-permute-start.2 = (bf16[16,16,128]{2,1,0:T(8,128)(2,1)S(1)}, bf16[16,16,128]{2,1,0:T(8,128)(2,1)S(1)}, u32[]{:S(2)}, u32[]{:S(2)}) collective-permute-start(bf16[16,16,128]{2,1,0:T(8,128)(2,1)S(1)} %get-tuple-element.57.after_ref), channel_id=1, source_target_pairs={{0,4},{1,5},{2,6},{3,7},{4,0},{5,1},{6,2},{7,3},{8,12},{9,13},{10,... | collective-permute-start | bytes 196616 | tf_op jit(solution)/shard_map/ppermute | solution.py:345
  13.9 0.6 %arrange.11.refs_0_ = bf16[32,2,64,128]{3,2,1,0:T(8,128)(2,1)S(1)} custom-call(bf16[10,64,64,128]{3,2,1,0:T(8,128)(2,1)S(1)} %copy-done, bf16[16,16,128]{2,1,0:T(8,128)(2,1)S(1)} %get-tuple-element.57.after_ref), custom_call_target="tpu_custom_call" | custom-call | flops 2000000 | bytes 2097152 | tf_op jit(solution)/shard_map/arrange/pallas_call | solution.py:258
  14.6 1.7 %collective-permute-done.9.refs_2_ = bf16[17,16,128]{2,1,0:T(8,128)(2,1)S(1)} collective-permute-done((bf16[17,16,128]{2,1,0:T(8,128)(2,1)S(1)}, bf16[17,16,128]{2,1,0:T(8,128)(2,1)S(1)}, u32[]{:S(2)}, u32[]{:S(2)}) %collective-permute-start.9) | collective-permute-done | bytes 69664 | tf_op jit(solution)/shard_map/ppermute | solution.py:345
  16.7 1.3 %collective-permute-start.10 = (bf16[17,16,128]{2,1,0:T(8,128)(2,1)S(1)}, bf16[17,16,128]{2,1,0:T(8,128)(2,1)S(1)}, u32[]{:S(2)}, u32[]{:S(2)}) collective-permute-start(bf16[17,16,128]{2,1,0:T(8,128)(2,1)S(1)} %get-tuple-element.76), channel_id=1, source_target_pairs={{0,8},{1,9},{2,10},{3,11},{4,12},{5,13},{6,14},{7,15},{8,0},{9,1},... | collective-permute-start | bytes 208904 | tf_op jit(solution)/shard_map/ppermute | solution.py:345
  18.3 1.4 %collective-permute-start.3 = (bf16[16,16,128]{2,1,0:T(8,128)(2,1)S(1)}, bf16[16,16,128]{2,1,0:T(8,128)(2,1)S(1)}, u32[]{:S(2)}, u32[]{:S(2)}) collective-permute-start(bf16[16,16,128]{2,1,0:T(8,128)(2,1)S(1)} %get-tuple-element.59.after_ref), channel_id=1, source_target_pairs={{0,8},{1,9},{2,10},{3,11},{4,12},{5,13},{6,14},{7,15},{8,0},{9,1},... | collective-permute-start | bytes 196616 | tf_op jit(solution)/shard_map/ppermute | solution.py:345
  19.7 0.6 %arrange.12.refs_0_ = bf16[32,2,64,128]{3,2,1,0:T(8,128)(2,1)S(1)} custom-call(bf16[10,64,64,128]{3,2,1,0:T(8,128)(2,1)S(1)} %copy-done, bf16[16,16,128]{2,1,0:T(8,128)(2,1)S(1)} %get-tuple-element.59.after_ref), custom_call_target="tpu_custom_call" | custom-call | flops 2000000 | bytes 2097152 | tf_op jit(solution)/shard_map/arrange/pallas_call | solution.py:258
  20.4 0.7 %collective-permute-done.10.refs_2_ = bf16[17,16,128]{2,1,0:T(8,128)(2,1)S(1)} collective-permute-done((bf16[17,16,128]{2,1,0:T(8,128)(2,1)S(1)}, bf16[17,16,128]{2,1,0:T(8,128)(2,1)S(1)}, u32[]{:S(2)}, u32[]{:S(2)}) %collective-permute-start.10) | collective-permute-done | bytes 69664 | tf_op jit(solution)/shard_map/ppermute | solution.py:345
  21.5 2.9 %collective-permute-start.11 = (bf16[17,16,128]{2,1,0:T(8,128)(2,1)S(1)}, bf16[17,16,128]{2,1,0:T(8,128)(2,1)S(1)}, u32[]{:S(2)}, u32[]{:S(2)}) collective-permute-start(bf16[17,16,128]{2,1,0:T(8,128)(2,1)S(1)} %get-tuple-element.79), channel_id=1, source_target_pairs={{0,16},{1,17},{2,18},{3,19},{4,20},{5,21},{6,22},{7,23},{8,24},{9,... | collective-permute-start | bytes 208904 | tf_op jit(solution)/shard_map/ppermute | solution.py:345
  24.7 1.8 %collective-permute-start.4 = (bf16[16,16,128]{2,1,0:T(8,128)(2,1)S(1)}, bf16[16,16,128]{2,1,0:T(8,128)(2,1)S(1)}, u32[]{:S(2)}, u32[]{:S(2)}) collective-permute-start(bf16[16,16,128]{2,1,0:T(8,128)(2,1)S(1)} %get-tuple-element.61.after_ref), channel_id=1, source_target_pairs={{0,16},{1,17},{2,18},{3,19},{4,20},{5,21},{6,22},{7,23},{8,24},{9,... | collective-permute-start | bytes 196616 | tf_op jit(solution)/shard_map/ppermute | solution.py:345
  26.5 0.6 %arrange.13.refs_0_ = bf16[32,2,64,128]{3,2,1,0:T(8,128)(2,1)S(1)} custom-call(bf16[10,64,64,128]{3,2,1,0:T(8,128)(2,1)S(1)} %copy-done, bf16[16,16,128]{2,1,0:T(8,128)(2,1)S(1)} %get-tuple-element.61.after_ref), custom_call_target="tpu_custom_call" | custom-call | flops 2000000 | bytes 2097152 | tf_op jit(solution)/shard_map/arrange/pallas_call | solution.py:258
  27.7 1.9 %collective-permute-start.12 = (bf16[17,16,128]{2,1,0:T(8,128)(2,1)S(1)}, bf16[17,16,128]{2,1,0:T(8,128)(2,1)S(1)}, u32[]{:S(2)}, u32[]{:S(2)}) collective-permute-start(bf16[17,16,128]{2,1,0:T(8,128)(2,1)S(1)} %get-tuple-element.82), channel_id=1, source_target_pairs={{0,32},{1,33},{2,34},{3,35},{4,36},{5,37},{6,38},{7,39},{8,40},{9,... | collective-permute-start | bytes 208904 | tf_op jit(solution)/shard_map/ppermute | solution.py:345
  29.6 1.2 %collective-permute-done.4.refs_2_ = bf16[16,16,128]{2,1,0:T(8,128)(2,1)S(1)} collective-permute-done((bf16[16,16,128]{2,1,0:T(8,128)(2,1)S(1)}, bf16[16,16,128]{2,1,0:T(8,128)(2,1)S(1)}, u32[]{:S(2)}, u32[]{:S(2)}) %collective-permute-start.4) | collective-permute-done | bytes 65568 | tf_op jit(solution)/shard_map/ppermute | solution.py:345
  31.1 2.2 %collective-permute-start.5 = (bf16[16,16,128]{2,1,0:T(8,128)(2,1)S(1)}, bf16[16,16,128]{2,1,0:T(8,128)(2,1)S(1)}, u32[]{:S(2)}, u32[]{:S(2)}) collective-permute-start(bf16[16,16,128]{2,1,0:T(8,128)(2,1)S(1)} %get-tuple-element.63.after_ref), channel_id=1, source_target_pairs={{0,32},{1,33},{2,34},{3,35},{4,36},{5,37},{6,38},{7,39},{8,40},{9,... | collective-permute-start | bytes 196616 | tf_op jit(solution)/shard_map/ppermute | solution.py:345
  33.3 0.6 %arrange.14.refs_0_ = bf16[32,2,64,128]{3,2,1,0:T(8,128)(2,1)S(1)} custom-call(bf16[10,64,64,128]{3,2,1,0:T(8,128)(2,1)S(1)} %copy-done, bf16[16,16,128]{2,1,0:T(8,128)(2,1)S(1)} %get-tuple-element.63.after_ref), custom_call_target="tpu_custom_call" | custom-call | flops 2000000 | bytes 2097152 | tf_op jit(solution)/shard_map/arrange/pallas_call | solution.py:258
  34.0 0.4 level.25
  34.4 3.4 %collective-permute-start.13 = (bf16[17,16,128]{2,1,0:T(8,128)(2,1)S(1)}, bf16[17,16,128]{2,1,0:T(8,128)(2,1)S(1)}, u32[]{:S(2)}, u32[]{:S(2)}) collective-permute-start(bf16[17,16,128]{2,1,0:T(8,128)(2,1)S(1)} %get-tuple-element.85), channel_id=1, source_target_pairs={{0,64},{1,65},{2,66},{3,67},{4,68},{5,69},{6,70},{7,71},{8,72},{9,... | collective-permute-start | bytes 208904 | tf_op jit(solution)/shard_map/ppermute | solution.py:345
  38.1 1.3 %collective-permute-start.6 = (bf16[16,16,128]{2,1,0:T(8,128)(2,1)S(1)}, bf16[16,16,128]{2,1,0:T(8,128)(2,1)S(1)}, u32[]{:S(2)}, u32[]{:S(2)}) collective-permute-start(bf16[16,16,128]{2,1,0:T(8,128)(2,1)S(1)} %get-tuple-element.65.after_ref), channel_id=1, source_target_pairs={{0,64},{1,65},{2,66},{3,67},{4,68},{5,69},{6,70},{7,71},{8,72},{9,... | collective-permute-start | bytes 196616 | tf_op jit(solution)/shard_map/ppermute | solution.py:345
  39.5 0.6 %arrange.15.refs_0_ = bf16[32,2,64,128]{3,2,1,0:T(8,128)(2,1)S(1)} custom-call(bf16[10,64,64,128]{3,2,1,0:T(8,128)(2,1)S(1)} %copy-done, bf16[16,16,128]{2,1,0:T(8,128)(2,1)S(1)} %get-tuple-element.65.after_ref), custom_call_target="tpu_custom_call" | custom-call | flops 2000000 | bytes 2097152 | tf_op jit(solution)/shard_map/arrange/pallas_call | solution.py:258
  40.7 3.4 %collective-permute-done.6.refs_2_ = bf16[16,16,128]{2,1,0:T(8,128)(2,1)S(1)} collective-permute-done((bf16[16,16,128]{2,1,0:T(8,128)(2,1)S(1)}, bf16[16,16,128]{2,1,0:T(8,128)(2,1)S(1)}, u32[]{:S(2)}, u32[]{:S(2)}) %collective-permute-start.6) | collective-permute-done | bytes 65568 | tf_op jit(solution)/shard_map/ppermute | solution.py:345
  44.5 7.7 %collective-permute-start.14 = (bf16[33,16,128]{2,1,0:T(8,128)(2,1)S(1)}, bf16[33,16,128]{2,1,0:T(8,128)(2,1)S(1)}, u32[]{:S(2)}, u32[]{:S(2)}) collective-permute-start(bf16[33,16,128]{2,1,0:T(8,128)(2,1)S(1)} %get-tuple-element.89.after_ref), channel_id=1, source_target_pairs={{0,128},{1,129},{2,130},{3,131},{4,132},{5,133},{6,134},{7,135},{8... | collective-permute-start | bytes 405512 | tf_op jit(solution)/shard_map/ppermute | solution.py:360
  52.2 0.6 %arrange.17.root_ref = bf16[32,2,64,128]{3,2,1,0:T(8,128)(2,1)S(1)} custom-call(bf16[10,64,64,128]{3,2,1,0:T(8,128)(2,1)S(1)} %copy-done, bf16[33,16,128]{2,1,0:T(8,128)(2,1)S(1)} %get-tuple-element.89.after_ref), custom_call_target="tpu_custom_call" | custom-call | flops 2000000 | bytes 2097152 | tf_op jit(solution)/shard_map/arrange/pallas_call | solution.py:258
  52.8 0.6 %arrange.16.last_ref = bf16[32,2,64,128]{3,2,1,0:T(8,128)(2,1)S(1)} custom-call(bf16[10,64,64,128]{3,2,1,0:T(8,128)(2,1)S(1)} %copy-done, bf16[33,16,128]{2,1,0:T(8,128)(2,1)S(1)} %get-tuple-element.89.after_ref), custom_call_target="tpu_custom_call" | custom-call | flops 2000000 | bytes 2097152 | tf_op jit(solution)/shard_map/arrange/pallas_call | solution.py:258
  53.5 1.7 %near.1 = (f32[2,32,16,128]{3,2,1,0:T(8,128)S(1)}, bf16[2,32,128]{2,1,0:T(8,128)(2,1)S(1)}) custom-call(bf16[2,32,16,128]{3,2,1,0:T(8,128)(2,1)S(1)} %get-tuple-element.92.halves_ref, bf16[3,32,32,256]{3,2,1,0:T(8,128)(2,1)S(1)} %copy-done.1, bf16[33,16,128]{2,1,0:T(8,128)(2,1)S(1)} %get-tuple-element.89.after_ref), custom_call_target="tpu_custom_call" | custom-call | flops 4000000 | bytes 3145728 | tf_op jit(solution)/shard_map/near/pallas_call | solution.py:310
  55.2 2.5 %tail.1 = bf16[16,32,256]{2,1,0:T(8,128)(2,1)} custom-call(bf16[32,2,64,128]{3,2,1,0:T(8,128)(2,1)S(1)} %arrange.16.last_ref, bf16[32,2,64,128]{3,2,1,0:T(8,128)(2,1)S(1)} %arrange.17.root_ref, bf16[33,16,128]{2,1,0:T(8,128)(2,1)S(1)} %get-tuple-element.90.kept_ref, bf16[33,16,128]{2,1,0:T(8,128)(2,1)S(1)} %collective-permute-done.14.received_ref, ...), custom_call_target="tpu_custom_call" | custom-call | tf_op jit(solution)/shard_map/tail/pallas_call | solution.py:326
  (29 shorter events, 5.6 us)
Async XLA Ops:
  0.0 7.1 %copy-start = (bf16[10,64,64,128]{3,2,1,0:T(8,128)(2,1)S(1)}, bf16[10,64,64,128]{3,2,1,0:T(8,128)(2,1)}, u32[]{:S(2)}) copy-start(bf16[10,64,64,128]{3,2,1,0:T(8,128)(2,1)} %weights_ref.7) | copy-start | bytes 31457284
  2.8 1.3 %collective-permute-start.7 = (bf16[17,16,128]{2,1,0:T(8,128)(2,1)S(1)}, bf16[17,16,128]{2,1,0:T(8,128)(2,1)S(1)}, u32[]{:S(2)}, u32[]{:S(2)}) collective-permute-start(bf16[17,16,128]{2,1,0:T(8,128)(2,1)S(1)} %get-tuple-element.68), channel_id=1, source_target_pairs={{0,1},{1,0},{2,3},{3,2},{4,5},{5,4},{6,7},{7,6},{8,9},{9,8},{10,11... | collective-permute-start | bytes 208904 | tf_op jit(solution)/shard_map/ppermute | solution.py:345
  2.9 2.5 %collective-permute-start = (bf16[16,16,128]{2,1,0:T(8,128)(2,1)S(1)}, bf16[16,16,128]{2,1,0:T(8,128)(2,1)S(1)}, u32[]{:S(2)}, u32[]{:S(2)}) collective-permute-start(bf16[16,16,128]{2,1,0:T(8,128)(2,1)S(1)} %get-tuple-element.53.after_ref), channel_id=1, source_target_pairs={{0,1},{1,0},{2,3},{3,2},{4,5},{5,4},{6,7},{7,6},{8,9},{9,8},{10,11... | collective-permute-start | bytes 196616 | tf_op jit(solution)/shard_map/ppermute | solution.py:345
  4.5 4.9 %collective-permute-start.8 = (bf16[17,16,128]{2,1,0:T(8,128)(2,1)S(1)}, bf16[17,16,128]{2,1,0:T(8,128)(2,1)S(1)}, u32[]{:S(2)}, u32[]{:S(2)}) collective-permute-start(bf16[17,16,128]{2,1,0:T(8,128)(2,1)S(1)} %get-tuple-element.70), channel_id=1, source_target_pairs={{0,2},{1,3},{2,0},{3,1},{4,6},{5,7},{6,4},{7,5},{8,10},{9,11},{10,... | collective-permute-start | bytes 208904 | tf_op jit(solution)/shard_map/ppermute | solution.py:345
  5.8 5.4 %collective-permute-start.1 = (bf16[16,16,128]{2,1,0:T(8,128)(2,1)S(1)}, bf16[16,16,128]{2,1,0:T(8,128)(2,1)S(1)}, u32[]{:S(2)}, u32[]{:S(2)}) collective-permute-start(bf16[16,16,128]{2,1,0:T(8,128)(2,1)S(1)} %get-tuple-element.55.after_ref), channel_id=1, source_target_pairs={{0,2},{1,3},{2,0},{3,1},{4,6},{5,7},{6,4},{7,5},{8,10},{9,11},{10,... | collective-permute-start | bytes 196616 | tf_op jit(solution)/shard_map/ppermute | solution.py:345
  9.8 6.4 %collective-permute-start.9 = (bf16[17,16,128]{2,1,0:T(8,128)(2,1)S(1)}, bf16[17,16,128]{2,1,0:T(8,128)(2,1)S(1)}, u32[]{:S(2)}, u32[]{:S(2)}) collective-permute-start(bf16[17,16,128]{2,1,0:T(8,128)(2,1)S(1)} %get-tuple-element.73), channel_id=1, source_target_pairs={{0,4},{1,5},{2,6},{3,7},{4,0},{5,1},{6,2},{7,3},{8,12},{9,13},{10,... | collective-permute-start | bytes 208904 | tf_op jit(solution)/shard_map/ppermute | solution.py:345
  11.6 6.3 %collective-permute-start.2 = (bf16[16,16,128]{2,1,0:T(8,128)(2,1)S(1)}, bf16[16,16,128]{2,1,0:T(8,128)(2,1)S(1)}, u32[]{:S(2)}, u32[]{:S(2)}) collective-permute-start(bf16[16,16,128]{2,1,0:T(8,128)(2,1)S(1)} %get-tuple-element.57.after_ref), channel_id=1, source_target_pairs={{0,4},{1,5},{2,6},{3,7},{4,0},{5,1},{6,2},{7,3},{8,12},{9,13},{10,... | collective-permute-start | bytes 196616 | tf_op jit(solution)/shard_map/ppermute | solution.py:345
  16.7 4.4 %collective-permute-start.10 = (bf16[17,16,128]{2,1,0:T(8,128)(2,1)S(1)}, bf16[17,16,128]{2,1,0:T(8,128)(2,1)S(1)}, u32[]{:S(2)}, u32[]{:S(2)}) collective-permute-start(bf16[17,16,128]{2,1,0:T(8,128)(2,1)S(1)} %get-tuple-element.76), channel_id=1, source_target_pairs={{0,8},{1,9},{2,10},{3,11},{4,12},{5,13},{6,14},{7,15},{8,0},{9,1},... | collective-permute-start | bytes 208904 | tf_op jit(solution)/shard_map/ppermute | solution.py:345
  18.3 6.0 %collective-permute-start.3 = (bf16[16,16,128]{2,1,0:T(8,128)(2,1)S(1)}, bf16[16,16,128]{2,1,0:T(8,128)(2,1)S(1)}, u32[]{:S(2)}, u32[]{:S(2)}) collective-permute-start(bf16[16,16,128]{2,1,0:T(8,128)(2,1)S(1)} %get-tuple-element.59.after_ref), channel_id=1, source_target_pairs={{0,8},{1,9},{2,10},{3,11},{4,12},{5,13},{6,14},{7,15},{8,0},{9,1},... | collective-permute-start | bytes 196616 | tf_op jit(solution)/shard_map/ppermute | solution.py:345
  21.5 5.9 %collective-permute-start.11 = (bf16[17,16,128]{2,1,0:T(8,128)(2,1)S(1)}, bf16[17,16,128]{2,1,0:T(8,128)(2,1)S(1)}, u32[]{:S(2)}, u32[]{:S(2)}) collective-permute-start(bf16[17,16,128]{2,1,0:T(8,128)(2,1)S(1)} %get-tuple-element.79), channel_id=1, source_target_pairs={{0,16},{1,17},{2,18},{3,19},{4,20},{5,21},{6,22},{7,23},{8,24},{9,... | collective-permute-start | bytes 208904 | tf_op jit(solution)/shard_map/ppermute | solution.py:345
  24.7 6.0 %collective-permute-start.4 = (bf16[16,16,128]{2,1,0:T(8,128)(2,1)S(1)}, bf16[16,16,128]{2,1,0:T(8,128)(2,1)S(1)}, u32[]{:S(2)}, u32[]{:S(2)}) collective-permute-start(bf16[16,16,128]{2,1,0:T(8,128)(2,1)S(1)} %get-tuple-element.61.after_ref), channel_id=1, source_target_pairs={{0,16},{1,17},{2,18},{3,19},{4,20},{5,21},{6,22},{7,23},{8,24},{9,... | collective-permute-start | bytes 196616 | tf_op jit(solution)/shard_map/ppermute | solution.py:345
  27.7 6.3 %collective-permute-start.12 = (bf16[17,16,128]{2,1,0:T(8,128)(2,1)S(1)}, bf16[17,16,128]{2,1,0:T(8,128)(2,1)S(1)}, u32[]{:S(2)}, u32[]{:S(2)}) collective-permute-start(bf16[17,16,128]{2,1,0:T(8,128)(2,1)S(1)} %get-tuple-element.82), channel_id=1, source_target_pairs={{0,32},{1,33},{2,34},{3,35},{4,36},{5,37},{6,38},{7,39},{8,40},{9,... | collective-permute-start | bytes 208904 | tf_op jit(solution)/shard_map/ppermute | solution.py:345
  31.1 6.6 %collective-permute-start.5 = (bf16[16,16,128]{2,1,0:T(8,128)(2,1)S(1)}, bf16[16,16,128]{2,1,0:T(8,128)(2,1)S(1)}, u32[]{:S(2)}, u32[]{:S(2)}) collective-permute-start(bf16[16,16,128]{2,1,0:T(8,128)(2,1)S(1)} %get-tuple-element.63.after_ref), channel_id=1, source_target_pairs={{0,32},{1,33},{2,34},{3,35},{4,36},{5,37},{6,38},{7,39},{8,40},{9,... | collective-permute-start | bytes 196616 | tf_op jit(solution)/shard_map/ppermute | solution.py:345
  34.4 5.9 %collective-permute-start.13 = (bf16[17,16,128]{2,1,0:T(8,128)(2,1)S(1)}, bf16[17,16,128]{2,1,0:T(8,128)(2,1)S(1)}, u32[]{:S(2)}, u32[]{:S(2)}) collective-permute-start(bf16[17,16,128]{2,1,0:T(8,128)(2,1)S(1)} %get-tuple-element.85), channel_id=1, source_target_pairs={{0,64},{1,65},{2,66},{3,67},{4,68},{5,69},{6,70},{7,71},{8,72},{9,... | collective-permute-start | bytes 208904 | tf_op jit(solution)/shard_map/ppermute | solution.py:345
  38.1 5.9 %collective-permute-start.6 = (bf16[16,16,128]{2,1,0:T(8,128)(2,1)S(1)}, bf16[16,16,128]{2,1,0:T(8,128)(2,1)S(1)}, u32[]{:S(2)}, u32[]{:S(2)}) collective-permute-start(bf16[16,16,128]{2,1,0:T(8,128)(2,1)S(1)} %get-tuple-element.65.after_ref), channel_id=1, source_target_pairs={{0,64},{1,65},{2,66},{3,67},{4,68},{5,69},{6,70},{7,71},{8,72},{9,... | collective-permute-start | bytes 196616 | tf_op jit(solution)/shard_map/ppermute | solution.py:345
  44.5 9.0 %copy-start.1 = (bf16[3,32,32,256]{3,2,1,0:T(8,128)(2,1)S(1)}, bf16[3,32,32,256]{3,2,1,0:T(8,128)(2,1)}, u32[]{:S(2)}) copy-start(bf16[3,32,32,256]{3,2,1,0:T(8,128)(2,1)} %blocks_ref.1) | copy-start | bytes 4718596
  44.5 10.7 %collective-permute-start.14 = (bf16[33,16,128]{2,1,0:T(8,128)(2,1)S(1)}, bf16[33,16,128]{2,1,0:T(8,128)(2,1)S(1)}, u32[]{:S(2)}, u32[]{:S(2)}) collective-permute-start(bf16[33,16,128]{2,1,0:T(8,128)(2,1)S(1)} %get-tuple-element.89.after_ref), channel_id=1, source_target_pairs={{0,128},{1,129},{2,130},{3,131},{4,132},{5,133},{6,134},{7,135},{8... | collective-permute-start | bytes 405512 | tf_op jit(solution)/shard_map/ppermute | solution.py:360

commit v3 on v2

--- a/solution.py
+++ b/solution.py
@@ -38,14 +38,21 @@
     return blocks
 
 
-def arrange_section(weights_ref, arranged_ref, turned_ref):
+def turn_section(weights_ref, turned_ref):
     for a in range(RANK):
         both = jnp.concatenate([weights_ref[a], weights_ref[RANK + a]], axis=0)
         turned_ref[a * PITCH : a * PITCH + LANES, :] = both.T.astype(F32)
+
+
+def dense_quad(turned_ref, q):
+    rows = [turned_ref[pl.ds(part * QUADS + q, RANK, stride=PITCH), :] for part in range(4)]
+    return jnp.concatenate(rows, axis=0).astype(BF16).T
+
+
+def arrange_section(weights_ref, arranged_ref, turned_ref):
+    turn_section(weights_ref, turned_ref)
     for q in range(QUADS):
-        rows = [turned_ref[pl.ds(part * QUADS + q, RANK, stride=PITCH), :] for part in range(4)]
-        turned = jnp.concatenate(rows, axis=0).astype(BF16).T
-        arranged_ref[q] = turned.reshape(2, 2 * RANK, LANES)
+        arranged_ref[q] = dense_quad(turned_ref, q).reshape(2, 2 * RANK, LANES)
 
 
 def diagonal_blocks(block, group):
@@ -64,6 +71,12 @@
     return jnp.dot(stack, matrix, preferred_element_type=F32)
 
 
+def half_dot(stack, pair):
+    dense = jnp.concatenate(pair, axis=1)
+    matrix = jnp.concatenate([diagonal_blocks(dense, group) for group in range(4)], axis=0)
+    return jnp.dot(stack, matrix, preferred_element_type=F32)
+
+
 def emit_halves(mixed, q, upper, own_ref, send_ref):
     first, second = mixed[:, :LANES], mixed[:, LANES:]
     own_ref[q] = jnp.where(upper, second, first)
@@ -83,18 +96,22 @@
     halves_ref, next_ref = outputs[2 * CHAINS :]
     vectors_ref, weights_ref, rows_ref, turned_ref, arranged_ref, sems = scratch
     copies = [
-        pltpu.make_async_copy(vectors_hbm, vectors_ref, sems.at[0]),
-        pltpu.make_async_copy(weights_hbm.at[0], weights_ref, sems.at[1]),
-        pltpu.make_async_copy(weights_hbm.at[1], next_ref, sems.at[2]),
+        pltpu.make_async_copy(
+            vectors_hbm.at[:, :, pl.ds(half * HALF, HALF)], vectors_ref.at[half], sems.at[half]
+        )
+        for half in range(2)
+    ]
+    copies += [
+        pltpu.make_async_copy(weights_hbm.at[0], weights_ref, sems.at[2]),
+        pltpu.make_async_copy(weights_hbm.at[1], next_ref, sems.at[3]),
     ]
     for copy in copies:
         copy.start()
-    copies[0].wait()
     for half in range(2):
-        lanes = slice(half * HALF, (half + 1) * HALF)
+        copies[half].wait()
         for e in range(4):
             parts = [
-                swap_lane_groups([vectors_ref[4 * d + e, rows : rows + 16, lanes] for d in range(4)])
+                swap_lane_groups([vectors_ref[half, 4 * d + e, rows : rows + 16, :] for d in range(4)])
                 for rows in (0, 16)
             ]
             tall = jnp.concatenate([parts[upper][g4] for g4 in range(4) for upper in range(2)], axis=0)
@@ -104,7 +121,7 @@
                 rows_ref[half, start : start + QUADS, :] = turned[d * QUADS : (d + 1) * QUADS, :]
         for q in range(QUADS):
             halves_ref[half, q] = rows_ref[half, pl.ds(q, RHS, stride=QUADS + 1), :].astype(BF16)
-    copies[1].wait()
+    copies[2].wait()
     arrange_section(weights_ref, arranged_ref, turned_ref)
     upper = level_bit(0)
     for chain in range(CHAINS):
@@ -117,18 +134,34 @@
             edge = jnp.where(edge_lanes(0), halves_ref[0, 0], halves_ref[1, QUADS - 1])
             own_ref[SLOTS] = edge
             send_ref[SLOTS] = edge
-    copies[2].wait()
+    copies[3].wait()
 
 
 def arrange_kernel(index, weights_ref, after_ref, arranged_ref, turned_ref):
     del after_ref
-    arrange_section(weights_ref if index is None else weights_ref.at[index], arranged_ref, turned_ref)
-
-
-def mix_quad(arranged_ref, q, upper, kept, received):
-    lower = jnp.where(upper, received, kept)
-    higher = jnp.where(upper, kept, received)
-    return section_quad(arranged_ref, q, lower, higher).astype(BF16)
+    arrange_section(weights_ref.at[index], arranged_ref, turned_ref)
+
+
+def stage_kernel(level, index, chains, *refs):
+    weights_ref, *kept_refs = refs[: 1 + chains]
+    partial_ref, arranged_ref, turned_ref = refs[len(refs) - 3 :]
+    upper = level_bit(level)
+    turn_section(weights_ref if index is None else weights_ref.at[index], turned_ref)
+    for q in range(QUADS):
+        dense = dense_quad(turned_ref, q)
+        low, high = [
+            [dense[(2 * k + half) * RANK : (2 * k + half + 1) * RANK] for k in range(2)] for half in range(2)
+        ]
+        mine = [jnp.where(upper, second, first) for first, second in zip(low, high)]
+        chain, slot = divmod(q, QUADS // chains)
+        partial_ref[q] = half_dot(kept_refs[chain][slot], mine)
+        for k in range(2):
+            arranged_ref[q, k] = jnp.where(upper, low[k], high[k])
+
+
+def arrive(partial_ref, arranged_ref, q, received):
+    mixed = half_dot(received, [arranged_ref[q, 0], arranged_ref[q, 1]])
+    return (mixed + partial_ref[q]).astype(BF16)
 
 
 def meet_border(level, upper, kept, received, beside):
@@ -140,17 +173,17 @@
 
 
 def level_kernel(level, chain, merge, *refs):
-    arranged_ref, kept_ref, received_ref = refs[:3]
+    partial_ref, arranged_ref, received_ref = refs[:3]
     outputs = refs[len(refs) - (3 if chain == 0 else 2) :]
     own_ref, send_ref = outputs[:2]
     upper, next_upper = level_bit(level), level_bit(level + 1)
     for slot in range(SLOTS):
         q = chain * SLOTS + slot
-        mixed = mix_quad(arranged_ref, q, upper, kept_ref[slot], received_ref[slot])
+        mixed = arrive(partial_ref, arranged_ref, q, received_ref[slot])
         emit_halves(mixed, q if merge else slot, next_upper, own_ref, send_ref)
     if chain == 0:
-        kept, received = kept_ref[SLOTS], received_ref[SLOTS]
-        outputs[2][...] = meet_border(level, upper, kept, received, refs[3][...])
+        kept, received = refs[3][SLOTS], received_ref[SLOTS]
+        outputs[2][...] = meet_border(level, upper, kept, received, refs[4][...])
         theirs = jnp.logical_xor(edge_lanes(0), jnp.logical_not(upper))
         edge = jnp.where(theirs, received, kept)
         place = QUADS if merge else SLOTS
@@ -169,8 +202,7 @@
             turned = jnp.concatenate(shifts, axis=0).T.astype(F32)
             turned_ref[a * PITCH : a * PITCH + LANES, :] = turned
         for q in range(QUADS):
-            rows = [turned_ref[pl.ds(part * QUADS + q, RANK, stride=PITCH), :] for part in range(4)]
-            arranged_ref[q] = jnp.concatenate(rows, axis=0).astype(BF16).T
+            arranged_ref[q] = dense_quad(turned_ref, q)
         if half == 0:
             border_ref[0] = arranged_ref[0, RANK : 2 * RANK, :]
         else:
@@ -210,13 +242,24 @@
 
 
 def tail_kernel(
-    level, last_ref, root_ref, kept_ref, received_ref, beside_ref, near_ref, border_ref, product_ref, rows_ref
+    level,
+    partial_ref,
+    last_ref,
+    root_ref,
+    kept_ref,
+    received_ref,
+    beside_ref,
+    near_ref,
+    border_ref,
+    product_ref,
+    coeffs_ref,
+    rows_ref,
 ):
-    upper = level_bit(level)
-    beside = meet_border(level, upper, kept_ref[QUADS], received_ref[QUADS], beside_ref[...])
     for q in range(QUADS):
-        mixed = mix_quad(last_ref, q, upper, kept_ref[q], received_ref[q])
-        mixed = section_quad(root_ref, q, mixed[:, :LANES], mixed[:, LANES:])
+        coeffs_ref[q] = arrive(partial_ref, last_ref, q, received_ref[q])
+    beside = meet_border(level, level_bit(level), kept_ref[QUADS], received_ref[QUADS], beside_ref[...])
+    for q in range(QUADS):
+        mixed = section_quad(root_ref, q, coeffs_ref[q, :, :LANES], coeffs_ref[q, :, LANES:])
         for half in range(2):
             total = mixed[:, half * LANES : (half + 1) * LANES] + near_ref[half, q]
             if q == half * (QUADS - 1):
@@ -267,6 +310,22 @@
     )(factors, after)
 
 
+def stage(level, weights, index, kept, after):
+    return pl.pallas_call(
+        functools.partial(stage_kernel, level, index, len(kept)),
+        out_shape=(
+            jax.ShapeDtypeStruct((QUADS, RHS, 2 * LANES), F32),
+            jax.ShapeDtypeStruct((QUADS, 2, RANK, LANES), BF16),
+        ),
+        in_specs=[VMEM_SPEC] * (1 + len(kept)) + [ANY_SPEC],
+        out_specs=(VMEM_SPEC, VMEM_SPEC),
+        scratch_shapes=[TURNED],
+        compiler_params=params(16),
+        cost_estimate=pl.CostEstimate(flops=2 * 10**6, bytes_accessed=2 * 2**20, transcendentals=0),
+        name="stage",
+    )(weights, *kept, after)
+
+
 def head(vectors, factors):
     section = (2 * RANK, 2 * RANK, HALF)
     outs = [payload(chain) for chain in range(CHAINS) for _ in range(2)]
@@ -277,12 +336,12 @@
         in_specs=[HBM_SPEC, HBM_SPEC],
         out_specs=(VMEM_SPEC,) * len(outs),
         scratch_shapes=[
-            pltpu.VMEM((RHS, RANK, 2 * HALF), BF16),
+            pltpu.VMEM((2, RHS, RANK, HALF), BF16),
             pltpu.VMEM(section, BF16),
             pltpu.VMEM((2, RHS * (QUADS + 1), LANES), F32),
             TURNED,
             pltpu.VMEM(ARRANGED, BF16),
-            pltpu.SemaphoreType.DMA((3,)),
+            pltpu.SemaphoreType.DMA((4,)),
         ],
         compiler_params=params(14),
         name="head",
@@ -290,11 +349,11 @@
     return pairs[::2], pairs[1::2], halves, section_1
 
 
-def level_step(level, chain, arranged, kept, received, beside, into=None):
+def level_step(level, chain, partial, arranged, kept, received, beside, into=None):
     merge = into is not None
-    edges = [beside] if chain == 0 else []
+    edges = [kept, beside] if chain == 0 else []
     filled = list(into) if merge and chain > 0 else []
-    outs = [payload(chain, merge)] * 2 + [EDGE] * len(edges)
+    outs = [payload(chain, merge)] * 2 + [EDGE] * (chain == 0)
     return pl.pallas_call(
         functools.partial(level_kernel, level, chain, merge),
         out_shape=tuple(outs),
@@ -303,7 +362,7 @@
         input_output_aliases={3: 0, 4: 1} if filled else {},
         compiler_params=params(6),
         name="level",
-    )(arranged, kept, received, *edges, *filled)
+    )(partial, arranged, received, *edges, *filled)
 
 
 def near_field(halves, neighbor_blocks, after):
@@ -328,7 +387,10 @@
         out_shape=jax.ShapeDtypeStruct((RHS, RANK, 2 * HALF), BF16),
         in_specs=[VMEM_SPEC] * len(operands),
         out_specs=VMEM_SPEC,
-        scratch_shapes=[pltpu.VMEM((2, QUADS * (RHS + 1), LANES), F32)],
+        scratch_shapes=[
+            pltpu.VMEM((QUADS, RHS, 2 * LANES), BF16),
+            pltpu.VMEM((2, QUADS * (RHS + 1), LANES), F32),
+        ],
         compiler_params=params(12),
         name="tail",
     )(*operands)
@@ -344,12 +406,12 @@
         partners = [(i, i ^ (1 << level)) for i in range(count)]
         received = [lax.ppermute(part, "rows", partners) for part in sending]
         if level == 0:
-            arranged = arrange(section_1, None, sending[-1])
+            staged = stage(level, section_1, None, kept, sending[-1])
         else:
-            arranged = arrange(factors, level + 1, sending[-1])
+            staged = stage(level, factors, level + 1, kept, sending[-1])
         into = () if level == level_count - 2 else None
         for chain in range(CHAINS):
-            outs = level_step(level, chain, arranged, kept[chain], received[chain], beside, into)
+            outs = level_step(level, chain, *staged, kept[chain], received[chain], beside, into)
             kept[chain], sending[chain] = outs[:2]
             if chain == 0:
                 beside = outs[2]
@@ -359,9 +421,9 @@
     kept, sending = into
     received = lax.ppermute(sending, "rows", [(i, i ^ (1 << level)) for i in range(count)])
     near, border = near_field(halves, neighbor_blocks, sending)
-    last = arrange(factors, level + 1, sending)
+    partial, last = stage(level, factors, level + 1, [kept], sending)
     root = arrange(factors, level + 2, sending)
-    return tail(level, last, root, kept, received, beside, near, border)
+    return tail(level, partial, last, root, kept, received, beside, near, border)
 
 
 def solution(mesh):

time: 58.6 us -> 57.1 us (0.974); the launches traced: 57.7 us -> 57 us
  waiting for transfers between devices: 9.19 us -> 13.4 us
  starting transfers between devices: 30.3 us -> 26.7 us
  Pallas kernels: 18.1 us -> 16.9 us
    pallas_call x0 -> x8, Pallas kernels: none -> 6.17 us  [stage(): pl.pallas_call(functools.partial(stage_kernel, level, index, len(kept)),...]
    pallas_call x9 -> x1, Pallas kernels: 5.74 us -> 0.64 us  [arrange(): pl.pallas_call(functools.partial(arrange_kernel, index), out_shape=jax.Sh...]
    ppermute x1, starting transfers between devices: 7.71 us -> 4.6 us  [shards(): lax.ppermute(sending, 'rows', [(i, i ^ 1 << level) for i in range(count)])]
    ppermute x14, waiting for transfers between devices: 9.17 us -> 12.1 us  [shards(): received = [lax.ppermute(part, 'rows', partners) for part in sending]]
    pallas_call x14, Pallas kernels: 5.4 us -> 3.65 us  [level_step(): pl.pallas_call(functools.partial(level_kernel, level, chain, merge), out_...]
    ppermute x1, waiting for transfers between devices: 0.02 us -> 1.31 us  [shards(): lax.ppermute(sending, 'rows', [(i, i ^ 1 << level) for i in range(count)])]
  transfers between devices with their start and end apart: 15 -> 15, of which waited for: 8 -> 8; matrix products, arithmetic and copies ran while one was open for 0% -> 0% of each run, Pallas kernels for 22% -> 21%
where the time goes in v3:
time: 57.1 us; the launch traced here: 57 us
  starting transfers between devices  26.7 us (47%)
  Pallas kernels  16.9 us (30%)
  waiting for transfers between devices  13.4 us (23%)
    ppermute x14, starting transfers between devices, shards(): received = [lax.ppermute(part, 'rows', partners) for part in sending]  22.1 us
    ppermute x14, waiting for transfers between devices, shards(): received = [lax.ppermute(part, 'rows', partners) for part in sending]  12.1 us
    pallas_call x8, Pallas kernels, stage(): pl.pallas_call(functools.partial(stage_kernel, level, index, len(kept)),...  6.17 us
    ppermute x1, starting transfers between devices, shards(): lax.ppermute(sending, 'rows', [(i, i ^ 1 << level) for i in range(count)])  4.6 us
    pallas_call x14, Pallas kernels, level_step(): pl.pallas_call(functools.partial(level_kernel, level, chain, merge), out_...  3.65 us
    pallas_call x1, Pallas kernels, head(): pl.pallas_call(head_kernel, out_shape=tuple(outs), in_specs=[HBM_SPEC, HB...  2.75 us
    pallas_call x1, Pallas kernels, tail(): pl.pallas_call(functools.partial(tail_kernel, level), out_shape=jax.Shape...  1.98 us
    pallas_call x1, Pallas kernels, near_field(): pl.pallas_call(near_kernel, out_shape=(jax.ShapeDtypeStruct((2, QUADS, RH...  1.67 us
  transfers between devices with their start and end apart: 15, of which 8 were waited for; matrix products, arithmetic and copies ran while one was open for 0% of the time, Pallas kernels for 21%

profile of v3, /device:TPU:6, one launch (start us, length us, event | category | flops | bytes accessed | tf_op | source)
XLA Modules:
  0.0 57.0 jit_solution(9192932839158193529)
XLA Ops:
  0.0 2.7 %head.1 = (bf16[17,16,128]{2,1,0:T(8,128)(2,1)S(1)}, bf16[17,16,128]{2,1,0:T(8,128)(2,1)S(1)}, bf16[16,16,128]{2,1,0:T(8,128)(2,1)S(1)}, bf16[16,16,128]{2,1,0:T...) custom-call(bf16[16,32,256]{2,1,0:T(8,128)(2,1)} %vectors_hbm.1, ...), custom_call_target="tpu_custom_call" | custom-call | tf_op jit(solution)/shard_map/head/pallas_call | solution.py:333
  2.9 0.5 collective-permute-start.1
  3.4 0.8 %stage.8 = (f32[32,16,256]{2,1,0:T(8,128)S(1)}, bf16[32,2,32,128]{3,2,1,0:T(8,128)(2,1)S(1)}) custom-call(bf16[64,64,128]{2,1,0:T(8,128)(2,1)S(1)} %get-tuple-element.68.refs_0_, bf16[17,16,128]{2,1,0:T(8,128)(2,1)S(1)} %get-tuple-element.69.refs_1_.refs_3_, bf16[16,16,128]{2,1,0:T(8,128)(2,1)S(1)} %get-tuple-element.70.refs_2_, ...), custom_call_target="tpu_custom_call" | custom-call | flops 2000000 | bytes 2097152 | tf_op jit(solution)/shard_map/stage/pallas_call | solution.py:314
  4.4 0.9 %collective-permute-start.2 = (bf16[17,16,128]{2,1,0:T(8,128)(2,1)S(1)}, bf16[17,16,128]{2,1,0:T(8,128)(2,1)S(1)}, u32[]{:S(2)}, u32[]{:S(2)}) collective-permute-start(bf16[17,16,128]{2,1,0:T(8,128)(2,1)S(1)} %get-tuple-element.80), channel_id=1, source_target_pairs={{0,2},{1,3},{2,0},{3,1},{4,6},{5,7},{6,4},{7,5},{8,10},{9,11},{10,... | collective-permute-start | bytes 208904 | tf_op jit(solution)/shard_map/ppermute | solution.py:407
  5.6 1.3 %collective-permute-start.3 = (bf16[16,16,128]{2,1,0:T(8,128)(2,1)S(1)}, bf16[16,16,128]{2,1,0:T(8,128)(2,1)S(1)}, u32[]{:S(2)}, u32[]{:S(2)}) collective-permute-start(bf16[16,16,128]{2,1,0:T(8,128)(2,1)S(1)} %get-tuple-element.77.refs_3_), channel_id=1, source_target_pairs={{0,2},{1,3},{2,0},{3,1},{4,6},{5,7},{6,4},{7,5},{8,10},{9,11},{10,... | collective-permute-start | bytes 196616 | tf_op jit(solution)/shard_map/ppermute | solution.py:407
  6.9 0.8 %stage.9 = (f32[32,16,256]{2,1,0:T(8,128)S(1)}, bf16[32,2,32,128]{3,2,1,0:T(8,128)(2,1)S(1)}) custom-call(bf16[10,64,64,128]{3,2,1,0:T(8,128)(2,1)S(1)} %copy-done, bf16[17,16,128]{2,1,0:T(8,128)(2,1)S(1)} %get-tuple-element.75.refs_1_.refs_3_, bf16[16,16,128]{2,1,0:T(8,128)(2,1)S(1)} %get-tuple-element.76.refs_2_, ...), custom_call_target="tpu_custom_call" | custom-call | flops 2000000 | bytes 2097152 | tf_op jit(solution)/shard_map/stage/pallas_call | solution.py:314
  7.6 1.8 %collective-permute-done.2.refs_2_ = bf16[17,16,128]{2,1,0:T(8,128)(2,1)S(1)} collective-permute-done((bf16[17,16,128]{2,1,0:T(8,128)(2,1)S(1)}, bf16[17,16,128]{2,1,0:T(8,128)(2,1)S(1)}, u32[]{:S(2)}, u32[]{:S(2)}) %collective-permute-start.2) | collective-permute-done | bytes 69664 | tf_op jit(solution)/shard_map/ppermute | solution.py:407
  9.7 1.2 %collective-permute-start.4 = (bf16[17,16,128]{2,1,0:T(8,128)(2,1)S(1)}, bf16[17,16,128]{2,1,0:T(8,128)(2,1)S(1)}, u32[]{:S(2)}, u32[]{:S(2)}) collective-permute-start(bf16[17,16,128]{2,1,0:T(8,128)(2,1)S(1)} %get-tuple-element.87), channel_id=1, source_target_pairs={{0,4},{1,5},{2,6},{3,7},{4,0},{5,1},{6,2},{7,3},{8,12},{9,13},{10,... | collective-permute-start | bytes 208904 | tf_op jit(solution)/shard_map/ppermute | solution.py:407
  11.2 2.5 %collective-permute-start.5 = (bf16[16,16,128]{2,1,0:T(8,128)(2,1)S(1)}, bf16[16,16,128]{2,1,0:T(8,128)(2,1)S(1)}, u32[]{:S(2)}, u32[]{:S(2)}) collective-permute-start(bf16[16,16,128]{2,1,0:T(8,128)(2,1)S(1)} %get-tuple-element.84.refs_3_), channel_id=1, source_target_pairs={{0,4},{1,5},{2,6},{3,7},{4,0},{5,1},{6,2},{7,3},{8,12},{9,13},{10,... | collective-permute-start | bytes 196616 | tf_op jit(solution)/shard_map/ppermute | solution.py:407
  13.7 0.8 %stage.10 = (f32[32,16,256]{2,1,0:T(8,128)S(1)}, bf16[32,2,32,128]{3,2,1,0:T(8,128)(2,1)S(1)}) custom-call(bf16[10,64,64,128]{3,2,1,0:T(8,128)(2,1)S(1)} %copy-done, bf16[17,16,128]{2,1,0:T(8,128)(2,1)S(1)} %get-tuple-element.82.refs_1_.refs_3_, bf16[16,16,128]{2,1,0:T(8,128)(2,1)S(1)} %get-tuple-element.83.refs_2_, ...), custom_call_target="tpu_custom_call" | custom-call | flops 2000000 | bytes 2097152 | tf_op jit(solution)/shard_map/stage/pallas_call | solution.py:314
  14.5 1.7 %collective-permute-done.4.refs_2_ = bf16[17,16,128]{2,1,0:T(8,128)(2,1)S(1)} collective-permute-done((bf16[17,16,128]{2,1,0:T(8,128)(2,1)S(1)}, bf16[17,16,128]{2,1,0:T(8,128)(2,1)S(1)}, u32[]{:S(2)}, u32[]{:S(2)}) %collective-permute-start.4) | collective-permute-done | bytes 69664 | tf_op jit(solution)/shard_map/ppermute | solution.py:407
  16.5 1.1 %collective-permute-start.6 = (bf16[17,16,128]{2,1,0:T(8,128)(2,1)S(1)}, bf16[17,16,128]{2,1,0:T(8,128)(2,1)S(1)}, u32[]{:S(2)}, u32[]{:S(2)}) collective-permute-start(bf16[17,16,128]{2,1,0:T(8,128)(2,1)S(1)} %get-tuple-element.94), channel_id=1, source_target_pairs={{0,8},{1,9},{2,10},{3,11},{4,12},{5,13},{6,14},{7,15},{8,0},{9,1},... | collective-permute-start | bytes 208904 | tf_op jit(solution)/shard_map/ppermute | solution.py:407
  17.8 1.4 %collective-permute-start.7 = (bf16[16,16,128]{2,1,0:T(8,128)(2,1)S(1)}, bf16[16,16,128]{2,1,0:T(8,128)(2,1)S(1)}, u32[]{:S(2)}, u32[]{:S(2)}) collective-permute-start(bf16[16,16,128]{2,1,0:T(8,128)(2,1)S(1)} %get-tuple-element.91.refs_3_), channel_id=1, source_target_pairs={{0,8},{1,9},{2,10},{3,11},{4,12},{5,13},{6,14},{7,15},{8,0},{9,1},... | collective-permute-start | bytes 196616 | tf_op jit(solution)/shard_map/ppermute | solution.py:407
  19.2 0.8 %stage.11 = (f32[32,16,256]{2,1,0:T(8,128)S(1)}, bf16[32,2,32,128]{3,2,1,0:T(8,128)(2,1)S(1)}) custom-call(bf16[10,64,64,128]{3,2,1,0:T(8,128)(2,1)S(1)} %copy-done, bf16[17,16,128]{2,1,0:T(8,128)(2,1)S(1)} %get-tuple-element.89.refs_1_.refs_3_, bf16[16,16,128]{2,1,0:T(8,128)(2,1)S(1)} %get-tuple-element.90.refs_2_, ...), custom_call_target="tpu_custom_call" | custom-call | flops 2000000 | bytes 2097152 | tf_op jit(solution)/shard_map/stage/pallas_call | solution.py:314
  20.0 0.9 %collective-permute-done.6.refs_2_ = bf16[17,16,128]{2,1,0:T(8,128)(2,1)S(1)} collective-permute-done((bf16[17,16,128]{2,1,0:T(8,128)(2,1)S(1)}, bf16[17,16,128]{2,1,0:T(8,128)(2,1)S(1)}, u32[]{:S(2)}, u32[]{:S(2)}) %collective-permute-start.6) | collective-permute-done | bytes 69664 | tf_op jit(solution)/shard_map/ppermute | solution.py:407
  21.1 2.7 %collective-permute-start.8 = (bf16[17,16,128]{2,1,0:T(8,128)(2,1)S(1)}, bf16[17,16,128]{2,1,0:T(8,128)(2,1)S(1)}, u32[]{:S(2)}, u32[]{:S(2)}) collective-permute-start(bf16[17,16,128]{2,1,0:T(8,128)(2,1)S(1)} %get-tuple-element.101), channel_id=1, source_target_pairs={{0,16},{1,17},{2,18},{3,19},{4,20},{5,21},{6,22},{7,23},{8,24},{9,... | collective-permute-start | bytes 208904 | tf_op jit(solution)/shard_map/ppermute | solution.py:407
  24.1 1.7 %collective-permute-start.9 = (bf16[16,16,128]{2,1,0:T(8,128)(2,1)S(1)}, bf16[16,16,128]{2,1,0:T(8,128)(2,1)S(1)}, u32[]{:S(2)}, u32[]{:S(2)}) collective-permute-start(bf16[16,16,128]{2,1,0:T(8,128)(2,1)S(1)} %get-tuple-element.98.refs_3_), channel_id=1, source_target_pairs={{0,16},{1,17},{2,18},{3,19},{4,20},{5,21},{6,22},{7,23},{8,24},{9,... | collective-permute-start | bytes 196616 | tf_op jit(solution)/shard_map/ppermute | solution.py:407
  25.8 0.8 %stage.12 = (f32[32,16,256]{2,1,0:T(8,128)S(1)}, bf16[32,2,32,128]{3,2,1,0:T(8,128)(2,1)S(1)}) custom-call(bf16[10,64,64,128]{3,2,1,0:T(8,128)(2,1)S(1)} %copy-done, bf16[17,16,128]{2,1,0:T(8,128)(2,1)S(1)} %get-tuple-element.96.refs_1_.refs_3_, bf16[16,16,128]{2,1,0:T(8,128)(2,1)S(1)} %get-tuple-element.97.refs_2_, ...), custom_call_target="tpu_custom_call" | custom-call | flops 2000000 | bytes 2097152 | tf_op jit(solution)/shard_map/stage/pallas_call | solution.py:314
  27.3 1.7 %collective-permute-start.10 = (bf16[17,16,128]{2,1,0:T(8,128)(2,1)S(1)}, bf16[17,16,128]{2,1,0:T(8,128)(2,1)S(1)}, u32[]{:S(2)}, u32[]{:S(2)}) collective-permute-start(bf16[17,16,128]{2,1,0:T(8,128)(2,1)S(1)} %get-tuple-element.108), channel_id=1, source_target_pairs={{0,32},{1,33},{2,34},{3,35},{4,36},{5,37},{6,38},{7,39},{8,40},{9,... | collective-permute-start | bytes 208904 | tf_op jit(solution)/shard_map/ppermute | solution.py:407
  28.9 1.0 %collective-permute-done.9.refs_2_ = bf16[16,16,128]{2,1,0:T(8,128)(2,1)S(1)} collective-permute-done((bf16[16,16,128]{2,1,0:T(8,128)(2,1)S(1)}, bf16[16,16,128]{2,1,0:T(8,128)(2,1)S(1)}, u32[]{:S(2)}, u32[]{:S(2)}) %collective-permute-start.9) | collective-permute-done | bytes 65568 | tf_op jit(solution)/shard_map/ppermute | solution.py:407
  30.2 2.4 %collective-permute-start.11 = (bf16[16,16,128]{2,1,0:T(8,128)(2,1)S(1)}, bf16[16,16,128]{2,1,0:T(8,128)(2,1)S(1)}, u32[]{:S(2)}, u32[]{:S(2)}) collective-permute-start(bf16[16,16,128]{2,1,0:T(8,128)(2,1)S(1)} %get-tuple-element.105.refs_3_), channel_id=1, source_target_pairs={{0,32},{1,33},{2,34},{3,35},{4,36},{5,37},{6,38},{7,39},{8,40},{9,... | collective-permute-start | bytes 196616 | tf_op jit(solution)/shard_map/ppermute | solution.py:407
  32.6 0.8 %stage.13 = (f32[32,16,256]{2,1,0:T(8,128)S(1)}, bf16[32,2,32,128]{3,2,1,0:T(8,128)(2,1)S(1)}) custom-call(bf16[10,64,64,128]{3,2,1,0:T(8,128)(2,1)S(1)} %copy-done, bf16[17,16,128]{2,1,0:T(8,128)(2,1)S(1)} %get-tuple-element.103.refs_1_.refs_3_, bf16[16,16,128]{2,1,0:T(8,128)(2,1)S(1)} %get-tuple-element.104.refs_2_, ...), custom_call_target="tpu_custom_call" | custom-call | flops 2000000 | bytes 2097152 | tf_op jit(solution)/shard_map/stage/pallas_call | solution.py:314
  33.6 3.4 %collective-permute-start.13 = (bf16[17,16,128]{2,1,0:T(8,128)(2,1)S(1)}, bf16[17,16,128]{2,1,0:T(8,128)(2,1)S(1)}, u32[]{:S(2)}, u32[]{:S(2)}) collective-permute-start(bf16[17,16,128]{2,1,0:T(8,128)(2,1)S(1)} %get-tuple-element.115), channel_id=1, source_target_pairs={{0,64},{1,65},{2,66},{3,67},{4,68},{5,69},{6,70},{7,71},{8,72},{9,... | collective-permute-start | bytes 208904 | tf_op jit(solution)/shard_map/ppermute | solution.py:407
  37.3 1.3 %collective-permute-start.12 = (bf16[16,16,128]{2,1,0:T(8,128)(2,1)S(1)}, bf16[16,16,128]{2,1,0:T(8,128)(2,1)S(1)}, u32[]{:S(2)}, u32[]{:S(2)}) collective-permute-start(bf16[16,16,128]{2,1,0:T(8,128)(2,1)S(1)} %get-tuple-element.112.refs_3_), channel_id=1, source_target_pairs={{0,64},{1,65},{2,66},{3,67},{4,68},{5,69},{6,70},{7,71},{8,72},{9,... | collective-permute-start | bytes 196616 | tf_op jit(solution)/shard_map/ppermute | solution.py:407
  38.6 0.8 %stage.14 = (f32[32,16,256]{2,1,0:T(8,128)S(1)}, bf16[32,2,32,128]{3,2,1,0:T(8,128)(2,1)S(1)}) custom-call(bf16[10,64,64,128]{3,2,1,0:T(8,128)(2,1)S(1)} %copy-done, bf16[17,16,128]{2,1,0:T(8,128)(2,1)S(1)} %get-tuple-element.110.refs_1_.refs_3_, bf16[16,16,128]{2,1,0:T(8,128)(2,1)S(1)} %get-tuple-element.111.refs_2_, ...), custom_call_target="tpu_custom_call" | custom-call | flops 2000000 | bytes 2097152 | tf_op jit(solution)/shard_map/stage/pallas_call | solution.py:314
  39.9 5.9 %collective-permute-done.12.refs_2_ = bf16[16,16,128]{2,1,0:T(8,128)(2,1)S(1)} collective-permute-done((bf16[16,16,128]{2,1,0:T(8,128)(2,1)S(1)}, bf16[16,16,128]{2,1,0:T(8,128)(2,1)S(1)}, u32[]{:S(2)}, u32[]{:S(2)}) %collective-permute-start.12) | collective-permute-done | bytes 65568 | tf_op jit(solution)/shard_map/ppermute | solution.py:407
  46.0 4.6 %collective-permute-start.14 = (bf16[33,16,128]{2,1,0:T(8,128)(2,1)S(1)}, bf16[33,16,128]{2,1,0:T(8,128)(2,1)S(1)}, u32[]{:S(2)}, u32[]{:S(2)}) collective-permute-start(bf16[33,16,128]{2,1,0:T(8,128)(2,1)S(1)} %get-tuple-element.120.refs_2_.after_ref), channel_id=1, source_target_pairs={{0,128},{1,129},{2,130},{3,131},{4,132},{5,133},{6,134},{7,135},{8... | collective-permute-start | bytes 405512 | tf_op jit(solution)/shard_map/ppermute | solution.py:422
  50.6 0.6 %arrange.1.root_ref = bf16[32,2,64,128]{3,2,1,0:T(8,128)(2,1)S(1)} custom-call(bf16[10,64,64,128]{3,2,1,0:T(8,128)(2,1)S(1)} %copy-done, bf16[33,16,128]{2,1,0:T(8,128)(2,1)S(1)} %get-tuple-element.120.refs_2_.after_ref), custom_call_target="tpu_custom_call" | custom-call | flops 2000000 | bytes 2097152 | tf_op jit(solution)/shard_map/arrange/pallas_call | solution.py:301
  51.3 0.8 %stage.15 = (f32[32,16,256]{2,1,0:T(8,128)S(1)}, bf16[32,2,32,128]{3,2,1,0:T(8,128)(2,1)S(1)}) custom-call(bf16[10,64,64,128]{3,2,1,0:T(8,128)(2,1)S(1)} %copy-done, bf16[33,16,128]{2,1,0:T(8,128)(2,1)S(1)} %get-tuple-element.119.refs_1_.kept_ref, bf16[33,16,128]{2,1,0:T(8,128)(2,1)S(1)} %get-tuple-element.120.refs_2_.after_ref), custom_call_target="tpu_custom_call" | custom-call | flops 2000000 | bytes 2097152 | tf_op jit(solution)/shard_map/stage/pallas_call | solution.py:314
  52.0 1.7 %near.1 = (f32[2,32,16,128]{3,2,1,0:T(8,128)S(1)}, bf16[2,32,128]{2,1,0:T(8,128)(2,1)S(1)}) custom-call(bf16[2,32,16,128]{3,2,1,0:T(8,128)(2,1)S(1)} %get-tuple-element.124.halves_ref, bf16[3,32,32,256]{3,2,1,0:T(8,128)(2,1)S(1)} %copy-done.1, bf16[33,16,128]{2,1,0:T(8,128)(2,1)S(1)} %get-tuple-element.120.refs_2_.after_ref), custom_call_target="tpu_custom_call" | custom-call | flops 4000000 | bytes 3145728 | tf_op jit(solution)/shard_map/near/pallas_call | solution.py:369
  53.7 1.3 %collective-permute-done.14.received_ref = bf16[33,16,128]{2,1,0:T(8,128)(2,1)S(1)} collective-permute-done((bf16[33,16,128]{2,1,0:T(8,128)(2,1)S(1)}, bf16[33,16,128]{2,1,0:T(8,128)(2,1)S(1)}, u32[]{:S(2)}, u32[]{:S(2)}) %collective-permute-start.14) | collective-permute-done | bytes 135200 | tf_op jit(solution)/shard_map/ppermute | solution.py:422
  55.0 2.0 %tail.1 = bf16[16,32,256]{2,1,0:T(8,128)(2,1)} custom-call(f32[32,16,256]{2,1,0:T(8,128)S(1)} %get-tuple-element.121.partial_ref, bf16[32,2,32,128]{3,2,1,0:T(8,128)(2,1)S(1)} %get-tuple-element.122.last_ref, bf16[32,2,64,128]{3,2,1,0:T(8,128)(2,1)S(1)} %arrange.1.root_ref, bf16[33,16,128]{2,1,0:T(8,128)(2,1)S(1)} %get-tuple-element.119.refs_1_.kept_ref, ...), custom_call_target="tpu_custom_call" | custom-call | tf_op jit(solution)/shard_map/tail/pallas_call | solution.py:385
  (29 shorter events, 4.4 us)
Async XLA Ops:
  0.0 6.9 %copy-start = (bf16[10,64,64,128]{3,2,1,0:T(8,128)(2,1)S(1)}, bf16[10,64,64,128]{3,2,1,0:T(8,128)(2,1)}, u32[]{:S(2)}) copy-start(bf16[10,64,64,128]{3,2,1,0:T(8,128)(2,1)} %weights_ref) | copy-start | bytes 31457284
  2.8 1.4 %collective-permute-start = (bf16[17,16,128]{2,1,0:T(8,128)(2,1)S(1)}, bf16[17,16,128]{2,1,0:T(8,128)(2,1)S(1)}, u32[]{:S(2)}, u32[]{:S(2)}) collective-permute-start(bf16[17,16,128]{2,1,0:T(8,128)(2,1)S(1)} %get-tuple-element.74), channel_id=1, source_target_pairs={{0,1},{1,0},{2,3},{3,2},{4,5},{5,4},{6,7},{7,6},{8,9},{9,8},{10,11... | collective-permute-start | bytes 208904 | tf_op jit(solution)/shard_map/ppermute | solution.py:407
  2.9 2.5 %collective-permute-start.1 = (bf16[16,16,128]{2,1,0:T(8,128)(2,1)S(1)}, bf16[16,16,128]{2,1,0:T(8,128)(2,1)S(1)}, u32[]{:S(2)}, u32[]{:S(2)}) collective-permute-start(bf16[16,16,128]{2,1,0:T(8,128)(2,1)S(1)} %get-tuple-element.71.refs_3_), channel_id=1, source_target_pairs={{0,1},{1,0},{2,3},{3,2},{4,5},{5,4},{6,7},{7,6},{8,9},{9,8},{10,11... | collective-permute-start | bytes 196616 | tf_op jit(solution)/shard_map/ppermute | solution.py:407
  4.4 5.1 %collective-permute-start.2 = (bf16[17,16,128]{2,1,0:T(8,128)(2,1)S(1)}, bf16[17,16,128]{2,1,0:T(8,128)(2,1)S(1)}, u32[]{:S(2)}, u32[]{:S(2)}) collective-permute-start(bf16[17,16,128]{2,1,0:T(8,128)(2,1)S(1)} %get-tuple-element.80), channel_id=1, source_target_pairs={{0,2},{1,3},{2,0},{3,1},{4,6},{5,7},{6,4},{7,5},{8,10},{9,11},{10,... | collective-permute-start | bytes 208904 | tf_op jit(solution)/shard_map/ppermute | solution.py:407
  5.6 5.4 %collective-permute-start.3 = (bf16[16,16,128]{2,1,0:T(8,128)(2,1)S(1)}, bf16[16,16,128]{2,1,0:T(8,128)(2,1)S(1)}, u32[]{:S(2)}, u32[]{:S(2)}) collective-permute-start(bf16[16,16,128]{2,1,0:T(8,128)(2,1)S(1)} %get-tuple-element.77.refs_3_), channel_id=1, source_target_pairs={{0,2},{1,3},{2,0},{3,1},{4,6},{5,7},{6,4},{7,5},{8,10},{9,11},{10,... | collective-permute-start | bytes 196616 | tf_op jit(solution)/shard_map/ppermute | solution.py:407
  9.7 6.5 %collective-permute-start.4 = (bf16[17,16,128]{2,1,0:T(8,128)(2,1)S(1)}, bf16[17,16,128]{2,1,0:T(8,128)(2,1)S(1)}, u32[]{:S(2)}, u32[]{:S(2)}) collective-permute-start(bf16[17,16,128]{2,1,0:T(8,128)(2,1)S(1)} %get-tuple-element.87), channel_id=1, source_target_pairs={{0,4},{1,5},{2,6},{3,7},{4,0},{5,1},{6,2},{7,3},{8,12},{9,13},{10,... | collective-permute-start | bytes 208904 | tf_op jit(solution)/shard_map/ppermute | solution.py:407
  11.2 6.3 %collective-permute-start.5 = (bf16[16,16,128]{2,1,0:T(8,128)(2,1)S(1)}, bf16[16,16,128]{2,1,0:T(8,128)(2,1)S(1)}, u32[]{:S(2)}, u32[]{:S(2)}) collective-permute-start(bf16[16,16,128]{2,1,0:T(8,128)(2,1)S(1)} %get-tuple-element.84.refs_3_), channel_id=1, source_target_pairs={{0,4},{1,5},{2,6},{3,7},{4,0},{5,1},{6,2},{7,3},{8,12},{9,13},{10,... | collective-permute-start | bytes 196616 | tf_op jit(solution)/shard_map/ppermute | solution.py:407
  16.5 4.4 %collective-permute-start.6 = (bf16[17,16,128]{2,1,0:T(8,128)(2,1)S(1)}, bf16[17,16,128]{2,1,0:T(8,128)(2,1)S(1)}, u32[]{:S(2)}, u32[]{:S(2)}) collective-permute-start(bf16[17,16,128]{2,1,0:T(8,128)(2,1)S(1)} %get-tuple-element.94), channel_id=1, source_target_pairs={{0,8},{1,9},{2,10},{3,11},{4,12},{5,13},{6,14},{7,15},{8,0},{9,1},... | collective-permute-start | bytes 208904 | tf_op jit(solution)/shard_map/ppermute | solution.py:407
  17.8 6.0 %collective-permute-start.7 = (bf16[16,16,128]{2,1,0:T(8,128)(2,1)S(1)}, bf16[16,16,128]{2,1,0:T(8,128)(2,1)S(1)}, u32[]{:S(2)}, u32[]{:S(2)}) collective-permute-start(bf16[16,16,128]{2,1,0:T(8,128)(2,1)S(1)} %get-tuple-element.91.refs_3_), channel_id=1, source_target_pairs={{0,8},{1,9},{2,10},{3,11},{4,12},{5,13},{6,14},{7,15},{8,0},{9,1},... | collective-permute-start | bytes 196616 | tf_op jit(solution)/shard_map/ppermute | solution.py:407
  21.1 5.9 %collective-permute-start.8 = (bf16[17,16,128]{2,1,0:T(8,128)(2,1)S(1)}, bf16[17,16,128]{2,1,0:T(8,128)(2,1)S(1)}, u32[]{:S(2)}, u32[]{:S(2)}) collective-permute-start(bf16[17,16,128]{2,1,0:T(8,128)(2,1)S(1)} %get-tuple-element.101), channel_id=1, source_target_pairs={{0,16},{1,17},{2,18},{3,19},{4,20},{5,21},{6,22},{7,23},{8,24},{9,... | collective-permute-start | bytes 208904 | tf_op jit(solution)/shard_map/ppermute | solution.py:407
  24.1 5.9 %collective-permute-start.9 = (bf16[16,16,128]{2,1,0:T(8,128)(2,1)S(1)}, bf16[16,16,128]{2,1,0:T(8,128)(2,1)S(1)}, u32[]{:S(2)}, u32[]{:S(2)}) collective-permute-start(bf16[16,16,128]{2,1,0:T(8,128)(2,1)S(1)} %get-tuple-element.98.refs_3_), channel_id=1, source_target_pairs={{0,16},{1,17},{2,18},{3,19},{4,20},{5,21},{6,22},{7,23},{8,24},{9,... | collective-permute-start | bytes 196616 | tf_op jit(solution)/shard_map/ppermute | solution.py:407
  27.3 6.1 %collective-permute-start.10 = (bf16[17,16,128]{2,1,0:T(8,128)(2,1)S(1)}, bf16[17,16,128]{2,1,0:T(8,128)(2,1)S(1)}, u32[]{:S(2)}, u32[]{:S(2)}) collective-permute-start(bf16[17,16,128]{2,1,0:T(8,128)(2,1)S(1)} %get-tuple-element.108), channel_id=1, source_target_pairs={{0,32},{1,33},{2,34},{3,35},{4,36},{5,37},{6,38},{7,39},{8,40},{9,... | collective-permute-start | bytes 208904 | tf_op jit(solution)/shard_map/ppermute | solution.py:407
  30.2 6.8 %collective-permute-start.11 = (bf16[16,16,128]{2,1,0:T(8,128)(2,1)S(1)}, bf16[16,16,128]{2,1,0:T(8,128)(2,1)S(1)}, u32[]{:S(2)}, u32[]{:S(2)}) collective-permute-start(bf16[16,16,128]{2,1,0:T(8,128)(2,1)S(1)} %get-tuple-element.105.refs_3_), channel_id=1, source_target_pairs={{0,32},{1,33},{2,34},{3,35},{4,36},{5,37},{6,38},{7,39},{8,40},{9,... | collective-permute-start | bytes 196616 | tf_op jit(solution)/shard_map/ppermute | solution.py:407
  33.6 6.0 %collective-permute-start.13 = (bf16[17,16,128]{2,1,0:T(8,128)(2,1)S(1)}, bf16[17,16,128]{2,1,0:T(8,128)(2,1)S(1)}, u32[]{:S(2)}, u32[]{:S(2)}) collective-permute-start(bf16[17,16,128]{2,1,0:T(8,128)(2,1)S(1)} %get-tuple-element.115), channel_id=1, source_target_pairs={{0,64},{1,65},{2,66},{3,67},{4,68},{5,69},{6,70},{7,71},{8,72},{9,... | collective-permute-start | bytes 208904 | tf_op jit(solution)/shard_map/ppermute | solution.py:407
  37.3 8.5 %collective-permute-start.12 = (bf16[16,16,128]{2,1,0:T(8,128)(2,1)S(1)}, bf16[16,16,128]{2,1,0:T(8,128)(2,1)S(1)}, u32[]{:S(2)}, u32[]{:S(2)}) collective-permute-start(bf16[16,16,128]{2,1,0:T(8,128)(2,1)S(1)} %get-tuple-element.112.refs_3_), channel_id=1, source_target_pairs={{0,64},{1,65},{2,66},{3,67},{4,68},{5,69},{6,70},{7,71},{8,72},{9,... | collective-permute-start | bytes 196616 | tf_op jit(solution)/shard_map/ppermute | solution.py:407
  46.0 6.0 %copy-start.1 = (bf16[3,32,32,256]{3,2,1,0:T(8,128)(2,1)S(1)}, bf16[3,32,32,256]{3,2,1,0:T(8,128)(2,1)}, u32[]{:S(2)}) copy-start(bf16[3,32,32,256]{3,2,1,0:T(8,128)(2,1)} %blocks_ref.1) | copy-start | bytes 4718596
  46.0 9.0 %collective-permute-start.14 = (bf16[33,16,128]{2,1,0:T(8,128)(2,1)S(1)}, bf16[33,16,128]{2,1,0:T(8,128)(2,1)S(1)}, u32[]{:S(2)}, u32[]{:S(2)}) collective-permute-start(bf16[33,16,128]{2,1,0:T(8,128)(2,1)S(1)} %get-tuple-element.120.refs_2_.after_ref), channel_id=1, source_target_pairs={{0,128},{1,129},{2,130},{3,131},{4,132},{5,133},{6,134},{7,135},{8... | collective-permute-start | bytes 405512 | tf_op jit(solution)/shard_map/ppermute | solution.py:422

commit v4 on v3

--- a/solution.py
+++ b/solution.py
@@ -191,8 +191,7 @@
         send_ref[place] = edge
 
 
-def near_kernel(halves_ref, blocks_ref, after_ref, near_ref, border_ref, arranged_ref, turned_ref):
-    del after_ref
+def near_sums(halves_ref, blocks_ref, near_ref, border_ref, arranged_ref, turned_ref):
     first_group, last_group = edge_lanes(0), edge_lanes(3)
     zeros = jnp.zeros((RHS, LANES), BF16)
     for half in range(2):
@@ -231,6 +230,26 @@
             near_ref[half, q] = jnp.dot(stack, matrix, preferred_element_type=F32)
 
 
+def early_near_kernel(halves_ref, blocks_hbm, after_ref, near_ref, border_ref, blocks_ref, *scratch):
+    del after_ref
+    *scratch, sem = scratch
+
+    @pl.when(lax.axis_index("rows") & 1 == 1)
+    def _():
+        copy = pltpu.make_async_copy(blocks_hbm, blocks_ref, sem)
+        copy.start()
+        copy.wait()
+        near_sums(halves_ref, blocks_ref, near_ref, border_ref, *scratch)
+
+
+def late_near_kernel(halves_ref, blocks_ref, near_in, border_in, after_ref, near_ref, border_ref, *scratch):
+    del near_in, border_in, after_ref
+
+    @pl.when(lax.axis_index("rows") & 1 == 0)
+    def _():
+        near_sums(halves_ref, blocks_ref, near_ref, border_ref, *scratch)
+
+
 def border_term(border_ref, beside, half):
     zeros = jnp.zeros((RHS, LANES), BF16)
     if half == 0:
@@ -279,7 +298,7 @@
 VMEM_SPEC = pl.BlockSpec(memory_space=pltpu.VMEM)
 ANY_SPEC = pl.BlockSpec(memory_space=pl.ANY)
 HBM_SPEC = pl.BlockSpec(memory_space=pltpu.HBM)
-TURNED = pltpu.VMEM((RANK * PITCH, LANES), F32)
+TURNED = pltpu.VMEM((RANK * PITCH + LANES, LANES), F32)
 ARRANGED = (QUADS, 2, 2 * RANK, LANES)
 EDGE = jax.ShapeDtypeStruct((RHS, LANES), BF16)
 
@@ -338,7 +357,7 @@
         scratch_shapes=[
             pltpu.VMEM((2, RHS, RANK, HALF), BF16),
             pltpu.VMEM(section, BF16),
-            pltpu.VMEM((2, RHS * (QUADS + 1), LANES), F32),
+            pltpu.VMEM((2, RHS * (QUADS + 1) + QUADS, LANES), F32),
             TURNED,
             pltpu.VMEM(ARRANGED, BF16),
             pltpu.SemaphoreType.DMA((4,)),
@@ -349,7 +368,7 @@
     return pairs[::2], pairs[1::2], halves, section_1
 
 
-def level_step(level, chain, partial, arranged, kept, received, beside, into=None):
+def level_step(level, chain, partial, arranged, kept, received, beside, into=None, after=()):
     merge = into is not None
     edges = [kept, beside] if chain == 0 else []
     filled = list(into) if merge and chain > 0 else []
@@ -357,28 +376,33 @@
     return pl.pallas_call(
         functools.partial(level_kernel, level, chain, merge),
         out_shape=tuple(outs),
-        in_specs=[VMEM_SPEC] * (3 + len(edges) + len(filled)),
+        in_specs=[VMEM_SPEC] * (3 + len(edges) + len(filled)) + [ANY_SPEC] * len(after),
         out_specs=(VMEM_SPEC,) * len(outs),
         input_output_aliases={3: 0, 4: 1} if filled else {},
         compiler_params=params(6),
         name="level",
-    )(partial, arranged, received, *edges, *filled)
-
-
-def near_field(halves, neighbor_blocks, after):
+    )(partial, arranged, received, *edges, *filled, *after)
+
+
+def near_field(halves, neighbor_blocks, after, filled=()):
+    early = not filled
+    scratch = [pltpu.VMEM((QUADS, LANES, LANES), BF16), TURNED]
+    if early:
+        scratch = [pltpu.VMEM(neighbor_blocks.shape, BF16), *scratch, pltpu.SemaphoreType.DMA(())]
     return pl.pallas_call(
-        near_kernel,
+        early_near_kernel if early else late_near_kernel,
         out_shape=(
             jax.ShapeDtypeStruct((2, QUADS, RHS, LANES), F32),
             jax.ShapeDtypeStruct((2, RANK, LANES), BF16),
         ),
-        in_specs=[VMEM_SPEC, VMEM_SPEC, ANY_SPEC],
+        in_specs=[VMEM_SPEC, HBM_SPEC if early else VMEM_SPEC] + [VMEM_SPEC] * len(filled) + [ANY_SPEC],
         out_specs=(VMEM_SPEC, VMEM_SPEC),
-        scratch_shapes=[pltpu.VMEM((QUADS, LANES, LANES), BF16), TURNED],
+        input_output_aliases={} if early else {2: 0, 3: 1},
+        scratch_shapes=scratch,
         compiler_params=params(12),
         cost_estimate=pl.CostEstimate(flops=4 * 10**6, bytes_accessed=3 * 2**20, transcendentals=0),
         name="near",
-    )(halves, neighbor_blocks, after)
+    )(halves, in_hbm(neighbor_blocks) if early else neighbor_blocks, *filled, after)
 
 
 def tail(level, *operands):
@@ -389,7 +413,7 @@
         out_specs=VMEM_SPEC,
         scratch_shapes=[
             pltpu.VMEM((QUADS, RHS, 2 * LANES), BF16),
-            pltpu.VMEM((2, QUADS * (RHS + 1), LANES), F32),
+            pltpu.VMEM((2, QUADS * (RHS + 1) + RHS, LANES), F32),
         ],
         compiler_params=params(12),
         name="tail",
@@ -410,8 +434,12 @@
         else:
             staged = stage(level, factors, level + 1, kept, sending[-1])
         into = () if level == level_count - 2 else None
+        after = ()
+        if level == 0:
+            filled = near_field(halves, neighbor_blocks, staged[0])
+            after = filled[:1]
         for chain in range(CHAINS):
-            outs = level_step(level, chain, *staged, kept[chain], received[chain], beside, into)
+            outs = level_step(level, chain, *staged, kept[chain], received[chain], beside, into, after)
             kept[chain], sending[chain] = outs[:2]
             if chain == 0:
                 beside = outs[2]
@@ -420,7 +448,7 @@
     level = level_count - 1
     kept, sending = into
     received = lax.ppermute(sending, "rows", [(i, i ^ (1 << level)) for i in range(count)])
-    near, border = near_field(halves, neighbor_blocks, sending)
+    near, border = near_field(halves, neighbor_blocks, sending, filled)
     partial, last = stage(level, factors, level + 1, [kept], sending)
     root = arrange(factors, level + 2, sending)
     return tail(level, partial, last, root, kept, received, beside, near, border)

time: 57.1 us -> 54.5 us (0.954)
  waiting for transfers between devices: 13.4 us -> 7.39 us
  starting transfers between devices: 26.7 us -> 29.8 us
    ppermute x14, waiting for transfers between devices: 12.1 us -> 7.28 us  [shards(): received = [lax.ppermute(part, 'rows', partners) for part in sending]]
    ppermute x14, starting transfers between devices: 22.1 us -> 23.9 us  [shards(): received = [lax.ppermute(part, 'rows', partners) for part in sending]]
    ppermute x1, starting transfers between devices: 4.6 us -> 5.9 us  [shards(): lax.ppermute(sending, 'rows', [(i, i ^ 1 << level) for i in range(count)])]
    ppermute x1, waiting for transfers between devices: 1.31 us -> 0.11 us  [shards(): lax.ppermute(sending, 'rows', [(i, i ^ 1 << level) for i in range(count)])]
    pallas_call x1 -> x2, Pallas kernels: 1.67 us -> 1.68 us  [near_field(): pl.pallas_call(early_near_kernel if early else late_near_kernel, out_shap...]
  transfers between devices with their start and end apart: 15 -> 15, of which waited for: 8 -> 7; matrix products, arithmetic and copies ran while one was open for 0% -> 0% of each run, Pallas kernels for 21% -> 22%
where the time goes in v4:
time: 54.5 us; the launch traced here: 54.2 us
  starting transfers between devices  29.8 us (55%)
  Pallas kernels  16.9 us (31%)
  waiting for transfers between devices  7.39 us (14%)
    ppermute x14, starting transfers between devices, shards(): received = [lax.ppermute(part, 'rows', partners) for part in sending]  23.9 us
    ppermute x14, waiting for transfers between devices, shards(): received = [lax.ppermute(part, 'rows', partners) for part in sending]  7.28 us
    pallas_call x8, Pallas kernels, stage(): pl.pallas_call(functools.partial(stage_kernel, level, index, len(kept)),...  6.17 us
    ppermute x1, starting transfers between devices, shards(): lax.ppermute(sending, 'rows', [(i, i ^ 1 << level) for i in range(count)])  5.9 us
    pallas_call x14, Pallas kernels, level_step(): pl.pallas_call(functools.partial(level_kernel, level, chain, merge), out_...  3.65 us
    pallas_call x1, Pallas kernels, head(): pl.pallas_call(head_kernel, out_shape=tuple(outs), in_specs=[HBM_SPEC, HB...  2.75 us
    pallas_call x1, Pallas kernels, tail(): pl.pallas_call(functools.partial(tail_kernel, level), out_shape=jax.Shape...  1.99 us
    pallas_call x2, Pallas kernels, near_field(): pl.pallas_call(early_near_kernel if early else late_near_kernel, out_shap...  1.68 us
  transfers between devices with their start and end apart: 15, of which 7 were waited for; matrix products, arithmetic and copies ran while one was open for 0% of the time, Pallas kernels for 22%

profile of v4, /device:TPU:6, one launch (start us, length us, event | category | flops | bytes accessed | tf_op | source)
XLA Modules:
  0.0 54.2 jit_solution(16762473774779381567)
XLA Ops:
  0.0 2.7 %head.1 = (bf16[17,16,128]{2,1,0:T(8,128)(2,1)S(1)}, bf16[17,16,128]{2,1,0:T(8,128)(2,1)S(1)}, bf16[16,16,128]{2,1,0:T(8,128)(2,1)S(1)}, bf16[16,16,128]{2,1,0:T...) custom-call(bf16[16,32,256]{2,1,0:T(8,128)(2,1)} %vectors_hbm.1, ...), custom_call_target="tpu_custom_call" | custom-call | tf_op jit(solution)/shard_map/head/pallas_call | solution.py:352
  2.9 0.5 collective-permute-start.1
  3.4 0.8 %stage.8 = (f32[32,16,256]{2,1,0:T(8,128)S(1)}, bf16[32,2,32,128]{3,2,1,0:T(8,128)(2,1)S(1)}) custom-call(bf16[64,64,128]{2,1,0:T(8,128)(2,1)S(1)} %get-tuple-element.70.refs_0_, bf16[17,16,128]{2,1,0:T(8,128)(2,1)S(1)} %get-tuple-element.71.refs_1_.refs_3_, bf16[16,16,128]{2,1,0:T(8,128)(2,1)S(1)} %get-tuple-element.72.refs_2_, ...), custom_call_target="tpu_custom_call" | custom-call | flops 2000000 | bytes 2097152 | tf_op jit(solution)/shard_map/stage/pallas_call | solution.py:333
  4.4 0.9 %collective-permute-start.2 = (bf16[17,16,128]{2,1,0:T(8,128)(2,1)S(1)}, bf16[17,16,128]{2,1,0:T(8,128)(2,1)S(1)}, u32[]{:S(2)}, u32[]{:S(2)}) collective-permute-start(bf16[17,16,128]{2,1,0:T(8,128)(2,1)S(1)} %get-tuple-element.84), channel_id=1, source_target_pairs={{0,2},{1,3},{2,0},{3,1},{4,6},{5,7},{6,4},{7,5},{8,10},{9,11},{10,... | collective-permute-start | bytes 208904 | tf_op jit(solution)/shard_map/ppermute | solution.py:431
  5.6 1.3 %collective-permute-start.3 = (bf16[16,16,128]{2,1,0:T(8,128)(2,1)S(1)}, bf16[16,16,128]{2,1,0:T(8,128)(2,1)S(1)}, u32[]{:S(2)}, u32[]{:S(2)}) collective-permute-start(bf16[16,16,128]{2,1,0:T(8,128)(2,1)S(1)} %get-tuple-element.81.refs_3_), channel_id=1, source_target_pairs={{0,2},{1,3},{2,0},{3,1},{4,6},{5,7},{6,4},{7,5},{8,10},{9,11},{10,... | collective-permute-start | bytes 196616 | tf_op jit(solution)/shard_map/ppermute | solution.py:431
  6.9 0.8 %stage.9 = (f32[32,16,256]{2,1,0:T(8,128)S(1)}, bf16[32,2,32,128]{3,2,1,0:T(8,128)(2,1)S(1)}) custom-call(bf16[10,64,64,128]{3,2,1,0:T(8,128)(2,1)S(1)} %copy-done, bf16[17,16,128]{2,1,0:T(8,128)(2,1)S(1)} %get-tuple-element.79.refs_1_.refs_3_, bf16[16,16,128]{2,1,0:T(8,128)(2,1)S(1)} %get-tuple-element.80.refs_2_, ...), custom_call_target="tpu_custom_call" | custom-call | flops 2000000 | bytes 2097152 | tf_op jit(solution)/shard_map/stage/pallas_call | solution.py:333
  7.7 1.2 %collective-permute-done.2.refs_2_ = bf16[17,16,128]{2,1,0:T(8,128)(2,1)S(1)} collective-permute-done((bf16[17,16,128]{2,1,0:T(8,128)(2,1)S(1)}, bf16[17,16,128]{2,1,0:T(8,128)(2,1)S(1)}, u32[]{:S(2)}, u32[]{:S(2)}) %collective-permute-start.2) | collective-permute-done | bytes 69664 | tf_op jit(solution)/shard_map/ppermute | solution.py:431
  9.1 1.7 %collective-permute-start.4 = (bf16[17,16,128]{2,1,0:T(8,128)(2,1)S(1)}, bf16[17,16,128]{2,1,0:T(8,128)(2,1)S(1)}, u32[]{:S(2)}, u32[]{:S(2)}) collective-permute-start(bf16[17,16,128]{2,1,0:T(8,128)(2,1)S(1)} %get-tuple-element.91), channel_id=1, source_target_pairs={{0,4},{1,5},{2,6},{3,7},{4,0},{5,1},{6,2},{7,3},{8,12},{9,13},{10,... | collective-permute-start | bytes 208904 | tf_op jit(solution)/shard_map/ppermute | solution.py:431
  11.1 2.7 %collective-permute-start.5 = (bf16[16,16,128]{2,1,0:T(8,128)(2,1)S(1)}, bf16[16,16,128]{2,1,0:T(8,128)(2,1)S(1)}, u32[]{:S(2)}, u32[]{:S(2)}) collective-permute-start(bf16[16,16,128]{2,1,0:T(8,128)(2,1)S(1)} %get-tuple-element.88.refs_3_), channel_id=1, source_target_pairs={{0,4},{1,5},{2,6},{3,7},{4,0},{5,1},{6,2},{7,3},{8,12},{9,13},{10,... | collective-permute-start | bytes 196616 | tf_op jit(solution)/shard_map/ppermute | solution.py:431
  13.7 0.8 %stage.10 = (f32[32,16,256]{2,1,0:T(8,128)S(1)}, bf16[32,2,32,128]{3,2,1,0:T(8,128)(2,1)S(1)}) custom-call(bf16[10,64,64,128]{3,2,1,0:T(8,128)(2,1)S(1)} %copy-done, bf16[17,16,128]{2,1,0:T(8,128)(2,1)S(1)} %get-tuple-element.86.refs_1_.refs_3_, bf16[16,16,128]{2,1,0:T(8,128)(2,1)S(1)} %get-tuple-element.87.refs_2_, ...), custom_call_target="tpu_custom_call" | custom-call | flops 2000000 | bytes 2097152 | tf_op jit(solution)/shard_map/stage/pallas_call | solution.py:333
  14.5 0.5 collective-permute-done.4.refs_2_
  15.3 1.7 %collective-permute-start.6 = (bf16[17,16,128]{2,1,0:T(8,128)(2,1)S(1)}, bf16[17,16,128]{2,1,0:T(8,128)(2,1)S(1)}, u32[]{:S(2)}, u32[]{:S(2)}) collective-permute-start(bf16[17,16,128]{2,1,0:T(8,128)(2,1)S(1)} %get-tuple-element.98), channel_id=1, source_target_pairs={{0,8},{1,9},{2,10},{3,11},{4,12},{5,13},{6,14},{7,15},{8,0},{9,1},... | collective-permute-start | bytes 208904 | tf_op jit(solution)/shard_map/ppermute | solution.py:431
  17.2 1.5 %collective-permute-start.7 = (bf16[16,16,128]{2,1,0:T(8,128)(2,1)S(1)}, bf16[16,16,128]{2,1,0:T(8,128)(2,1)S(1)}, u32[]{:S(2)}, u32[]{:S(2)}) collective-permute-start(bf16[16,16,128]{2,1,0:T(8,128)(2,1)S(1)} %get-tuple-element.95.refs_3_), channel_id=1, source_target_pairs={{0,8},{1,9},{2,10},{3,11},{4,12},{5,13},{6,14},{7,15},{8,0},{9,1},... | collective-permute-start | bytes 196616 | tf_op jit(solution)/shard_map/ppermute | solution.py:431
  18.7 0.8 %stage.11 = (f32[32,16,256]{2,1,0:T(8,128)S(1)}, bf16[32,2,32,128]{3,2,1,0:T(8,128)(2,1)S(1)}) custom-call(bf16[10,64,64,128]{3,2,1,0:T(8,128)(2,1)S(1)} %copy-done, bf16[17,16,128]{2,1,0:T(8,128)(2,1)S(1)} %get-tuple-element.93.refs_1_.refs_3_, bf16[16,16,128]{2,1,0:T(8,128)(2,1)S(1)} %get-tuple-element.94.refs_2_, ...), custom_call_target="tpu_custom_call" | custom-call | flops 2000000 | bytes 2097152 | tf_op jit(solution)/shard_map/stage/pallas_call | solution.py:333
  19.4 0.8 %collective-permute-done.6.refs_2_ = bf16[17,16,128]{2,1,0:T(8,128)(2,1)S(1)} collective-permute-done((bf16[17,16,128]{2,1,0:T(8,128)(2,1)S(1)}, bf16[17,16,128]{2,1,0:T(8,128)(2,1)S(1)}, u32[]{:S(2)}, u32[]{:S(2)}) %collective-permute-start.6) | collective-permute-done | bytes 69664 | tf_op jit(solution)/shard_map/ppermute | solution.py:431
  20.5 3.1 %collective-permute-start.8 = (bf16[17,16,128]{2,1,0:T(8,128)(2,1)S(1)}, bf16[17,16,128]{2,1,0:T(8,128)(2,1)S(1)}, u32[]{:S(2)}, u32[]{:S(2)}) collective-permute-start(bf16[17,16,128]{2,1,0:T(8,128)(2,1)S(1)} %get-tuple-element.105), channel_id=1, source_target_pairs={{0,16},{1,17},{2,18},{3,19},{4,20},{5,21},{6,22},{7,23},{8,24},{9,... | collective-permute-start | bytes 208904 | tf_op jit(solution)/shard_map/ppermute | solution.py:431
  23.9 1.7 %collective-permute-start.9 = (bf16[16,16,128]{2,1,0:T(8,128)(2,1)S(1)}, bf16[16,16,128]{2,1,0:T(8,128)(2,1)S(1)}, u32[]{:S(2)}, u32[]{:S(2)}) collective-permute-start(bf16[16,16,128]{2,1,0:T(8,128)(2,1)S(1)} %get-tuple-element.102.refs_3_), channel_id=1, source_target_pairs={{0,16},{1,17},{2,18},{3,19},{4,20},{5,21},{6,22},{7,23},{8,24},{9,... | collective-permute-start | bytes 196616 | tf_op jit(solution)/shard_map/ppermute | solution.py:431
  25.7 0.8 %stage.12 = (f32[32,16,256]{2,1,0:T(8,128)S(1)}, bf16[32,2,32,128]{3,2,1,0:T(8,128)(2,1)S(1)}) custom-call(bf16[10,64,64,128]{3,2,1,0:T(8,128)(2,1)S(1)} %copy-done, bf16[17,16,128]{2,1,0:T(8,128)(2,1)S(1)} %get-tuple-element.100.refs_1_.refs_3_, bf16[16,16,128]{2,1,0:T(8,128)(2,1)S(1)} %get-tuple-element.101.refs_2_, ...), custom_call_target="tpu_custom_call" | custom-call | flops 2000000 | bytes 2097152 | tf_op jit(solution)/shard_map/stage/pallas_call | solution.py:333
  26.7 2.0 %collective-permute-start.10 = (bf16[17,16,128]{2,1,0:T(8,128)(2,1)S(1)}, bf16[17,16,128]{2,1,0:T(8,128)(2,1)S(1)}, u32[]{:S(2)}, u32[]{:S(2)}) collective-permute-start(bf16[17,16,128]{2,1,0:T(8,128)(2,1)S(1)} %get-tuple-element.112), channel_id=1, source_target_pairs={{0,32},{1,33},{2,34},{3,35},{4,36},{5,37},{6,38},{7,39},{8,40},{9,... | collective-permute-start | bytes 208904 | tf_op jit(solution)/shard_map/ppermute | solution.py:431
  28.7 1.2 %collective-permute-done.9.refs_2_ = bf16[16,16,128]{2,1,0:T(8,128)(2,1)S(1)} collective-permute-done((bf16[16,16,128]{2,1,0:T(8,128)(2,1)S(1)}, bf16[16,16,128]{2,1,0:T(8,128)(2,1)S(1)}, u32[]{:S(2)}, u32[]{:S(2)}) %collective-permute-start.9) | collective-permute-done | bytes 65568 | tf_op jit(solution)/shard_map/ppermute | solution.py:431
  30.2 2.0 %collective-permute-start.11 = (bf16[16,16,128]{2,1,0:T(8,128)(2,1)S(1)}, bf16[16,16,128]{2,1,0:T(8,128)(2,1)S(1)}, u32[]{:S(2)}, u32[]{:S(2)}) collective-permute-start(bf16[16,16,128]{2,1,0:T(8,128)(2,1)S(1)} %get-tuple-element.109.refs_3_), channel_id=1, source_target_pairs={{0,32},{1,33},{2,34},{3,35},{4,36},{5,37},{6,38},{7,39},{8,40},{9,... | collective-permute-start | bytes 196616 | tf_op jit(solution)/shard_map/ppermute | solution.py:431
  32.2 0.8 %stage.13 = (f32[32,16,256]{2,1,0:T(8,128)S(1)}, bf16[32,2,32,128]{3,2,1,0:T(8,128)(2,1)S(1)}) custom-call(bf16[10,64,64,128]{3,2,1,0:T(8,128)(2,1)S(1)} %copy-done, bf16[17,16,128]{2,1,0:T(8,128)(2,1)S(1)} %get-tuple-element.107.refs_1_.refs_3_, bf16[16,16,128]{2,1,0:T(8,128)(2,1)S(1)} %get-tuple-element.108.refs_2_, ...), custom_call_target="tpu_custom_call" | custom-call | flops 2000000 | bytes 2097152 | tf_op jit(solution)/shard_map/stage/pallas_call | solution.py:333
  33.3 3.4 %collective-permute-start.13 = (bf16[17,16,128]{2,1,0:T(8,128)(2,1)S(1)}, bf16[17,16,128]{2,1,0:T(8,128)(2,1)S(1)}, u32[]{:S(2)}, u32[]{:S(2)}) collective-permute-start(bf16[17,16,128]{2,1,0:T(8,128)(2,1)S(1)} %get-tuple-element.119), channel_id=1, source_target_pairs={{0,64},{1,65},{2,66},{3,67},{4,68},{5,69},{6,70},{7,71},{8,72},{9,... | collective-permute-start | bytes 208904 | tf_op jit(solution)/shard_map/ppermute | solution.py:431
  36.9 1.4 %collective-permute-start.12 = (bf16[16,16,128]{2,1,0:T(8,128)(2,1)S(1)}, bf16[16,16,128]{2,1,0:T(8,128)(2,1)S(1)}, u32[]{:S(2)}, u32[]{:S(2)}) collective-permute-start(bf16[16,16,128]{2,1,0:T(8,128)(2,1)S(1)} %get-tuple-element.116.refs_3_), channel_id=1, source_target_pairs={{0,64},{1,65},{2,66},{3,67},{4,68},{5,69},{6,70},{7,71},{8,72},{9,... | collective-permute-start | bytes 196616 | tf_op jit(solution)/shard_map/ppermute | solution.py:431
  38.3 0.8 %stage.14 = (f32[32,16,256]{2,1,0:T(8,128)S(1)}, bf16[32,2,32,128]{3,2,1,0:T(8,128)(2,1)S(1)}) custom-call(bf16[10,64,64,128]{3,2,1,0:T(8,128)(2,1)S(1)} %copy-done, bf16[17,16,128]{2,1,0:T(8,128)(2,1)S(1)} %get-tuple-element.114.refs_1_.refs_3_, bf16[16,16,128]{2,1,0:T(8,128)(2,1)S(1)} %get-tuple-element.115.refs_2_, ...), custom_call_target="tpu_custom_call" | custom-call | flops 2000000 | bytes 2097152 | tf_op jit(solution)/shard_map/stage/pallas_call | solution.py:333
  39.1 1.5 %collective-permute-done.13.refs_2_ = bf16[17,16,128]{2,1,0:T(8,128)(2,1)S(1)} collective-permute-done((bf16[17,16,128]{2,1,0:T(8,128)(2,1)S(1)}, bf16[17,16,128]{2,1,0:T(8,128)(2,1)S(1)}, u32[]{:S(2)}, u32[]{:S(2)}) %collective-permute-start.13) | collective-permute-done | bytes 69664 | tf_op jit(solution)/shard_map/ppermute | solution.py:431
  40.9 2.0 %collective-permute-done.12.refs_2_ = bf16[16,16,128]{2,1,0:T(8,128)(2,1)S(1)} collective-permute-done((bf16[16,16,128]{2,1,0:T(8,128)(2,1)S(1)}, bf16[16,16,128]{2,1,0:T(8,128)(2,1)S(1)}, u32[]{:S(2)}, u32[]{:S(2)}) %collective-permute-start.12) | collective-permute-done | bytes 65568 | tf_op jit(solution)/shard_map/ppermute | solution.py:431
  43.1 5.9 %collective-permute-start.14 = (bf16[33,16,128]{2,1,0:T(8,128)(2,1)S(1)}, bf16[33,16,128]{2,1,0:T(8,128)(2,1)S(1)}, u32[]{:S(2)}, u32[]{:S(2)}) collective-permute-start(bf16[33,16,128]{2,1,0:T(8,128)(2,1)S(1)} %get-tuple-element.124.refs_2_.after_ref), channel_id=1, source_target_pairs={{0,128},{1,129},{2,130},{3,131},{4,132},{5,133},{6,134},{7,135},{8... | collective-permute-start | bytes 405512 | tf_op jit(solution)/shard_map/ppermute | solution.py:450
  49.0 0.6 %arrange.1.root_ref = bf16[32,2,64,128]{3,2,1,0:T(8,128)(2,1)S(1)} custom-call(bf16[10,64,64,128]{3,2,1,0:T(8,128)(2,1)S(1)} %copy-done, bf16[33,16,128]{2,1,0:T(8,128)(2,1)S(1)} %get-tuple-element.124.refs_2_.after_ref), custom_call_target="tpu_custom_call" | custom-call | flops 2000000 | bytes 2097152 | tf_op jit(solution)/shard_map/arrange/pallas_call | solution.py:320
  49.7 0.8 %stage.15 = (f32[32,16,256]{2,1,0:T(8,128)S(1)}, bf16[32,2,32,128]{3,2,1,0:T(8,128)(2,1)S(1)}) custom-call(bf16[10,64,64,128]{3,2,1,0:T(8,128)(2,1)S(1)} %copy-done, bf16[33,16,128]{2,1,0:T(8,128)(2,1)S(1)} %get-tuple-element.123.refs_1_.kept_ref, bf16[33,16,128]{2,1,0:T(8,128)(2,1)S(1)} %get-tuple-element.124.refs_2_.after_ref), custom_call_target="tpu_custom_call" | custom-call | flops 2000000 | bytes 2097152 | tf_op jit(solution)/shard_map/stage/pallas_call | solution.py:333
  50.4 1.7 %near.3 = (f32[2,32,16,128]{3,2,1,0:T(8,128)S(1)}, bf16[2,32,128]{2,1,0:T(8,128)(2,1)S(1)}) custom-call(bf16[2,32,16,128]{3,2,1,0:T(8,128)(2,1)S(1)} %get-tuple-element.77.halves_ref, bf16[3,32,32,256]{3,2,1,0:T(8,128)(2,1)S(1)} %copy-done.1, ...), custom_call_target="tpu_custom_call", output_to_operand_aliasing={{0}: (2, {}), {1}: (3, {})} | custom-call | flops 4000000 | bytes 3145728 | tf_op jit(solution)/shard_map/near/pallas_call | solution.py:392
  52.2 2.0 %tail.1 = bf16[16,32,256]{2,1,0:T(8,128)(2,1)} custom-call(f32[32,16,256]{2,1,0:T(8,128)S(1)} %get-tuple-element.125.partial_ref, bf16[32,2,32,128]{3,2,1,0:T(8,128)(2,1)S(1)} %get-tuple-element.126.last_ref, bf16[32,2,64,128]{3,2,1,0:T(8,128)(2,1)S(1)} %arrange.1.root_ref, bf16[33,16,128]{2,1,0:T(8,128)(2,1)S(1)} %get-tuple-element.123.refs_1_.kept_ref, ...), custom_call_target="tpu_custom_call" | custom-call | tf_op jit(solution)/shard_map/tail/pallas_call | solution.py:409
  (30 shorter events, 3.9 us)
Async XLA Ops:
  0.0 6.9 %copy-start = (bf16[10,64,64,128]{3,2,1,0:T(8,128)(2,1)S(1)}, bf16[10,64,64,128]{3,2,1,0:T(8,128)(2,1)}, u32[]{:S(2)}) copy-start(bf16[10,64,64,128]{3,2,1,0:T(8,128)(2,1)} %weights_ref) | copy-start | bytes 31457284
  2.8 1.4 %collective-permute-start = (bf16[17,16,128]{2,1,0:T(8,128)(2,1)S(1)}, bf16[17,16,128]{2,1,0:T(8,128)(2,1)S(1)}, u32[]{:S(2)}, u32[]{:S(2)}) collective-permute-start(bf16[17,16,128]{2,1,0:T(8,128)(2,1)S(1)} %get-tuple-element.76), channel_id=1, source_target_pairs={{0,1},{1,0},{2,3},{3,2},{4,5},{5,4},{6,7},{7,6},{8,9},{9,8},{10,11... | collective-permute-start | bytes 208904 | tf_op jit(solution)/shard_map/ppermute | solution.py:431
  2.9 2.5 %collective-permute-start.1 = (bf16[16,16,128]{2,1,0:T(8,128)(2,1)S(1)}, bf16[16,16,128]{2,1,0:T(8,128)(2,1)S(1)}, u32[]{:S(2)}, u32[]{:S(2)}) collective-permute-start(bf16[16,16,128]{2,1,0:T(8,128)(2,1)S(1)} %get-tuple-element.73.refs_3_), channel_id=1, source_target_pairs={{0,1},{1,0},{2,3},{3,2},{4,5},{5,4},{6,7},{7,6},{8,9},{9,8},{10,11... | collective-permute-start | bytes 196616 | tf_op jit(solution)/shard_map/ppermute | solution.py:431
  4.4 4.4 %collective-permute-start.2 = (bf16[17,16,128]{2,1,0:T(8,128)(2,1)S(1)}, bf16[17,16,128]{2,1,0:T(8,128)(2,1)S(1)}, u32[]{:S(2)}, u32[]{:S(2)}) collective-permute-start(bf16[17,16,128]{2,1,0:T(8,128)(2,1)S(1)} %get-tuple-element.84), channel_id=1, source_target_pairs={{0,2},{1,3},{2,0},{3,1},{4,6},{5,7},{6,4},{7,5},{8,10},{9,11},{10,... | collective-permute-start | bytes 208904 | tf_op jit(solution)/shard_map/ppermute | solution.py:431
  5.6 5.2 %collective-permute-start.3 = (bf16[16,16,128]{2,1,0:T(8,128)(2,1)S(1)}, bf16[16,16,128]{2,1,0:T(8,128)(2,1)S(1)}, u32[]{:S(2)}, u32[]{:S(2)}) collective-permute-start(bf16[16,16,128]{2,1,0:T(8,128)(2,1)S(1)} %get-tuple-element.81.refs_3_), channel_id=1, source_target_pairs={{0,2},{1,3},{2,0},{3,1},{4,6},{5,7},{6,4},{7,5},{8,10},{9,11},{10,... | collective-permute-start | bytes 196616 | tf_op jit(solution)/shard_map/ppermute | solution.py:431
  9.1 5.9 %collective-permute-start.4 = (bf16[17,16,128]{2,1,0:T(8,128)(2,1)S(1)}, bf16[17,16,128]{2,1,0:T(8,128)(2,1)S(1)}, u32[]{:S(2)}, u32[]{:S(2)}) collective-permute-start(bf16[17,16,128]{2,1,0:T(8,128)(2,1)S(1)} %get-tuple-element.91), channel_id=1, source_target_pairs={{0,4},{1,5},{2,6},{3,7},{4,0},{5,1},{6,2},{7,3},{8,12},{9,13},{10,... | collective-permute-start | bytes 208904 | tf_op jit(solution)/shard_map/ppermute | solution.py:431
  11.1 5.9 %collective-permute-start.5 = (bf16[16,16,128]{2,1,0:T(8,128)(2,1)S(1)}, bf16[16,16,128]{2,1,0:T(8,128)(2,1)S(1)}, u32[]{:S(2)}, u32[]{:S(2)}) collective-permute-start(bf16[16,16,128]{2,1,0:T(8,128)(2,1)S(1)} %get-tuple-element.88.refs_3_), channel_id=1, source_target_pairs={{0,4},{1,5},{2,6},{3,7},{4,0},{5,1},{6,2},{7,3},{8,12},{9,13},{10,... | collective-permute-start | bytes 196616 | tf_op jit(solution)/shard_map/ppermute | solution.py:431
  15.3 5.0 %collective-permute-start.6 = (bf16[17,16,128]{2,1,0:T(8,128)(2,1)S(1)}, bf16[17,16,128]{2,1,0:T(8,128)(2,1)S(1)}, u32[]{:S(2)}, u32[]{:S(2)}) collective-permute-start(bf16[17,16,128]{2,1,0:T(8,128)(2,1)S(1)} %get-tuple-element.98), channel_id=1, source_target_pairs={{0,8},{1,9},{2,10},{3,11},{4,12},{5,13},{6,14},{7,15},{8,0},{9,1},... | collective-permute-start | bytes 208904 | tf_op jit(solution)/shard_map/ppermute | solution.py:431
  17.2 6.4 %collective-permute-start.7 = (bf16[16,16,128]{2,1,0:T(8,128)(2,1)S(1)}, bf16[16,16,128]{2,1,0:T(8,128)(2,1)S(1)}, u32[]{:S(2)}, u32[]{:S(2)}) collective-permute-start(bf16[16,16,128]{2,1,0:T(8,128)(2,1)S(1)} %get-tuple-element.95.refs_3_), channel_id=1, source_target_pairs={{0,8},{1,9},{2,10},{3,11},{4,12},{5,13},{6,14},{7,15},{8,0},{9,1},... | collective-permute-start | bytes 196616 | tf_op jit(solution)/shard_map/ppermute | solution.py:431
  20.5 5.9 %collective-permute-start.8 = (bf16[17,16,128]{2,1,0:T(8,128)(2,1)S(1)}, bf16[17,16,128]{2,1,0:T(8,128)(2,1)S(1)}, u32[]{:S(2)}, u32[]{:S(2)}) collective-permute-start(bf16[17,16,128]{2,1,0:T(8,128)(2,1)S(1)} %get-tuple-element.105), channel_id=1, source_target_pairs={{0,16},{1,17},{2,18},{3,19},{4,20},{5,21},{6,22},{7,23},{8,24},{9,... | collective-permute-start | bytes 208904 | tf_op jit(solution)/shard_map/ppermute | solution.py:431
  23.9 6.0 %collective-permute-start.9 = (bf16[16,16,128]{2,1,0:T(8,128)(2,1)S(1)}, bf16[16,16,128]{2,1,0:T(8,128)(2,1)S(1)}, u32[]{:S(2)}, u32[]{:S(2)}) collective-permute-start(bf16[16,16,128]{2,1,0:T(8,128)(2,1)S(1)} %get-tuple-element.102.refs_3_), channel_id=1, source_target_pairs={{0,16},{1,17},{2,18},{3,19},{4,20},{5,21},{6,22},{7,23},{8,24},{9,... | collective-permute-start | bytes 196616 | tf_op jit(solution)/shard_map/ppermute | solution.py:431
  26.7 6.3 %collective-permute-start.10 = (bf16[17,16,128]{2,1,0:T(8,128)(2,1)S(1)}, bf16[17,16,128]{2,1,0:T(8,128)(2,1)S(1)}, u32[]{:S(2)}, u32[]{:S(2)}) collective-permute-start(bf16[17,16,128]{2,1,0:T(8,128)(2,1)S(1)} %get-tuple-element.112), channel_id=1, source_target_pairs={{0,32},{1,33},{2,34},{3,35},{4,36},{5,37},{6,38},{7,39},{8,40},{9,... | collective-permute-start | bytes 208904 | tf_op jit(solution)/shard_map/ppermute | solution.py:431
  30.2 6.4 %collective-permute-start.11 = (bf16[16,16,128]{2,1,0:T(8,128)(2,1)S(1)}, bf16[16,16,128]{2,1,0:T(8,128)(2,1)S(1)}, u32[]{:S(2)}, u32[]{:S(2)}) collective-permute-start(bf16[16,16,128]{2,1,0:T(8,128)(2,1)S(1)} %get-tuple-element.109.refs_3_), channel_id=1, source_target_pairs={{0,32},{1,33},{2,34},{3,35},{4,36},{5,37},{6,38},{7,39},{8,40},{9,... | collective-permute-start | bytes 196616 | tf_op jit(solution)/shard_map/ppermute | solution.py:431
  33.3 7.3 %collective-permute-start.13 = (bf16[17,16,128]{2,1,0:T(8,128)(2,1)S(1)}, bf16[17,16,128]{2,1,0:T(8,128)(2,1)S(1)}, u32[]{:S(2)}, u32[]{:S(2)}) collective-permute-start(bf16[17,16,128]{2,1,0:T(8,128)(2,1)S(1)} %get-tuple-element.119), channel_id=1, source_target_pairs={{0,64},{1,65},{2,66},{3,67},{4,68},{5,69},{6,70},{7,71},{8,72},{9,... | collective-permute-start | bytes 208904 | tf_op jit(solution)/shard_map/ppermute | solution.py:431
  36.9 6.0 %collective-permute-start.12 = (bf16[16,16,128]{2,1,0:T(8,128)(2,1)S(1)}, bf16[16,16,128]{2,1,0:T(8,128)(2,1)S(1)}, u32[]{:S(2)}, u32[]{:S(2)}) collective-permute-start(bf16[16,16,128]{2,1,0:T(8,128)(2,1)S(1)} %get-tuple-element.116.refs_3_), channel_id=1, source_target_pairs={{0,64},{1,65},{2,66},{3,67},{4,68},{5,69},{6,70},{7,71},{8,72},{9,... | collective-permute-start | bytes 196616 | tf_op jit(solution)/shard_map/ppermute | solution.py:431
  43.1 7.3 %copy-start.1 = (bf16[3,32,32,256]{3,2,1,0:T(8,128)(2,1)S(1)}, bf16[3,32,32,256]{3,2,1,0:T(8,128)(2,1)}, u32[]{:S(2)}) copy-start(bf16[3,32,32,256]{3,2,1,0:T(8,128)(2,1)} %blocks_ref.1) | copy-start | bytes 4718596
  43.1 9.1 %collective-permute-start.14 = (bf16[33,16,128]{2,1,0:T(8,128)(2,1)S(1)}, bf16[33,16,128]{2,1,0:T(8,128)(2,1)S(1)}, u32[]{:S(2)}, u32[]{:S(2)}) collective-permute-start(bf16[33,16,128]{2,1,0:T(8,128)(2,1)S(1)} %get-tuple-element.124.refs_2_.after_ref), channel_id=1, source_target_pairs={{0,128},{1,129},{2,130},{3,131},{4,132},{5,133},{6,134},{7,135},{8... | collective-permute-start | bytes 405512 | tf_op jit(solution)/shard_map/ppermute | solution.py:450
